TPU v7x, 512 devices: a whole 4x4x16 slice. The times are simulated.
512 devices in a mesh: lon: 32 (over x, y, z_hi), lat: 16 (over z_lo, core).
Axes of the slice: x: 4, y: 4, z: 16 (z_hi: 2, z_lo: 8; z = z_hi * 8 + z_lo), core: 2. Of those that a mesh axis runs over, the one named last changes fastest.
Arguments:
- tokens: bfloat16 [4, 192, 384, 512], P(None, 'lat', 'lon'), may hold values from -6 to 6
- gain_attn: float32 [512], replicated, may hold values from 0.1 to 1.9
- weight_qkv: bfloat16 [512, 1536], replicated, may hold values from -0.25 to 0.25
- weight_out: bfloat16 [512, 512], replicated, may hold values from -0.25 to 0.25
Outputs:
- mixed: bfloat16 [4, 192, 384, 512], P(None, 'lat', 'lon')
All inputs are finite; a program needn't handle non-finite values.
Results may differ from a plain program's by a relative error of at most 0.0043.
Values may be sent and summed in bfloat16 or wider, within the bound.
No kernel may reach another device: no remote copies, remote signals or barrier semaphores. Data moves between devices by JAX's collectives and lax.ppermute only.
A program may use at most 128 MiB of HBM per device.

v0:
```python
import jax
import jax.numpy as jnp
from jax import lax
from jax.sharding import PartitionSpec as P

HEADS = 8
HEAD_SIZE = 64
WIN_LEV = 2
WIN_LAT = 6
WIN_LON = 12
SHIFT_LEV = 1
SHIFT_LAT = 3
SHIFT_LON = 6


EPS = 1e-05


def from_behind(value, axis, by):
    count = lax.axis_size(axis)
    return lax.ppermute(value, axis, [(i, (i + by) % count) for i in range(count)])


def layer_norm(values, gain):
    center = values - jnp.mean(values, axis=-1, keepdims=True)
    spread = jnp.mean(center * center, axis=-1, keepdims=True)
    return center * lax.rsqrt(spread + EPS) * gain


def region_ids(lev_count, lat_rows, lat_total):
    levels = jnp.arange(lev_count, dtype=jnp.int32)
    lev_part = jnp.where(
        levels < lev_count - WIN_LEV, 0, jnp.where(levels < lev_count - SHIFT_LEV, 1, 2)
    )
    lat_part = jnp.where(
        lat_rows < lat_total - WIN_LAT, 0, jnp.where(lat_rows < lat_total - SHIFT_LAT, 1, 2)
    )
    return (lev_part[:, None] * 3 + lat_part[None, :]).astype(jnp.int32)


def to_windows(grid):
    lev_count, row_count, col_count, chans = grid.shape
    split = grid.reshape(
        lev_count // WIN_LEV,
        WIN_LEV,
        row_count // WIN_LAT,
        WIN_LAT,
        col_count // WIN_LON,
        WIN_LON,
        chans,
    )
    return split.transpose(0, 2, 4, 1, 3, 5, 6).reshape(-1, WIN_LEV * WIN_LAT * WIN_LON, chans)


def from_windows(windows, lev_count, row_count, col_count):
    chans = windows.shape[-1]
    split = windows.reshape(
        lev_count // WIN_LEV,
        row_count // WIN_LAT,
        col_count // WIN_LON,
        WIN_LEV,
        WIN_LAT,
        WIN_LON,
        chans,
    )
    return split.transpose(0, 3, 1, 4, 2, 5, 6).reshape(lev_count, row_count, col_count, chans)


def attend(shifted, region, gain_attn, weight_qkv, weight_out):
    lev_count, row_count, col_count, feat_width = shifted.shape
    normed = layer_norm(shifted.astype(jnp.float32), gain_attn).astype(jnp.bfloat16)
    packed = jnp.dot(
        normed.reshape(-1, feat_width), weight_qkv, preferred_element_type=jnp.float32
    ).astype(jnp.bfloat16)
    windows = to_windows(packed.reshape(lev_count, row_count, col_count, 3 * feat_width))
    win_count, span = (windows.shape[0], windows.shape[1])
    windows = windows.reshape(win_count, span, 3, HEADS, HEAD_SIZE)
    query, keys, values_in = (windows[:, :, 0], windows[:, :, 1], windows[:, :, 2])
    scores = jnp.einsum(
        "wqhe,wkhe->whqk", query, keys, preferred_element_type=jnp.float32
    ) * HEAD_SIZE ** (-0.5)
    labels = to_windows(
        jnp.broadcast_to(region[:, :, None, None], (lev_count, row_count, col_count, 1))
    )[:, :, 0]
    same = (labels[:, :, None] == labels[:, None, :])[:, None]
    expo = jnp.where(same, jnp.exp(scores), jnp.float32(0.0))
    attn_probs = (expo / jnp.sum(expo, axis=-1, keepdims=True)).astype(jnp.bfloat16)
    heads_out = jnp.einsum(
        "whqk,wkhe->wqhe", attn_probs, values_in, preferred_element_type=jnp.float32
    ).astype(jnp.bfloat16)
    merged = from_windows(
        heads_out.reshape(win_count, span, feat_width), lev_count, row_count, col_count
    )
    projected = jnp.dot(
        merged.reshape(-1, feat_width), weight_out, preferred_element_type=jnp.float32
    )
    return projected.astype(jnp.bfloat16).reshape(shifted.shape)


def unshift(block):
    rolled = jnp.roll(block, SHIFT_LEV, axis=0)
    back_rows = from_behind(rolled[:, -SHIFT_LAT:], "lat", 1)
    rolled = jnp.concatenate([back_rows, rolled[:, :-SHIFT_LAT]], axis=1)
    back_cols = from_behind(rolled[:, :, -SHIFT_LON:], "lon", 1)
    return jnp.concatenate([back_cols, rolled[:, :, :-SHIFT_LON]], axis=2)


def shards(tokens, gain_attn, weight_qkv, weight_out):
    lev_count, row_count, col_count, feat_width = tokens.shape
    lat_total = row_count * lax.axis_size("lat")
    lat_start = lax.axis_index("lat") * row_count
    east_cols = from_behind(tokens[:, :, :SHIFT_LON], "lon", -1)
    widened = jnp.concatenate([tokens[:, :, SHIFT_LON:], east_cols], axis=2)
    next_rows = from_behind(widened[:, :SHIFT_LAT], "lat", -1)
    moved = jnp.concatenate([widened[:, SHIFT_LAT:], next_rows], axis=1)
    shifted = jnp.roll(moved, -SHIFT_LEV, axis=0)
    lat_rows = lat_start + jnp.arange(row_count, dtype=jnp.int32)
    region = region_ids(lev_count, lat_rows, lat_total)
    attn_out = attend(shifted, region, gain_attn, weight_qkv, weight_out)
    returned = unshift(attn_out)
    return (tokens.astype(jnp.float32) + returned.astype(jnp.float32)).astype(jnp.bfloat16)


def solution(mesh):
    placed = (P(None, "lat", "lon", None), P(), P(), P())
    return jax.shard_map(
        shards, mesh=mesh, in_specs=placed, out_specs=P(None, "lat", "lon", None), check_vma=False
    )
```

profile of v0, /device:TPU:65, one launch (start us, length us, event | category | flops | bytes accessed | tf_op | source)
XLA Modules:
  0.0 139.5 jit_solution(12725526577901555584)
XLA Ops:
  0.0 1.4 fusion.22
  1.4 18.3 %collective-permute-start = (bf16[4,12,6,512]{3,0,2,1:T(4,128)(2,1)S(1)}, bf16[4,12,6,512]{3,0,2,1:T(4,128)(2,1)S(1)}, u32[]{:S(2)}, u32[]{:S(2)}) collective-permute-start(bf16[4,12,6,512]{3,0,2,1:T(4,128)(2,1)S(1)} %get-tuple-element.13), channel_id=1, source_target_pairs={{0,496},{16,0},{32,16},{48,32},{64,48},{80,64},{96,80},{112,96},{1... | collective-permute-start | bytes 884744 | tf_op jit(solution)/shard_map/ppermute | solution.py:21
  20.0 11.4 %collective-permute-done = bf16[4,12,6,512]{3,0,2,1:T(4,128)(2,1)S(1)} collective-permute-done((bf16[4,12,6,512]{3,0,2,1:T(4,128)(2,1)S(1)}, bf16[4,12,6,512]{3,0,2,1:T(4,128)(2,1)S(1)}, u32[]{:S(2)}, u32[]{:S(2)}) %collective-permute-start) | collective-permute-done | bytes 294944 | tf_op jit(solution)/shard_map/ppermute | solution.py:21
  31.5 3.4 %collective-permute-start.1 = (bf16[4,3,12,512]{3,0,2,1:T(4,128)(2,1)S(1)}, bf16[4,3,12,512]{3,0,2,1:T(4,128)(2,1)S(1)}, u32[]{:S(2)}, u32[]{:S(2)}) collective-permute-start(bf16[4,3,12,512]{3,0,2,1:T(4,128)(2,1)S(1)} %pad_maximum_fusion.3), channel_id=1, source_target_pairs={{0,15},{1,0},{2,1},{3,2},{4,3},{5,4},{6,5},{7,6},{8,7},{9,8},{10,9... | collective-permute-start | bytes 442376 | tf_op jit(solution)/shard_map/ppermute | solution.py:21
  35.1 0.3 fusion.14
  35.4 14.9 %collective-permute-done.1 = bf16[4,3,12,512]{3,0,2,1:T(4,128)(2,1)S(1)} collective-permute-done((bf16[4,3,12,512]{3,0,2,1:T(4,128)(2,1)S(1)}, bf16[4,3,12,512]{3,0,2,1:T(4,128)(2,1)S(1)}, u32[]{:S(2)}, u32[]{:S(2)}) %collective-permute-start.1) | collective-permute-done | bytes 147488 | tf_op jit(solution)/shard_map/ppermute | solution.py:21
  50.3 0.5 slice_maximum_fusion
  50.9 0.8 fusion.18
  51.8 0.5 multiply_reduce_fusion
  52.3 1.5 %copy.31 = f32[4,12,12,512]{3,2,1,0:T(8,128)} copy(f32[4,12,12,512]{3,0,2,1:T(4,128)S(1)} %get-tuple-element.6) | data formatting | bytes 2359296 | tf_op jit(solution)/shard_map/convert_element_type | solution.py:71
  54.3 2.6 %reshape.92 = f32[576,512]{1,0:T(8,128)} reshape(f32[4,12,12,512]{3,2,1,0:T(8,128)} %copy.31) | data formatting | bytes 2359296 | tf_op jit(solution)/shard_map/convert_element_type | solution.py:71
  56.9 2.4 %convolution_convert_fusion = bf16[576,1536]{1,0:T(8,128)(2,1)S(1)} fusion(bf16[512,1536]{1,0:T(8,128)(2,1)S(1)} %copy-done, f32[576,512]{1,0:T(8,128)} %reshape.92, f32[512]{0:T(512)S(1)} %copy-done.4, f32[576]{0:T(1024)S(1)} %rsqrt.12, f32[576]{0:T(1024)S(1)} %div.17), kind=kOutput, calls=%fused_computation.3 | convolution fusion | flops 908034048 | bytes 4528640 | tf_op jit(solution)/shard_map/dot_general | solution.py:72
  59.3 2.1 %reshape_reshape.12 = bf16[2,2,2,6,1,12,1536]{6,5,3,2,1,0,4:T(8,128)(2,1)} reshape(bf16[576,1536]{1,0:T(8,128)(2,1)S(1)} %convolution_convert_fusion) | data formatting | bytes 3538944 | tf_op jit(solution)/shard_map/reshape;reshape | solution.py:43
  61.4 3.5 %copy.37 = bf16[2,2,1,2,6,12,1536]{6,1,0,5,4,3,2:T(2,128)(2,1)S(1)} copy(bf16[2,2,1,2,6,12,1536]{6,5,4,1,3,0,2:T(8,128)(2,1)} %bitcast.32) | data formatting | bytes 3538944 | tf_op jit(solution)/shard_map/transpose | solution.py:52
  64.9 3.6 %reshape_reshape.13 = bf16[4,144,3,8,64]{4,3,2,0,1:T(8,128)(2,1)} reshape(bf16[2,2,1,2,6,12,1536]{6,1,0,5,4,3,2:T(2,128)(2,1)S(1)} %copy.37) | data formatting | bytes 3538944 | tf_op jit(solution)/shard_map/reshape;reshape | solution.py:77
  68.5 4.2 %fusion.20 = (bf16[4,144,1,8,64]{4,3,2,0,1:T(8,128)(2,1)}, bf16[4,144,1,8,64]{4,3,2,0,1:T(8,128)(2,1)}, bf16[4,144,1,8,64]{4,3,2,0,1:T(8,128)(2,1)S(1)}) fusion(bf16[4,144,3,8,64]{4,3,2,0,1:T(8,128)(2,1)} %reshape_reshape.13), kind=kLoop, calls=%fused_computation.42 | loop fusion | bytes 3538944 | tf_op jit(solution)/shard_map/slice | solution.py:78
  72.7 2.8 %copy.47 = bf16[4,144,1,8,64]{1,4,3,0,2:T(8,128)(2,1)} copy(bf16[4,144,1,8,64]{4,3,2,0,1:T(8,128)(2,1)} %get-tuple-element.7) | data formatting | bytes 1179648
  75.5 2.8 %copy.48 = bf16[4,144,1,8,64]{1,4,3,0,2:T(8,128)(2,1)} copy(bf16[4,144,1,8,64]{4,3,2,0,1:T(8,128)(2,1)} %get-tuple-element.8) | data formatting | bytes 1179648
  78.3 1.9 %copy.49 = bf16[4,144,1,8,64]{1,4,3,0,2:T(8,128)(2,1)} copy(bf16[4,144,1,8,64]{4,3,2,0,1:T(8,128)(2,1)S(1)} %get-tuple-element.9) | data formatting | bytes 1179648
  80.2 3.0 %fusion = (f32[4,8,144]{2,1,0:T(8,128)S(1)}, f32[4,8,144,144]{2,3,1,0:T(8,128)S(1)}) fusion(pred[4,144,144]{1,2,0:T(8,128)(4,1)S(1)} %broadcast_compare_fusion, bf16[4,144,1,8,64]{1,4,3,0,2:T(8,128)(2,1)} %copy.49, bf16[4,144,1,8,64]{1,4,3,0,2:T(8,128)(2,1)} %copy.48), kind=kOutput, calls=%fused_computation.2 | convolution fusion | flops 86920704 | bytes 3935232 | tf_op jit(solution)/shard_map/wqhe,wkhe->whqk/dot_general | solution.py:79
  83.2 2.3 %fusion.3 = bf16[4,144,8,64]{1,3,2,0:T(8,128)(2,1)} fusion(f32[4,8,144,144]{2,3,1,0:T(8,128)S(1)} %get-tuple-element.15, f32[4,8,144]{2,1,0:T(8,128)S(1)} %get-tuple-element.14, pred[4,144,144]{1,2,0:T(8,128)(4,1)S(1)} %broadcast_compare_fusion, bf16[4,144,1,8,64]{1,4,3,0,2:T(8,128)(2,1)S(1)} %copy-done.2), kind=kOutput, calls=%fused_computation.6 | convolution fusion | flops 87883776 | bytes 3935232 | tf_op jit(solution)/shard_map/whqk,wkhe->wqhe/dot_general | solution.py:88
  85.5 2.1 %copy.42 = bf16[4,144,8,64]{3,2,0,1:T(8,128)(2,1)S(1)} copy(bf16[4,144,8,64]{1,3,2,0:T(8,128)(2,1)} %fusion.3) | data formatting | bytes 1179648 | tf_op jit(solution)/shard_map/convert_element_type | solution.py:90
  87.7 0.6 reshape_reshape.14
  88.6 0.9 copy-done.3
  89.4 0.5 convolution_convert_fusion.1
  90.2 0.4 copy.45
  90.7 2.1 %collective-permute-start.2 = (bf16[4,3,12,512]{3,0,2,1:T(4,128)(2,1)S(1)}, bf16[4,3,12,512]{3,0,2,1:T(4,128)(2,1)S(1)}, u32[]{:S(2)}, u32[]{:S(2)}) collective-permute-start(bf16[4,3,12,512]{3,0,2,1:T(4,128)(2,1)S(1)} %pad_maximum_fusion.2), channel_id=1, source_target_pairs={{0,1},{1,2},{2,3},{3,4},{4,5},{5,6},{6,7},{7,8},{8,9},{9,10},{10,1... | collective-permute-start | bytes 442376 | tf_op jit(solution)/shard_map/ppermute | solution.py:21
  92.8 2.1 %collective-permute-done.2 = bf16[4,3,12,512]{3,0,2,1:T(4,128)(2,1)S(1)} collective-permute-done((bf16[4,3,12,512]{3,0,2,1:T(4,128)(2,1)S(1)}, bf16[4,3,12,512]{3,0,2,1:T(4,128)(2,1)S(1)}, u32[]{:S(2)}, u32[]{:S(2)}) %collective-permute-start.2) | collective-permute-done | bytes 147488 | tf_op jit(solution)/shard_map/ppermute | solution.py:21
  94.9 0.5 fusion.8
  95.6 7.2 %collective-permute-start.3 = (bf16[4,12,6,512]{3,0,2,1:T(4,128)(2,1)S(1)}, bf16[4,12,6,512]{3,0,2,1:T(4,128)(2,1)S(1)}, u32[]{:S(2)}, u32[]{:S(2)}) collective-permute-start(bf16[4,12,6,512]{3,0,2,1:T(4,128)(2,1)S(1)} %get-tuple-element.10), channel_id=1, source_target_pairs={{0,16},{16,32},{32,48},{48,64},{64,80},{80,96},{96,112},{112,128},... | collective-permute-start | bytes 884744 | tf_op jit(solution)/shard_map/ppermute | solution.py:21
  102.8 35.5 %collective-permute-done.3 = bf16[4,12,6,512]{3,0,2,1:T(4,128)(2,1)S(1)} collective-permute-done((bf16[4,12,6,512]{3,0,2,1:T(4,128)(2,1)S(1)}, bf16[4,12,6,512]{3,0,2,1:T(4,128)(2,1)S(1)}, u32[]{:S(2)}, u32[]{:S(2)}) %collective-permute-start.3) | collective-permute-done | bytes 294944 | tf_op jit(solution)/shard_map/ppermute | solution.py:21
  138.3 1.2 add_convert_fusion
  (30 shorter events, 2.0 us)
Async XLA Ops:
  0.0 56.9 %copy-start = (bf16[512,1536]{1,0:T(8,128)(2,1)S(1)}, bf16[512,1536]{1,0:T(8,128)(2,1)}, u32[]{:S(2)}) copy-start(bf16[512,1536]{1,0:T(8,128)(2,1)} %param.6) | copy-start | bytes 4718596
  1.4 30.0 %collective-permute-start = (bf16[4,12,6,512]{3,0,2,1:T(4,128)(2,1)S(1)}, bf16[4,12,6,512]{3,0,2,1:T(4,128)(2,1)S(1)}, u32[]{:S(2)}, u32[]{:S(2)}) collective-permute-start(bf16[4,12,6,512]{3,0,2,1:T(4,128)(2,1)S(1)} %get-tuple-element.13), channel_id=1, source_target_pairs={{0,496},{16,0},{32,16},{48,32},{64,48},{80,64},{96,80},{112,96},{1... | collective-permute-start | bytes 884744 | tf_op jit(solution)/shard_map/ppermute | solution.py:21
  31.5 18.8 %collective-permute-start.1 = (bf16[4,3,12,512]{3,0,2,1:T(4,128)(2,1)S(1)}, bf16[4,3,12,512]{3,0,2,1:T(4,128)(2,1)S(1)}, u32[]{:S(2)}, u32[]{:S(2)}) collective-permute-start(bf16[4,3,12,512]{3,0,2,1:T(4,128)(2,1)S(1)} %pad_maximum_fusion.3), channel_id=1, source_target_pairs={{0,15},{1,0},{2,1},{3,2},{4,3},{5,4},{6,5},{7,6},{8,7},{9,8},{10,9... | collective-permute-start | bytes 442376 | tf_op jit(solution)/shard_map/ppermute | solution.py:21
  54.3 2.6 %copy-start.4 = (f32[512]{0:T(512)S(1)}, f32[512]{0:T(512)}, u32[]{:S(2)}) copy-start(f32[512]{0:T(512)} %param.5) | copy-start | bytes 6148
  80.2 3.0 %copy-start.2 = (bf16[4,144,1,8,64]{1,4,3,0,2:T(8,128)(2,1)S(1)}, bf16[4,144,1,8,64]{1,4,3,0,2:T(8,128)(2,1)}, u32[]{:S(2)}) copy-start(bf16[4,144,1,8,64]{1,4,3,0,2:T(8,128)(2,1)} %copy.47) | copy-start | bytes 1769476
  88.4 1.0 copy-start.3
  90.7 47.6 %copy-start.1 = (bf16[4,12,12,512]{3,0,2,1:T(4,128)(2,1)S(1)}, bf16[4,12,12,512]{3,0,2,1:T(4,128)(2,1)}, u32[]{:S(2)}) copy-start(bf16[4,12,12,512]{3,0,2,1:T(4,128)(2,1)} %param.4) | copy-start | bytes 1769476
  90.7 4.1 %collective-permute-start.2 = (bf16[4,3,12,512]{3,0,2,1:T(4,128)(2,1)S(1)}, bf16[4,3,12,512]{3,0,2,1:T(4,128)(2,1)S(1)}, u32[]{:S(2)}, u32[]{:S(2)}) collective-permute-start(bf16[4,3,12,512]{3,0,2,1:T(4,128)(2,1)S(1)} %pad_maximum_fusion.2), channel_id=1, source_target_pairs={{0,1},{1,2},{2,3},{3,4},{4,5},{5,6},{6,7},{7,8},{8,9},{9,10},{10,1... | collective-permute-start | bytes 442376 | tf_op jit(solution)/shard_map/ppermute | solution.py:21
  95.6 42.7 %collective-permute-start.3 = (bf16[4,12,6,512]{3,0,2,1:T(4,128)(2,1)S(1)}, bf16[4,12,6,512]{3,0,2,1:T(4,128)(2,1)S(1)}, u32[]{:S(2)}, u32[]{:S(2)}) collective-permute-start(bf16[4,12,6,512]{3,0,2,1:T(4,128)(2,1)S(1)} %get-tuple-element.10), channel_id=1, source_target_pairs={{0,16},{16,32},{32,48},{48,64},{64,80},{80,96},{96,112},{112,128},... | collective-permute-start | bytes 884744 | tf_op jit(solution)/shard_map/ppermute | solution.py:21
where the time goes:
time: 140 us
  waiting for transfers between devices  63.9 us (46%)
  local copies, waits for them, and re-layouts  31.8 us (23%)
  starting transfers between devices  31 us (22%)
  matrix products  8.2 us (6%)
  other arithmetic  4.32 us (3%)
    ppermute x4, waiting for transfers between devices, from_behind(): lax.ppermute(value, axis, [(i, (i + by) % count) for i in range(count)])  63.9 us
    ppermute x4, starting transfers between devices, from_behind(): lax.ppermute(value, axis, [(i, (i + by) % count) for i in range(count)])  31 us
    unnamed x13, local copies, waits for them, and re-layouts  8.42 us
    slice x1, local copies, waits for them, and re-layouts, attend(): windows[:, :, 2]  4.2 us
    convert_element_type x2, local copies, waits for them, and re-layouts, attend(): shifted.astype(jnp.float32)  4.16 us
    another operation x1, local copies, waits for them, and re-layouts, attend(): windows = windows.reshape(win_count, span, 3, HEADS, HEAD_SIZE)  3.6 us
    transpose x2, local copies, waits for them, and re-layouts, to_windows(): split.transpose(0, 2, 4, 1, 3, 5, 6)  3.56 us
    dot_general x1, matrix products, attend(): jnp.einsum('wqhe,wkhe->whqk', query, keys, preferred_element_type=jnp.flo...  3.03 us
  transfers between devices with their start and end apart: 4, of which 4 were waited for; matrix products, arithmetic and copies ran while one was open for 0% of the time, Pallas kernels for 0%

commit v1 on v0

v1 whole, which is shorter than its diff:
```python
import jax
import jax.numpy as jnp
from jax import lax
from jax.experimental import pallas as pl
from jax.experimental.pallas import tpu as pltpu
from jax.sharding import PartitionSpec as P

HEADS = 8
HEAD_SIZE = 64
GROUP = 4
EPS = 1e-05
FAR = -1e30
HALF = 6
EDGE = 3


def shift(value, axis, by, wrap):
    count = lax.axis_size(axis)
    pairs = [(i, (i + by) % count) for i in range(count) if wrap or 0 <= i + by < count]
    return lax.ppermute(value, axis, pairs)


def layer_norm(values, gain):
    center = values - jnp.mean(values, axis=-1, keepdims=True)
    spread = jnp.mean(center * center, axis=-1, keepdims=True)
    return (center * lax.rsqrt(spread + EPS) * gain).astype(jnp.bfloat16)


def matmul(a, b):
    return jnp.dot(a, b, preferred_element_type=jnp.float32)


def attend(query, keys, values, bias):
    rows = query.shape[0]
    span = GROUP * HEAD_SIZE
    owner = lax.broadcasted_iota(jnp.int32, (rows, span), 1) // HEAD_SIZE
    tall = jnp.concatenate([bias] * GROUP, axis=0)
    parts = []
    for start in range(0, query.shape[1], span):
        piece = query[:, start : start + span]
        spread = jnp.concatenate(
            [jnp.where(owner == h, piece, 0.0) for h in range(GROUP)], axis=0
        ).astype(jnp.bfloat16)
        scores = lax.dot_general(
            spread,
            keys[:, start : start + span],
            (((1,), (1,)), ((), ())),
            preferred_element_type=jnp.float32,
        )
        scores = scores + tall
        expo = jnp.exp(scores - jnp.max(scores, axis=-1, keepdims=True))
        total = jnp.sum(expo, axis=-1, keepdims=True)
        out = matmul(expo.astype(jnp.bfloat16), values[:, start : start + span]) / total
        merged = jnp.zeros((rows, span), jnp.float32)
        for h in range(GROUP):
            merged = jnp.where(owner == h, out[h * rows : (h + 1) * rows], merged)
        parts.append(merged)
    return jnp.concatenate(parts, axis=1).astype(jnp.bfloat16)


def project(tokens, heads, weight_ref):
    branch = matmul(heads, weight_ref[...]).astype(jnp.bfloat16)
    return (tokens + branch.astype(jnp.float32)).astype(jnp.bfloat16)


def inner_kernel(own_ref, west_ref, east_ref, bias_ref, gain_ref, qkv_ref, out_w_ref, out_ref):
    width = own_ref.shape[-1]
    lo = EDGE * HALF * 4
    hi = own_ref.shape[1] - lo
    own = own_ref[...].astype(jnp.float32)
    halos = [west_ref[...].astype(jnp.float32), east_ref[...].astype(jnp.float32)]
    tokens = jnp.concatenate([own[0, lo:hi], own[1, lo:hi]], axis=0)
    count = hi - lo
    gain = gain_ref[...]
    mine = layer_norm(tokens, gain)
    theirs = layer_norm(jnp.concatenate([h[lo:hi] for h in halos], axis=0), gain)
    query = matmul(mine, qkv_ref[:, :width]).astype(jnp.bfloat16).astype(jnp.float32) * HEAD_SIZE**-0.5
    mine_kv = matmul(mine, qkv_ref[:, width:]).astype(jnp.bfloat16)
    their_kv = matmul(theirs, qkv_ref[:, width:]).astype(jnp.bfloat16)
    heads = []
    for side in range(2):
        at = slice(side * count, (side + 1) * count)
        both = jnp.concatenate([mine_kv[at], their_kv[at]], axis=0)
        heads.append(attend(query[at], both[:, :width], both[:, width:], bias_ref[...]))
    out_ref[...] = project(tokens, jnp.concatenate(heads, axis=0), out_w_ref)


def edge_kernel(own_ref, west_ref, east_ref, lat_ref, far_ref, bias_ref, gain_ref, qkv_ref, out_w_ref, out_ref):
    width = own_ref.shape[-1]
    count = EDGE * HALF * 4
    size = own_ref.shape[1]
    own = own_ref[...].astype(jnp.float32)
    halos = [west_ref[...].astype(jnp.float32), east_ref[...].astype(jnp.float32)]
    gain = gain_ref[...]
    tokens, heads = [], []
    for edge in range(2):
        at = slice(0, count) if edge == 0 else slice(size - count, size)
        for side in range(2):
            mine = own[side, at]
            tokens.append(mine)
            window = jnp.concatenate(
                [
                    mine,
                    halos[side][at],
                    lat_ref[edge, side].astype(jnp.float32),
                    far_ref[edge, side].astype(jnp.float32),
                ],
                axis=0,
            )
            normed = layer_norm(window, gain)
            query = matmul(normed, qkv_ref[:, :width])[:count]
            query = query.astype(jnp.bfloat16).astype(jnp.float32) * HEAD_SIZE**-0.5
            kv = matmul(normed, qkv_ref[:, width:]).astype(jnp.bfloat16)
            heads.append(attend(query, kv[:, :width], kv[:, width:], bias_ref[edge]))
    tokens = jnp.concatenate(tokens, axis=0)
    heads = jnp.concatenate([h.astype(jnp.float32) for h in heads], axis=0).astype(jnp.bfloat16)
    out_ref[...] = project(tokens, heads, out_w_ref)


def call(kernel, rows, flops, *operands):
    width = operands[0].shape[-1]
    moved = sum(x.size * x.dtype.itemsize for x in operands) + rows * width * 2
    vmem = pl.BlockSpec(memory_space=pltpu.VMEM)
    return pl.pallas_call(
        kernel,
        out_shape=jax.ShapeDtypeStruct((rows, width), jnp.bfloat16),
        in_specs=[vmem] * len(operands),
        out_specs=vmem,
        compiler_params=pltpu.CompilerParams(vmem_limit_bytes=40 * 2**20),
        cost_estimate=pl.CostEstimate(flops=flops, bytes_accessed=moved, transcendentals=rows * 2048),
    )(*operands)


def level_parts(count):
    level = jnp.arange(count, dtype=jnp.int32) % 4
    return jnp.where(level == 0, 2, jnp.where(level == 3, 1, 0))


def shards(tokens, gain_attn, weight_qkv, weight_out):
    lev_count, row_count, col_count, width = tokens.shape
    edge = EDGE * HALF * lev_count
    rows = row_count * HALF * lev_count
    halves = tokens.transpose(1, 2, 0, 3).reshape(row_count, 2, HALF, lev_count, width)
    own = halves.transpose(1, 0, 2, 3, 4).reshape(2, rows, width)
    east = shift(own[0], "lon", -1, True)
    west = shift(own[1], "lon", 1, True)
    south = shift(own[:, :edge], "lat", -1, False)
    north = shift(own[:, rows - edge :], "lat", 1, False)
    halos = jnp.stack([west, east])
    far_south = shift(halos[:, :edge], "lat", -1, False)
    far_north = shift(halos[:, rows - edge :], "lat", 1, False)

    gain = gain_attn.reshape(1, width)
    inner = rows - 2 * edge
    same = level_parts(inner)[:, None] == level_parts(2 * inner)[None, :]
    inner_bias = jnp.where(same, 0.0, FAR).astype(jnp.float32)
    same = level_parts(edge)[:, None] == level_parts(4 * edge)[None, :]
    here = jnp.arange(4 * edge) < 2 * edge
    place = lax.axis_index("lat")
    open_edges = jnp.stack([place > 0, place < lax.axis_size("lat") - 1])
    reach = same[None] & (here[None, None, :] | open_edges[:, None, None])
    edge_bias = jnp.where(reach, 0.0, FAR).astype(jnp.float32)

    middle = call(
        inner_kernel, 2 * inner, 1_400_000_000, own, west, east, inner_bias, gain, weight_qkv, weight_out
    )
    edges = call(
        edge_kernel,
        4 * edge,
        2_400_000_000,
        own,
        west,
        east,
        jnp.stack([north, south]),
        jnp.stack([far_north, far_south]),
        edge_bias,
        gain,
        weight_qkv,
        weight_out,
    )
    edges = edges.reshape(2, 2, edge, width)
    middle = middle.reshape(2, inner, width)
    mixed = jnp.concatenate([edges[0], middle, edges[1]], axis=1)
    mixed = mixed.reshape(2, row_count, HALF, lev_count, width).transpose(1, 0, 2, 3, 4)
    return mixed.reshape(row_count, col_count, lev_count, width).transpose(2, 0, 1, 3)


def solution(mesh):
    placed = (P(None, "lat", "lon", None), P(), P(), P())
    return jax.shard_map(
        shards, mesh=mesh, in_specs=placed, out_specs=P(None, "lat", "lon", None), check_vma=False
    )
```

time: 140 us -> 86.4 us (0.62)
  the two profiles are of different devices: /device:TPU:65 before, /device:TPU:1 now
where the time goes in v1:
time: 86.4 us; the launch traced here: 86.1 us
  starting transfers between devices  51.1 us (59%)
  waiting for transfers between devices  20.6 us (24%)
  Pallas kernels  7.57 us (9%)
  local copies, waits for them, and re-layouts  5.18 us (6%)
  other arithmetic  1.4 us (2%)
    ppermute x6, starting transfers between devices, shift(): return lax.ppermute(value, axis, pairs)  51.1 us
    ppermute x6, waiting for transfers between devices, shift(): return lax.ppermute(value, axis, pairs)  20.6 us
    pallas_call x2, Pallas kernels, call(): pl.pallas_call(kernel, out_shape=jax.ShapeDtypeStruct((rows, width), jnp....  7.57 us
  transfers between devices with their start and end apart: 6, of which 2 were waited for; matrix products, arithmetic and copies ran while one was open for 3% of the time, Pallas kernels for 3%

profile of v1, /device:TPU:1, one launch (start us, length us, event | category | flops | bytes accessed | tf_op | source)
XLA Modules:
  0.0 86.1 jit_solution(10850678995999852493)
XLA Ops:
  0.0 1.3 %copy.8 = bf16[12,2,6,4,512]{4,3,2,0,1:T(4,128)(2,1)S(1)} copy(bf16[12,2,6,4,512]{4,3,2,1,0:T(4,128)(2,1)} %bitcast.32) | data formatting | bytes 1179648 | tf_op jit(solution)/shard_map/reshape | solution.py:143
  1.3 0.2 fusion.6
  1.5 0.8 squeeze.12
  2.3 16.3 %collective-permute-start = (bf16[288,512]{1,0:T(8,128)(2,1)}, bf16[288,512]{1,0:T(8,128)(2,1)S(1)}, u32[]{:S(2)}, u32[]{:S(2)}) collective-permute-start(bf16[288,512]{1,0:T(8,128)(2,1)} %squeeze.12), channel_id=1, source_target_pairs={{0,16},{16,32},{32,48},{48,64},{64,80},{80,96},{96,112},{112,128},... | collective-permute-start | bytes 884744 | tf_op jit(solution)/shard_map/ppermute | solution.py:20
  18.5 0.8 squeeze.13
  19.3 6.6 %collective-permute-start.1 = (bf16[288,512]{1,0:T(8,128)(2,1)}, bf16[288,512]{1,0:T(8,128)(2,1)S(1)}, u32[]{:S(2)}, u32[]{:S(2)}) collective-permute-start(bf16[288,512]{1,0:T(8,128)(2,1)} %squeeze.13), channel_id=1, source_target_pairs={{0,496},{16,0},{32,16},{48,32},{64,48},{80,64},{96,80},{112,96},{1... | collective-permute-start | bytes 884744 | tf_op jit(solution)/shard_map/ppermute | solution.py:20
  25.9 0.1 reshape.127.own_ref
  26.0 0.0 copy-start
  26.0 0.0 copy-start.1
  26.1 0.0 copy-start.2
  26.1 0.7 fusion.5
  26.8 3.5 %collective-permute-start.2 = (bf16[2,72,512]{2,1,0:T(8,128)(2,1)}, bf16[2,72,512]{2,1,0:T(8,128)(2,1)S(1)}, u32[]{:S(2)}, u32[]{:S(2)}) collective-permute-start(bf16[2,72,512]{2,1,0:T(8,128)(2,1)} %get-tuple-element.7), channel_id=1, source_target_pairs={{0,1},{1,2},{2,3},{3,4},{4,5},{5,6},{6,7},{7,8},{8,9},{9,10},{10,1... | collective-permute-start | bytes 442376 | tf_op jit(solution)/shard_map/ppermute | solution.py:20
  30.3 2.5 %collective-permute-start.3 = (bf16[2,72,512]{2,1,0:T(8,128)(2,1)}, bf16[2,72,512]{2,1,0:T(8,128)(2,1)}, u32[]{:S(2)}, u32[]{:S(2)}) collective-permute-start(bf16[2,72,512]{2,1,0:T(8,128)(2,1)} %get-tuple-element.8), channel_id=1, source_target_pairs={{1,0},{2,1},{3,2},{4,3},{5,4},{6,5},{7,6},{8,7},{9,8},{10,9},{11,1... | collective-permute-start | bytes 442376 | tf_op jit(solution)/shard_map/ppermute | solution.py:20
  32.9 0.1 pad_add_fusion
  33.0 0.1 broadcast_or_fusion
  33.0 0.1 broadcast_compare_fusion
  33.2 0.1 compare_select_fusion.bias_ref
  33.3 0.0 collective-permute-done.west_ref
  33.3 20.0 %collective-permute-done.1.east_ref = bf16[288,512]{1,0:T(8,128)(2,1)S(1)} collective-permute-done((bf16[288,512]{1,0:T(8,128)(2,1)}, bf16[288,512]{1,0:T(8,128)(2,1)S(1)}, u32[]{:S(2)}, u32[]{:S(2)}) %collective-permute-start.1) | collective-permute-done | bytes 294944 | tf_op jit(solution)/shard_map/ppermute | solution.py:20
  53.3 20.3 %collective-permute-start.4 = (bf16[2,72,512]{2,1,0:T(8,128)(2,1)S(1)}, bf16[2,72,512]{2,1,0:T(8,128)(2,1)S(1)}, u32[]{:S(2)}, u32[]{:S(2)}) collective-permute-start(bf16[2,72,512]{2,1,0:T(8,128)(2,1)S(1)} %get-tuple-element.5), channel_id=1, source_target_pairs={{0,1},{1,2},{2,3},{3,4},{4,5},{5,6},{6,7},{7,8},{8,9},{9,10},{10,1... | collective-permute-start | bytes 442376 | tf_op jit(solution)/shard_map/ppermute | solution.py:20
  73.6 1.9 %collective-permute-start.5 = (bf16[2,72,512]{2,1,0:T(8,128)(2,1)S(1)}, bf16[2,72,512]{2,1,0:T(8,128)(2,1)S(1)}, u32[]{:S(2)}, u32[]{:S(2)}) collective-permute-start(bf16[2,72,512]{2,1,0:T(8,128)(2,1)S(1)} %get-tuple-element.6), channel_id=1, source_target_pairs={{1,0},{2,1},{3,2},{4,3},{5,4},{6,5},{7,6},{8,7},{9,8},{10,9},{11,1... | collective-permute-start | bytes 442376 | tf_op jit(solution)/shard_map/ppermute | solution.py:20
  75.6 0.0 collective-permute-done.2
  75.6 0.0 collective-permute-done.3
  75.6 0.9 %pad_maximum_fusion.1.lat_ref = bf16[2,2,72,512]{3,2,1,0:T(8,128)(2,1)S(1)} fusion(bf16[1,2,72,512]{3,2,1,0:T(8,128)(2,1)} %bitcast.4, bf16[1,2,72,512]{3,2,1,0:T(8,128)(2,1)S(1)} %bitcast.33), kind=kLoop, calls=%fused_computation.2 | loop fusion | flops 147456 | bytes 589824 | tf_op jit(solution)/shard_map/stack | solution.py:174
  76.5 0.0 copy-done
  76.5 0.0 copy-done.1
  76.6 2.9 %shard_map.47 = bf16[288,512]{1,0:T(8,128)(2,1)S(1)} custom-call(bf16[2,288,512]{2,1,0:T(8,128)(2,1)S(1)} %reshape.127.own_ref, bf16[288,512]{1,0:T(8,128)(2,1)S(1)} %collective-permute-done.west_ref, bf16[288,512]{1,0:T(8,128)(2,1)S(1)} %collective-permute-done.1.east_ref, f32[144,288]{1,0:T(8,128)S(1)} %compare_select_fusion.bias_ref, ...), custom_call_target="tpu_custom_call" | custom-call | flops 1400000000 | bytes 3739648 | tf_op jit(solution)/shard_map/pallas_call | solution.py:124
  79.5 0.0 collective-permute-done.4
  79.5 0.6 collective-permute-done.5
  80.1 4.7 %shard_map.46 = bf16[288,512]{1,0:T(8,128)(2,1)S(1)} custom-call(bf16[2,288,512]{2,1,0:T(8,128)(2,1)S(1)} %reshape.127.own_ref, bf16[288,512]{1,0:T(8,128)(2,1)S(1)} %collective-permute-done.west_ref, bf16[288,512]{1,0:T(8,128)(2,1)S(1)} %collective-permute-done.1.east_ref, bf16[2,2,72,512]{3,2,1,0:T(8,128)(2,1)S(1)} %pad_maximum_fusion.1.lat_ref, ...), custom_call_target="tpu_custom_call" | custom-call | flops 2400000000 | bytes 4329472 | tf_op jit(solution)/shard_map/pallas_call | solution.py:124
  84.9 0.1 reshape.130
  85.0 1.1 %copy.6 = bf16[2,12,6,4,512]{4,3,2,0,1:T(4,128)(2,1)} copy(bf16[2,12,6,4,512]{4,3,2,1,0:T(4,128)(2,1)S(1)} %reshape.130) | data formatting | bytes 1179648 | tf_op jit(solution)/shard_map/reshape | solution.py:184
  (10 shorter events, 0.2 us)
Async XLA Ops:
  2.3 31.0 %collective-permute-start = (bf16[288,512]{1,0:T(8,128)(2,1)}, bf16[288,512]{1,0:T(8,128)(2,1)S(1)}, u32[]{:S(2)}, u32[]{:S(2)}) collective-permute-start(bf16[288,512]{1,0:T(8,128)(2,1)} %squeeze.12), channel_id=1, source_target_pairs={{0,16},{16,32},{32,48},{48,64},{64,80},{80,96},{96,112},{112,128},... | collective-permute-start | bytes 884744 | tf_op jit(solution)/shard_map/ppermute | solution.py:20
  19.3 33.9 %collective-permute-start.1 = (bf16[288,512]{1,0:T(8,128)(2,1)}, bf16[288,512]{1,0:T(8,128)(2,1)S(1)}, u32[]{:S(2)}, u32[]{:S(2)}) collective-permute-start(bf16[288,512]{1,0:T(8,128)(2,1)} %squeeze.13), channel_id=1, source_target_pairs={{0,496},{16,0},{32,16},{48,32},{64,48},{80,64},{96,80},{112,96},{1... | collective-permute-start | bytes 884744 | tf_op jit(solution)/shard_map/ppermute | solution.py:20
  26.0 50.5 %copy-start = (bf16[512,1536]{1,0:T(8,128)(2,1)S(1)}, bf16[512,1536]{1,0:T(8,128)(2,1)}, u32[]{:S(2)}) copy-start(bf16[512,1536]{1,0:T(8,128)(2,1)} %qkv_ref.3) | copy-start | bytes 4718596
  26.0 50.5 %copy-start.1 = (bf16[512,512]{1,0:T(8,128)(2,1)S(1)}, bf16[512,512]{1,0:T(8,128)(2,1)}, u32[]{:S(2)}) copy-start(bf16[512,512]{1,0:T(8,128)(2,1)} %out_w_ref.3) | copy-start | bytes 1572868
  26.1 50.5 %copy-start.2 = (f32[512]{0:T(512)S(1)}, f32[512]{0:T(512)}, u32[]{:S(2)}) copy-start(f32[512]{0:T(512)} %param.5) | copy-start | bytes 6148
  26.8 48.8 %collective-permute-start.2 = (bf16[2,72,512]{2,1,0:T(8,128)(2,1)}, bf16[2,72,512]{2,1,0:T(8,128)(2,1)S(1)}, u32[]{:S(2)}, u32[]{:S(2)}) collective-permute-start(bf16[2,72,512]{2,1,0:T(8,128)(2,1)} %get-tuple-element.7), channel_id=1, source_target_pairs={{0,1},{1,2},{2,3},{3,4},{4,5},{5,6},{6,7},{7,8},{8,9},{9,10},{10,1... | collective-permute-start | bytes 442376 | tf_op jit(solution)/shard_map/ppermute | solution.py:20
  30.3 45.3 %collective-permute-start.3 = (bf16[2,72,512]{2,1,0:T(8,128)(2,1)}, bf16[2,72,512]{2,1,0:T(8,128)(2,1)}, u32[]{:S(2)}, u32[]{:S(2)}) collective-permute-start(bf16[2,72,512]{2,1,0:T(8,128)(2,1)} %get-tuple-element.8), channel_id=1, source_target_pairs={{1,0},{2,1},{3,2},{4,3},{5,4},{6,5},{7,6},{8,7},{9,8},{10,9},{11,1... | collective-permute-start | bytes 442376 | tf_op jit(solution)/shard_map/ppermute | solution.py:20
  53.3 26.2 %collective-permute-start.4 = (bf16[2,72,512]{2,1,0:T(8,128)(2,1)S(1)}, bf16[2,72,512]{2,1,0:T(8,128)(2,1)S(1)}, u32[]{:S(2)}, u32[]{:S(2)}) collective-permute-start(bf16[2,72,512]{2,1,0:T(8,128)(2,1)S(1)} %get-tuple-element.5), channel_id=1, source_target_pairs={{0,1},{1,2},{2,3},{3,4},{4,5},{5,6},{6,7},{7,8},{8,9},{9,10},{10,1... | collective-permute-start | bytes 442376 | tf_op jit(solution)/shard_map/ppermute | solution.py:20
  73.6 6.5 %collective-permute-start.5 = (bf16[2,72,512]{2,1,0:T(8,128)(2,1)S(1)}, bf16[2,72,512]{2,1,0:T(8,128)(2,1)S(1)}, u32[]{:S(2)}, u32[]{:S(2)}) collective-permute-start(bf16[2,72,512]{2,1,0:T(8,128)(2,1)S(1)} %get-tuple-element.6), channel_id=1, source_target_pairs={{1,0},{2,1},{3,2},{4,3},{5,4},{6,5},{7,6},{8,7},{9,8},{10,9},{11,1... | collective-permute-start | bytes 442376 | tf_op jit(solution)/shard_map/ppermute | solution.py:20

commit v2 on v1

v2 whole, which is shorter than its diff:
```python
import jax
import jax.numpy as jnp
from jax import lax
from jax.experimental import pallas as pl
from jax.experimental.pallas import tpu as pltpu
from jax.sharding import PartitionSpec as P

HEADS = 8
HEAD_SIZE = 64
GROUP = 4
SPAN = GROUP * HEAD_SIZE
EPS = 1e-05
FAR = -1e30
HALF = 6
EDGE = 3
LEVELS = 4
RIM = EDGE * HALF * LEVELS


def shift(value, axis, by, wrap):
    count = lax.axis_size(axis)
    pairs = [(i, (i + by) % count) for i in range(count) if wrap or 0 <= i + by < count]
    return lax.ppermute(value, axis, pairs)


def layer_norm(values, gain):
    center = values - jnp.mean(values, axis=-1, keepdims=True)
    spread = jnp.mean(center * center, axis=-1, keepdims=True)
    return (center * lax.rsqrt(spread + EPS) * gain).astype(jnp.bfloat16)


def matmul(a, b):
    return jnp.dot(a, b, preferred_element_type=jnp.float32)


def rounded(values):
    return values.astype(jnp.bfloat16).astype(jnp.float32)


def level_bias(rows, keys):
    def part(axis):
        level = lax.broadcasted_iota(jnp.int32, (rows, keys), axis) % LEVELS
        return jnp.where(level == 0, 2, jnp.where(level == LEVELS - 1, 1, 0))

    return jnp.where(part(0) == part(1), 0.0, FAR).astype(jnp.float32)


def attend(query, keys, values, bias):
    rows = query.shape[0]
    owner = lax.broadcasted_iota(jnp.int32, (rows, SPAN), 1) // HEAD_SIZE
    tall = jnp.concatenate([bias] * GROUP, axis=0)

    def merge(tall_values):
        merged = jnp.broadcast_to(tall_values[:rows], (rows, SPAN))
        for h in range(1, GROUP):
            merged = jnp.where(owner == h, tall_values[h * rows : (h + 1) * rows], merged)
        return merged

    parts = []
    for start in range(0, query.shape[1], SPAN):
        piece = query[:, start : start + SPAN]
        spread = jnp.concatenate(
            [jnp.where(owner == h, piece, 0.0) for h in range(GROUP)], axis=0
        ).astype(jnp.bfloat16)
        scores = lax.dot_general(
            spread,
            keys[:, start : start + SPAN],
            (((1,), (1,)), ((), ())),
            preferred_element_type=jnp.float32,
        )
        scores = scores + tall
        top = jnp.max(scores, axis=-1, keepdims=True)
        expo = jnp.exp(scores - top)
        total = jnp.sum(expo, axis=-1, keepdims=True)
        out = matmul(expo.astype(jnp.bfloat16), values[:, start : start + SPAN])
        parts.append((merge(out), merge(top), merge(total)))
    return tuple(jnp.concatenate(p, axis=1) for p in zip(*parts))


def add_keys(state, more):
    out, top, total = state
    out_2, top_2, total_2 = more
    peak = jnp.maximum(top, top_2)
    old, new = jnp.exp(top - peak), jnp.exp(top_2 - peak)
    return out * old + out_2 * new, peak, total * old + total_2 * new


def load(ref, at):
    return tuple(ref[i, at] for i in range(3))


def store(ref, at, state):
    for i in range(3):
        ref[i, at] = state[i]


def project(tokens, state, weight_ref):
    out, _, total = state
    branch = matmul((out / total).astype(jnp.bfloat16), weight_ref[...])
    return (tokens + rounded(branch)).astype(jnp.bfloat16)


def own_kernel(closed_ref, west_ref, east_ref, north_ref, south_ref, gain_ref, qkv_ref, query_ref, state_ref):
    width = west_ref.shape[-1]
    rows = west_ref.shape[0]
    gain = gain_ref[...]
    mine = jnp.concatenate([r[...].astype(jnp.float32) for r in (west_ref, east_ref)], axis=0)
    theirs = jnp.concatenate([r[s].astype(jnp.float32) for r in (north_ref, south_ref) for s in range(2)], axis=0)
    mine = layer_norm(mine, gain)
    theirs = layer_norm(theirs, gain)
    query = rounded(matmul(mine, qkv_ref[:, :width])) * HEAD_SIZE**-0.5
    query_ref[...] = query
    mine = matmul(mine, qkv_ref[:, width:])
    theirs = matmul(theirs, qkv_ref[:, width:])
    inner = level_bias(rows - 2 * RIM, rows - 2 * RIM)
    rim = level_bias(RIM, 2 * RIM)
    distant = lax.broadcasted_iota(jnp.int32, (RIM, 2 * RIM), 1) >= RIM
    for side in range(2):
        base = side * rows
        at = slice(base + RIM, base + rows - RIM)
        kv = mine[at].astype(jnp.bfloat16)
        store(state_ref, at, attend(query[at], kv[:, :width], kv[:, width:], inner))
        for edge in range(2):
            begin = base + edge * (rows - RIM)
            at = slice(begin, begin + RIM)
            beyond = (edge * 2 + side) * RIM
            kv = jnp.concatenate([mine[at], theirs[beyond : beyond + RIM]], axis=0).astype(jnp.bfloat16)
            bias = rim + jnp.where(distant, closed_ref[edge], 0.0)
            store(state_ref, at, attend(query[at], kv[:, :width], kv[:, width:], bias))


def halo_kernel(
    query_ref, state_ref, own_w_ref, own_e_ref, west_ref, east_ref, gain_ref, qkv_ref, out_w_ref, out_ref, rim_ref
):
    width = west_ref.shape[-1]
    rows = west_ref.shape[0]
    halos = jnp.concatenate([r[...].astype(jnp.float32) for r in (west_ref, east_ref)], axis=0)
    halos = matmul(layer_norm(halos, gain_ref[...]), qkv_ref[:, width:])
    inner = level_bias(rows - 2 * RIM, rows - 2 * RIM)
    rim = level_bias(RIM, RIM)
    done, tokens = [], []
    for side in range(2):
        base = side * rows
        for edge in range(2):
            begin = base + edge * (rows - RIM)
            at = slice(begin, begin + RIM)
            kv = halos[at].astype(jnp.bfloat16)
            more = attend(query_ref[at], kv[:, :width], kv[:, width:], rim)
            place = (edge * 2 + side) * RIM
            store(rim_ref, slice(place, place + RIM), add_keys(load(state_ref, at), more))
        at = slice(base + RIM, base + rows - RIM)
        kv = halos[at].astype(jnp.bfloat16)
        more = attend(query_ref[at], kv[:, :width], kv[:, width:], inner)
        done.append(add_keys(load(state_ref, at), more))
        tokens.append((own_w_ref, own_e_ref)[side][...].astype(jnp.float32)[RIM : rows - RIM])
    done = tuple(jnp.concatenate(p, axis=0) for p in zip(*done))
    out_ref[...] = project(jnp.concatenate(tokens, axis=0), done, out_w_ref)


def corner_kernel(
    closed_ref,
    query_ref,
    rim_ref,
    own_w_ref,
    own_e_ref,
    north_ref,
    south_ref,
    middle_ref,
    gain_ref,
    qkv_ref,
    out_w_ref,
    out_ref,
):
    width = own_w_ref.shape[-1]
    rows = own_w_ref.shape[0]
    corners = jnp.concatenate([r[s].astype(jnp.float32) for r in (north_ref, south_ref) for s in range(2)], axis=0)
    corners = matmul(layer_norm(corners, gain_ref[...]), qkv_ref[:, width:])
    rim = level_bias(RIM, RIM)
    own = [r[...].astype(jnp.float32) for r in (own_w_ref, own_e_ref)]
    done, tokens = [], []
    for edge in range(2):
        for side in range(2):
            begin = edge * (rows - RIM)
            at = slice(begin, begin + RIM)
            place = (edge * 2 + side) * RIM
            kv = corners[place : place + RIM].astype(jnp.bfloat16)
            query = query_ref[slice(side * rows + begin, side * rows + begin + RIM)]
            more = attend(query, kv[:, :width], kv[:, width:], rim + closed_ref[edge])
            done.append(add_keys(load(rim_ref, slice(place, place + RIM)), more))
            tokens.append(own[side][at])
    done = tuple(jnp.concatenate(p, axis=0) for p in zip(*done))
    mixed = project(jnp.concatenate(tokens, axis=0), done, out_w_ref).astype(jnp.float32)
    middle = middle_ref[...].astype(jnp.float32)
    count = rows - 2 * RIM
    for side in range(2):
        out_ref[side] = jnp.concatenate(
            [
                mixed[side * RIM : (side + 1) * RIM],
                middle[side * count : (side + 1) * count],
                mixed[(2 + side) * RIM : (3 + side) * RIM],
            ],
            axis=0,
        ).astype(jnp.bfloat16)


def call(kernel, results, flops, *operands):
    moved = sum(x.size * x.dtype.itemsize for x in (*operands, *results))
    specs = [pl.BlockSpec(memory_space=pltpu.SMEM if x.ndim == 1 else pltpu.VMEM) for x in operands]
    return pl.pallas_call(
        kernel,
        out_shape=results,
        in_specs=specs,
        out_specs=[pl.BlockSpec(memory_space=pltpu.VMEM)] * len(results),
        compiler_params=pltpu.CompilerParams(vmem_limit_bytes=40 * 2**20),
        cost_estimate=pl.CostEstimate(flops=flops, bytes_accessed=moved, transcendentals=0),
    )(*operands)


def shards(tokens, gain_attn, weight_qkv, weight_out):
    lev_count, row_count, col_count, width = tokens.shape
    rows = row_count * HALF * lev_count
    by_place = tokens.transpose(1, 2, 0, 3)
    own_w = by_place[:, :HALF].reshape(rows, width)
    own_e = by_place[:, HALF:].reshape(rows, width)
    east = shift(own_w, "lon", -1, True)
    west = shift(own_e, "lon", 1, True)

    def both(a, b, at):
        return jnp.stack([a[at], b[at]])

    top, bottom = slice(0, RIM), slice(rows - RIM, rows)
    south = shift(both(own_w, own_e, top), "lat", -1, False)
    north = shift(both(own_w, own_e, bottom), "lat", 1, False)
    far_south = shift(both(west, east, top), "lat", -1, False)
    far_north = shift(both(west, east, bottom), "lat", 1, False)

    gain = gain_attn.reshape(1, width)
    place = lax.axis_index("lat")
    closed = jnp.stack([place == 0, place == lax.axis_size("lat") - 1])
    closed = jnp.where(closed, FAR, 0.0).astype(jnp.float32)

    def shape(*dims, dtype=jnp.float32):
        return jax.ShapeDtypeStruct(dims, dtype)

    query, state = call(
        own_kernel,
        [shape(2 * rows, width), shape(3, 2 * rows, width)],
        2_400_000_000,
        closed,
        own_w,
        own_e,
        north,
        south,
        gain,
        weight_qkv,
    )
    middle, rim = call(
        halo_kernel,
        [shape(2 * (rows - 2 * RIM), width, dtype=jnp.bfloat16), shape(3, 4 * RIM, width)],
        1_500_000_000,
        query,
        state,
        own_w,
        own_e,
        west,
        east,
        gain,
        weight_qkv,
        weight_out,
    )
    (mixed,) = call(
        corner_kernel,
        [shape(2, rows, width, dtype=jnp.bfloat16)],
        1_000_000_000,
        closed,
        query,
        rim,
        own_w,
        own_e,
        far_north,
        far_south,
        middle,
        gain,
        weight_qkv,
        weight_out,
    )
    mixed = mixed.reshape(2, row_count, HALF, lev_count, width).transpose(1, 0, 2, 3, 4)
    return mixed.reshape(row_count, col_count, lev_count, width).transpose(2, 0, 1, 3)


def solution(mesh):
    placed = (P(None, "lat", "lon", None), P(), P(), P())
    return jax.shard_map(
        shards, mesh=mesh, in_specs=placed, out_specs=P(None, "lat", "lon", None), check_vma=False
    )
```

time: 86.4 us -> 91.2 us (1.056)
  waiting for transfers between devices: 20.6 us -> 44.1 us
  starting transfers between devices: 51.1 us -> 33 us
  Pallas kernels: 7.57 us -> 10.4 us
  local copies, waits for them, and re-layouts: 5.18 us -> 2.93 us
  other arithmetic: 1.4 us -> 0.15 us
    ppermute x6, waiting for transfers between devices: 20.6 us -> 44.1 us  [shift(): return lax.ppermute(value, axis, pairs)]
    ppermute x6, starting transfers between devices: 51.1 us -> 33 us  [shift(): return lax.ppermute(value, axis, pairs)]
    pallas_call x2 -> x3, Pallas kernels: 7.57 us -> 10.4 us  [call(): pl.pallas_call(kernel, out_shape=results, in_specs=specs, out_specs=[pl.B...]
    squeeze x2 -> x0, local copies, waits for them, and re-layouts: 1.58 us -> none  [the longest x1 0.79 us: shards(): east = shift(own[0], 'lon', -1, True)]
    reshape x2, local copies, waits for them, and re-layouts: 1.4 us -> 0.15 us  [the longest x1 0.07 us: shards(): own_w = by_place[:, :HALF].reshape(rows, width)]
    reshape x2 -> x1, local copies, waits for them, and re-layouts: 1.22 us -> 0.14 us  [shards(): mixed.reshape(2, row_count, HALF, lev_count, width).transpose(1, 0, 2, 3, 4)]
    transpose x0 -> x1, local copies, waits for them, and re-layouts: none -> 1.08 us  [shards(): mixed.reshape(2, row_count, HALF, lev_count, width).transpose(1, 0, 2, 3, 4)]
    another operation x3 -> x4, other arithmetic: 1.05 us -> 0.07 us  [both(): return jnp.stack([a[at], b[at]])]
  transfers between devices with their start and end apart: 6 -> 6, of which waited for: 2 -> 1; matrix products, arithmetic and copies ran while one was open for 3% -> 0% of each run, Pallas kernels for 3% -> 9%
where the time goes in v2:
time: 91.2 us; the launch traced here: 90.9 us
  waiting for transfers between devices  44.1 us (48%)
  starting transfers between devices  33 us (36%)
  Pallas kernels  10.4 us (11%)
  local copies, waits for them, and re-layouts  2.93 us (3%)
    ppermute x6, waiting for transfers between devices, shift(): return lax.ppermute(value, axis, pairs)  44.1 us
    ppermute x6, starting transfers between devices, shift(): return lax.ppermute(value, axis, pairs)  33 us
    pallas_call x3, Pallas kernels, call(): pl.pallas_call(kernel, out_shape=results, in_specs=specs, out_specs=[pl.B...  10.4 us
  transfers between devices with their start and end apart: 6, of which 1 were waited for; matrix products, arithmetic and copies ran while one was open for 0% of the time, Pallas kernels for 9%

profile of v2, /device:TPU:1, one launch (start us, length us, event | category | flops | bytes accessed | tf_op | source)
XLA Modules:
  0.0 90.9 jit_solution(6094328194315372662)
XLA Ops:
  0.0 0.0 copy-start.3
  0.0 1.3 %fusion.1 = (bf16[12,6,4,512]{3,2,1,0:T(4,128)(2,1)S(1)}, bf16[12,6,4,512]{3,2,1,0:T(4,128)(2,1)S(1)}) fusion(bf16[12,12,4,512]{3,2,1,0:T(4,128)(2,1)} %bitcast.20), kind=kLoop, calls=%fused_computation.10 | loop fusion | bytes 1179648 | tf_op jit(solution)/shard_map/slice | solution.py:224
  1.3 0.1 reshape.24.east_ref.own_e_ref
  1.4 0.0 copy-start
  1.4 0.0 copy-start.2
  1.4 16.4 %collective-permute-start.2 = (bf16[288,512]{1,0:T(8,128)(2,1)S(1)}, bf16[288,512]{1,0:T(8,128)(2,1)S(1)}, u32[]{:S(2)}, u32[]{:S(2)}) collective-permute-start(bf16[288,512]{1,0:T(8,128)(2,1)S(1)} %reshape.24.east_ref.own_e_ref), channel_id=1, source_target_pairs={{0,16},{16,32},{32,48},{48,64},{64,80},{80,96},{96,112},{112,128},... | collective-permute-start | bytes 884744 | tf_op jit(solution)/shard_map/ppermute | solution.py:23
  17.8 0.0 copy-done.3
  17.8 0.1 fusion
  18.0 3.5 %collective-permute-start = (bf16[2,72,512]{2,1,0:T(8,128)(2,1)S(1)}, bf16[2,72,512]{2,1,0:T(8,128)(2,1)S(1)}, u32[]{:S(2)}, u32[]{:S(2)}) collective-permute-start(bf16[2,72,512]{2,1,0:T(8,128)(2,1)S(1)} %pad_maximum_fusion), channel_id=1, source_target_pairs={{0,1},{1,2},{2,3},{3,4},{4,5},{5,6},{6,7},{7,8},{8,9},{9,10},{10,1... | collective-permute-start | bytes 442376 | tf_op jit(solution)/shard_map/ppermute | solution.py:23
  21.6 1.9 %collective-permute-start.1 = (bf16[2,72,512]{2,1,0:T(8,128)(2,1)S(1)}, bf16[2,72,512]{2,1,0:T(8,128)(2,1)S(1)}, u32[]{:S(2)}, u32[]{:S(2)}) collective-permute-start(bf16[2,72,512]{2,1,0:T(8,128)(2,1)S(1)} %pad_maximum_fusion.1), channel_id=1, source_target_pairs={{1,0},{2,1},{3,2},{4,3},{5,4},{6,5},{7,6},{8,7},{9,8},{10,9},{11,1... | collective-permute-start | bytes 442376 | tf_op jit(solution)/shard_map/ppermute | solution.py:23
  23.5 0.1 reshape.23.west_ref.own_w_ref
  23.6 6.9 %collective-permute-start.3 = (bf16[288,512]{1,0:T(8,128)(2,1)S(1)}, bf16[288,512]{1,0:T(8,128)(2,1)S(1)}, u32[]{:S(2)}, u32[]{:S(2)}) collective-permute-start(bf16[288,512]{1,0:T(8,128)(2,1)S(1)} %reshape.23.west_ref.own_w_ref), channel_id=1, source_target_pairs={{0,496},{16,0},{32,16},{48,32},{64,48},{80,64},{96,80},{112,96},{1... | collective-permute-start | bytes 884744 | tf_op jit(solution)/shard_map/ppermute | solution.py:23
  30.5 0.1 add_select_fusion.closed_ref
  30.6 0.0 collective-permute-done.2.west_ref
  30.6 44.1 %collective-permute-done.3.east_ref = bf16[288,512]{1,0:T(8,128)(2,1)S(1)} collective-permute-done((bf16[288,512]{1,0:T(8,128)(2,1)S(1)}, bf16[288,512]{1,0:T(8,128)(2,1)S(1)}, u32[]{:S(2)}, u32[]{:S(2)}) %collective-permute-start.3) | collective-permute-done | bytes 294944 | tf_op jit(solution)/shard_map/ppermute | solution.py:23
  74.7 1.9 %collective-permute-start.4 = (bf16[2,72,512]{2,1,0:T(8,128)(2,1)S(1)}, bf16[2,72,512]{2,1,0:T(8,128)(2,1)S(1)}, u32[]{:S(2)}, u32[]{:S(2)}) collective-permute-start(bf16[2,72,512]{2,1,0:T(8,128)(2,1)S(1)} %pad_maximum_fusion.2), channel_id=1, source_target_pairs={{0,1},{1,2},{2,3},{3,4},{4,5},{5,6},{6,7},{7,8},{8,9},{9,10},{10,1... | collective-permute-start | bytes 442376 | tf_op jit(solution)/shard_map/ppermute | solution.py:23
  76.7 2.4 %collective-permute-start.5 = (bf16[2,72,512]{2,1,0:T(8,128)(2,1)S(1)}, bf16[2,72,512]{2,1,0:T(8,128)(2,1)S(1)}, u32[]{:S(2)}, u32[]{:S(2)}) collective-permute-start(bf16[2,72,512]{2,1,0:T(8,128)(2,1)S(1)} %pad_maximum_fusion.3), channel_id=1, source_target_pairs={{1,0},{2,1},{3,2},{4,3},{5,4},{6,5},{7,6},{8,7},{9,8},{10,9},{11,1... | collective-permute-start | bytes 442376 | tf_op jit(solution)/shard_map/ppermute | solution.py:23
  79.1 0.0 collective-permute-done.north_ref
  79.1 0.0 collective-permute-done.1.south_ref
  79.1 0.0 copy-done
  79.1 0.0 copy-done.2
  79.1 0.0 copy-start.1
  79.2 4.1 %shard_map.46 = (f32[576,512]{1,0:T(8,128)S(1)}, f32[3,576,512]{2,1,0:T(8,128)S(1)}) custom-call(f32[2]{0:T(128)S(1)} %add_select_fusion.closed_ref, bf16[288,512]{1,0:T(8,128)(2,1)S(1)} %reshape.23.west_ref.own_w_ref, bf16[288,512]{1,0:T(8,128)(2,1)S(1)} %reshape.24.east_ref.own_e_ref, bf16[2,72,512]{2,1,0:T(8,128)(2,1)S(1)} %collective-permute-done.north_ref, ...), custom_call_target="tpu_custom_call" | custom-call | flops 2400000000 | bytes 7178248 | tf_op jit(solution)/shard_map/pallas_call | solution.py:209
  83.2 0.0 copy-done.1
  83.3 3.8 %shard_map.47 = (bf16[288,512]{1,0:T(8,128)(2,1)S(1)}, f32[3,288,512]{2,1,0:T(8,128)S(1)}) custom-call(f32[576,512]{1,0:T(8,128)S(1)} %get-tuple-element.9.query_ref, f32[3,576,512]{2,1,0:T(8,128)S(1)} %get-tuple-element.10.state_ref, bf16[288,512]{1,0:T(8,128)(2,1)S(1)} %reshape.23.west_ref.own_w_ref, bf16[288,512]{1,0:T(8,128)(2,1)S(1)} %reshape.24.east_ref.own_e_ref, ...), custom_call_target="tpu_custom_call" | custom-call | flops 1500000000 | bytes 10061824 | tf_op jit(solution)/shard_map/pallas_call | solution.py:209
  87.1 0.0 collective-permute-done.4.north_ref
  87.1 0.0 collective-permute-done.5.south_ref
  87.1 2.5 %shard_map.48 = bf16[2,288,512]{2,1,0:T(8,128)(2,1)S(1)} custom-call(f32[2]{0:T(128)S(1)} %add_select_fusion.closed_ref, f32[576,512]{1,0:T(8,128)S(1)} %get-tuple-element.9.query_ref, f32[3,288,512]{2,1,0:T(8,128)S(1)} %get-tuple-element.11.rim_ref, bf16[288,512]{1,0:T(8,128)(2,1)S(1)} %reshape.23.west_ref.own_w_ref, ...), custom_call_target="tpu_custom_call" | custom-call | flops 1000000000 | bytes 6817800 | tf_op jit(solution)/shard_map/pallas_call | solution.py:209
  89.6 0.1 reshape.26
  89.8 1.1 %copy.5 = bf16[12,2,6,4,512]{4,3,2,1,0:T(4,128)(2,1)} copy(bf16[12,2,6,4,512]{4,3,2,0,1:T(4,128)(2,1)S(1)} %bitcast.19) | data formatting | bytes 1179648 | tf_op jit(solution)/shard_map/transpose | solution.py:287
  (10 shorter events, 0.2 us)
Async XLA Ops:
  0.0 17.8 %copy-start.3 = (bf16[4,12,12,512]{3,0,2,1:T(4,128)(2,1)S(1)}, bf16[4,12,12,512]{3,0,2,1:T(4,128)(2,1)}, u32[]{:S(2)}) copy-start(bf16[4,12,12,512]{3,0,2,1:T(4,128)(2,1)} %param.4) | copy-start | bytes 1769476
  1.4 77.7 %copy-start = (bf16[512,1536]{1,0:T(8,128)(2,1)S(1)}, bf16[512,1536]{1,0:T(8,128)(2,1)}, u32[]{:S(2)}) copy-start(bf16[512,1536]{1,0:T(8,128)(2,1)} %qkv_ref.5) | copy-start | bytes 4718596
  1.4 77.7 %copy-start.2 = (f32[512]{0:T(512)S(1)}, f32[512]{0:T(512)}, u32[]{:S(2)}) copy-start(f32[512]{0:T(512)} %param.5) | copy-start | bytes 6148
  1.4 29.2 %collective-permute-start.2 = (bf16[288,512]{1,0:T(8,128)(2,1)S(1)}, bf16[288,512]{1,0:T(8,128)(2,1)S(1)}, u32[]{:S(2)}, u32[]{:S(2)}) collective-permute-start(bf16[288,512]{1,0:T(8,128)(2,1)S(1)} %reshape.24.east_ref.own_e_ref), channel_id=1, source_target_pairs={{0,16},{16,32},{32,48},{48,64},{64,80},{80,96},{96,112},{112,128},... | collective-permute-start | bytes 884744 | tf_op jit(solution)/shard_map/ppermute | solution.py:23
  18.0 61.1 %collective-permute-start = (bf16[2,72,512]{2,1,0:T(8,128)(2,1)S(1)}, bf16[2,72,512]{2,1,0:T(8,128)(2,1)S(1)}, u32[]{:S(2)}, u32[]{:S(2)}) collective-permute-start(bf16[2,72,512]{2,1,0:T(8,128)(2,1)S(1)} %pad_maximum_fusion), channel_id=1, source_target_pairs={{0,1},{1,2},{2,3},{3,4},{4,5},{5,6},{6,7},{7,8},{8,9},{9,10},{10,1... | collective-permute-start | bytes 442376 | tf_op jit(solution)/shard_map/ppermute | solution.py:23
  21.6 57.5 %collective-permute-start.1 = (bf16[2,72,512]{2,1,0:T(8,128)(2,1)S(1)}, bf16[2,72,512]{2,1,0:T(8,128)(2,1)S(1)}, u32[]{:S(2)}, u32[]{:S(2)}) collective-permute-start(bf16[2,72,512]{2,1,0:T(8,128)(2,1)S(1)} %pad_maximum_fusion.1), channel_id=1, source_target_pairs={{1,0},{2,1},{3,2},{4,3},{5,4},{6,5},{7,6},{8,7},{9,8},{10,9},{11,1... | collective-permute-start | bytes 442376 | tf_op jit(solution)/shard_map/ppermute | solution.py:23
  23.6 51.1 %collective-permute-start.3 = (bf16[288,512]{1,0:T(8,128)(2,1)S(1)}, bf16[288,512]{1,0:T(8,128)(2,1)S(1)}, u32[]{:S(2)}, u32[]{:S(2)}) collective-permute-start(bf16[288,512]{1,0:T(8,128)(2,1)S(1)} %reshape.23.west_ref.own_w_ref), channel_id=1, source_target_pairs={{0,496},{16,0},{32,16},{48,32},{64,48},{80,64},{96,80},{112,96},{1... | collective-permute-start | bytes 884744 | tf_op jit(solution)/shard_map/ppermute | solution.py:23
  74.7 12.4 %collective-permute-start.4 = (bf16[2,72,512]{2,1,0:T(8,128)(2,1)S(1)}, bf16[2,72,512]{2,1,0:T(8,128)(2,1)S(1)}, u32[]{:S(2)}, u32[]{:S(2)}) collective-permute-start(bf16[2,72,512]{2,1,0:T(8,128)(2,1)S(1)} %pad_maximum_fusion.2), channel_id=1, source_target_pairs={{0,1},{1,2},{2,3},{3,4},{4,5},{5,6},{6,7},{7,8},{8,9},{9,10},{10,1... | collective-permute-start | bytes 442376 | tf_op jit(solution)/shard_map/ppermute | solution.py:23
  76.7 10.4 %collective-permute-start.5 = (bf16[2,72,512]{2,1,0:T(8,128)(2,1)S(1)}, bf16[2,72,512]{2,1,0:T(8,128)(2,1)S(1)}, u32[]{:S(2)}, u32[]{:S(2)}) collective-permute-start(bf16[2,72,512]{2,1,0:T(8,128)(2,1)S(1)} %pad_maximum_fusion.3), channel_id=1, source_target_pairs={{1,0},{2,1},{3,2},{4,3},{5,4},{6,5},{7,6},{8,7},{9,8},{10,9},{11,1... | collective-permute-start | bytes 442376 | tf_op jit(solution)/shard_map/ppermute | solution.py:23
  79.1 4.1 %copy-start.1 = (bf16[512,512]{1,0:T(8,128)(2,1)S(1)}, bf16[512,512]{1,0:T(8,128)(2,1)}, u32[]{:S(2)}) copy-start(bf16[512,512]{1,0:T(8,128)(2,1)} %out_w_ref.3) | copy-start | bytes 1572868

commit v3 on v2

--- a/solution.py
+++ b/solution.py
@@ -100,95 +100,100 @@
     return (tokens + rounded(branch)).astype(jnp.bfloat16)
 
 
-def own_kernel(closed_ref, west_ref, east_ref, north_ref, south_ref, gain_ref, qkv_ref, query_ref, state_ref):
+def own_kernel(west_ref, east_ref, gain_ref, qkv_ref, query_ref, inner_ref, rim_ref):
     width = west_ref.shape[-1]
     rows = west_ref.shape[0]
-    gain = gain_ref[...]
     mine = jnp.concatenate([r[...].astype(jnp.float32) for r in (west_ref, east_ref)], axis=0)
-    theirs = jnp.concatenate([r[s].astype(jnp.float32) for r in (north_ref, south_ref) for s in range(2)], axis=0)
-    mine = layer_norm(mine, gain)
-    theirs = layer_norm(theirs, gain)
+    mine = layer_norm(mine, gain_ref[...])
     query = rounded(matmul(mine, qkv_ref[:, :width])) * HEAD_SIZE**-0.5
     query_ref[...] = query
     mine = matmul(mine, qkv_ref[:, width:])
-    theirs = matmul(theirs, qkv_ref[:, width:])
-    inner = level_bias(rows - 2 * RIM, rows - 2 * RIM)
-    rim = level_bias(RIM, 2 * RIM)
-    distant = lax.broadcasted_iota(jnp.int32, (RIM, 2 * RIM), 1) >= RIM
+    add_halves(query, mine, inner_ref, rim_ref)
+
+
+def add_halves(query, kv_all, inner_ref, rim_ref, inner_before=None, rim_before=None):
+    rows = kv_all.shape[0] // 2
+    width = query.shape[-1]
+    count = rows - 2 * RIM
+    inner = level_bias(count, count)
+    rim = level_bias(RIM, RIM)
+    done = []
     for side in range(2):
         base = side * rows
-        at = slice(base + RIM, base + rows - RIM)
-        kv = mine[at].astype(jnp.bfloat16)
-        store(state_ref, at, attend(query[at], kv[:, :width], kv[:, width:], inner))
         for edge in range(2):
             begin = base + edge * (rows - RIM)
             at = slice(begin, begin + RIM)
-            beyond = (edge * 2 + side) * RIM
-            kv = jnp.concatenate([mine[at], theirs[beyond : beyond + RIM]], axis=0).astype(jnp.bfloat16)
-            bias = rim + jnp.where(distant, closed_ref[edge], 0.0)
-            store(state_ref, at, attend(query[at], kv[:, :width], kv[:, width:], bias))
+            kv = kv_all[at].astype(jnp.bfloat16)
+            more = attend(query[at], kv[:, :width], kv[:, width:], rim)
+            place = slice((edge * 2 + side) * RIM, (edge * 2 + side + 1) * RIM)
+            store(rim_ref, place, more if rim_before is None else add_keys(load(rim_before, place), more))
+        at = slice(base + RIM, base + rows - RIM)
+        kv = kv_all[at].astype(jnp.bfloat16)
+        more = attend(query[at], kv[:, :width], kv[:, width:], inner)
+        place = slice(side * count, (side + 1) * count)
+        if inner_before is None:
+            store(inner_ref, place, more)
+        else:
+            done.append(add_keys(load(inner_before, place), more))
+    return done
 
 
 def halo_kernel(
-    query_ref, state_ref, own_w_ref, own_e_ref, west_ref, east_ref, gain_ref, qkv_ref, out_w_ref, out_ref, rim_ref
+    query_ref, inner_ref, rim_ref, own_w_ref, own_e_ref, west_ref, east_ref, gain_ref, qkv_ref, out_w_ref, out_ref, rim_out_ref
 ):
     width = west_ref.shape[-1]
     rows = west_ref.shape[0]
     halos = jnp.concatenate([r[...].astype(jnp.float32) for r in (west_ref, east_ref)], axis=0)
     halos = matmul(layer_norm(halos, gain_ref[...]), qkv_ref[:, width:])
-    inner = level_bias(rows - 2 * RIM, rows - 2 * RIM)
+    done = add_halves(query_ref[...], halos, None, rim_out_ref, inner_ref, rim_ref)
+    done = tuple(jnp.concatenate(p, axis=0) for p in zip(*done))
+    tokens = [r[...].astype(jnp.float32)[RIM : rows - RIM] for r in (own_w_ref, own_e_ref)]
+    out_ref[...] = project(jnp.concatenate(tokens, axis=0), done, out_w_ref)
+
+
+def add_rims(closed_ref, query_ref, rim_ref, north_ref, south_ref, gain_ref, qkv_ref):
+    width = query_ref.shape[-1]
+    rows = query_ref.shape[0] // 2
+    beyond = jnp.concatenate([r[s].astype(jnp.float32) for r in (north_ref, south_ref) for s in range(2)], axis=0)
+    beyond = matmul(layer_norm(beyond, gain_ref[...]), qkv_ref[:, width:])
     rim = level_bias(RIM, RIM)
-    done, tokens = [], []
-    for side in range(2):
-        base = side * rows
-        for edge in range(2):
-            begin = base + edge * (rows - RIM)
-            at = slice(begin, begin + RIM)
-            kv = halos[at].astype(jnp.bfloat16)
-            more = attend(query_ref[at], kv[:, :width], kv[:, width:], rim)
-            place = (edge * 2 + side) * RIM
-            store(rim_ref, slice(place, place + RIM), add_keys(load(state_ref, at), more))
-        at = slice(base + RIM, base + rows - RIM)
-        kv = halos[at].astype(jnp.bfloat16)
-        more = attend(query_ref[at], kv[:, :width], kv[:, width:], inner)
-        done.append(add_keys(load(state_ref, at), more))
-        tokens.append((own_w_ref, own_e_ref)[side][...].astype(jnp.float32)[RIM : rows - RIM])
-    done = tuple(jnp.concatenate(p, axis=0) for p in zip(*done))
-    out_ref[...] = project(jnp.concatenate(tokens, axis=0), done, out_w_ref)
+    done = []
+    for edge in range(2):
+        for side in range(2):
+            begin = side * rows + edge * (rows - RIM)
+            place = slice((edge * 2 + side) * RIM, (edge * 2 + side + 1) * RIM)
+            kv = beyond[place].astype(jnp.bfloat16)
+            query = query_ref[begin : begin + RIM]
+            more = attend(query, kv[:, :width], kv[:, width:], rim + closed_ref[edge])
+            done.append(add_keys(load(rim_ref, place), more))
+    return done
+
+
+def latitude_kernel(closed_ref, query_ref, rim_ref, north_ref, south_ref, gain_ref, qkv_ref, rim_out_ref):
+    done = add_rims(closed_ref, query_ref, rim_ref, north_ref, south_ref, gain_ref, qkv_ref)
+    for place, state in enumerate(done):
+        store(rim_out_ref, slice(place * RIM, (place + 1) * RIM), state)
 
 
 def corner_kernel(
     closed_ref,
     query_ref,
     rim_ref,
+    north_ref,
+    south_ref,
+    gain_ref,
+    qkv_ref,
     own_w_ref,
     own_e_ref,
-    north_ref,
-    south_ref,
     middle_ref,
-    gain_ref,
-    qkv_ref,
     out_w_ref,
     out_ref,
 ):
-    width = own_w_ref.shape[-1]
     rows = own_w_ref.shape[0]
-    corners = jnp.concatenate([r[s].astype(jnp.float32) for r in (north_ref, south_ref) for s in range(2)], axis=0)
-    corners = matmul(layer_norm(corners, gain_ref[...]), qkv_ref[:, width:])
-    rim = level_bias(RIM, RIM)
+    done = add_rims(closed_ref, query_ref, rim_ref, north_ref, south_ref, gain_ref, qkv_ref)
+    done = tuple(jnp.concatenate(p, axis=0) for p in zip(*done))
     own = [r[...].astype(jnp.float32) for r in (own_w_ref, own_e_ref)]
-    done, tokens = [], []
-    for edge in range(2):
-        for side in range(2):
-            begin = edge * (rows - RIM)
-            at = slice(begin, begin + RIM)
-            place = (edge * 2 + side) * RIM
-            kv = corners[place : place + RIM].astype(jnp.bfloat16)
-            query = query_ref[slice(side * rows + begin, side * rows + begin + RIM)]
-            more = attend(query, kv[:, :width], kv[:, width:], rim + closed_ref[edge])
-            done.append(add_keys(load(rim_ref, slice(place, place + RIM)), more))
-            tokens.append(own[side][at])
-    done = tuple(jnp.concatenate(p, axis=0) for p in zip(*done))
+    tokens = [half[at] for at in (slice(0, RIM), slice(rows - RIM, rows)) for half in own]
     mixed = project(jnp.concatenate(tokens, axis=0), done, out_w_ref).astype(jnp.float32)
     middle = middle_ref[...].astype(jnp.float32)
     count = rows - 2 * RIM
@@ -229,11 +234,6 @@
         return jnp.stack([a[at], b[at]])
 
     top, bottom = slice(0, RIM), slice(rows - RIM, rows)
-    south = shift(both(own_w, own_e, top), "lat", -1, False)
-    north = shift(both(own_w, own_e, bottom), "lat", 1, False)
-    far_south = shift(both(west, east, top), "lat", -1, False)
-    far_north = shift(both(west, east, bottom), "lat", 1, False)
-
     gain = gain_attn.reshape(1, width)
     place = lax.axis_index("lat")
     closed = jnp.stack([place == 0, place == lax.axis_size("lat") - 1])
@@ -242,24 +242,31 @@
     def shape(*dims, dtype=jnp.float32):
         return jax.ShapeDtypeStruct(dims, dtype)
 
-    query, state = call(
+    inner_shape = shape(3, 2 * (rows - 2 * RIM), width)
+    rim_shape = shape(3, 4 * RIM, width)
+    query, inner, rim = call(
         own_kernel,
-        [shape(2 * rows, width), shape(3, 2 * rows, width)],
-        2_400_000_000,
-        closed,
+        [shape(2 * rows, width), inner_shape, rim_shape],
+        2_000_000_000,
         own_w,
         own_e,
-        north,
-        south,
         gain,
         weight_qkv,
     )
+    lat_w, lat_e, query, rim = lax.optimization_barrier((own_w, own_e, query, rim))
+    south = shift(both(lat_w, lat_e, top), "lat", -1, False)
+    north = shift(both(lat_w, lat_e, bottom), "lat", 1, False)
+    (rim,) = call(latitude_kernel, [rim_shape], 800_000_000, closed, query, rim, north, south, gain, weight_qkv)
+    west, east, query, rim = lax.optimization_barrier((west, east, query, rim))
+    far_south = shift(both(west, east, top), "lat", -1, False)
+    far_north = shift(both(west, east, bottom), "lat", 1, False)
     middle, rim = call(
         halo_kernel,
-        [shape(2 * (rows - 2 * RIM), width, dtype=jnp.bfloat16), shape(3, 4 * RIM, width)],
+        [shape(2 * (rows - 2 * RIM), width, dtype=jnp.bfloat16), rim_shape],
         1_500_000_000,
         query,
-        state,
+        inner,
+        rim,
         own_w,
         own_e,
         west,
@@ -275,13 +282,13 @@
         closed,
         query,
         rim,
+        far_north,
+        far_south,
+        gain,
+        weight_qkv,
         own_w,
         own_e,
-        far_north,
-        far_south,
         middle,
-        gain,
-        weight_qkv,
         weight_out,
     )
     mixed = mixed.reshape(2, row_count, HALF, lev_count, width).transpose(1, 0, 2, 3, 4)

time: 91.2 us -> 93.8 us (1.029)
  waiting for transfers between devices: 44.1 us -> 34 us
  local copies, waits for them, and re-layouts: 2.93 us -> 10.8 us
  Pallas kernels: 10.4 us -> 13.5 us
  other arithmetic: 0.15 us -> 1.46 us
    ppermute x6, waiting for transfers between devices: 44.1 us -> 34 us  [shift(): return lax.ppermute(value, axis, pairs)]
    unnamed x8 -> x16, local copies, waits for them, and re-layouts: 0.02 us -> 4.77 us
    pallas_call x3 -> x4, Pallas kernels: 10.4 us -> 13.5 us  [call(): pl.pallas_call(kernel, out_shape=results, in_specs=specs, out_specs=[pl.B...]
    another operation x6 -> x3, local copies, waits for them, and re-layouts: 0.11 us -> 1.88 us  [both(): return jnp.stack([a[at], b[at]])]
    reshape x1, local copies, waits for them, and re-layouts: 0.14 us -> 1.53 us  [shards(): mixed.reshape(2, row_count, HALF, lev_count, width).transpose(1, 0, 2, 3, 4)]
    another operation x4, other arithmetic: 0.07 us -> 1.39 us  [both(): return jnp.stack([a[at], b[at]])]
  transfers between devices with their start and end apart: 6 -> 6, of which waited for: 1 -> 2; matrix products, arithmetic and copies ran while one was open for 0% -> 2% of each run, Pallas kernels for 9% -> 12%
where the time goes in v3:
time: 93.8 us; the launch traced here: 93.3 us
  waiting for transfers between devices  34 us (36%)
  starting transfers between devices  33.4 us (36%)
  Pallas kernels  13.5 us (14%)
  local copies, waits for them, and re-layouts  10.8 us (12%)
  other arithmetic  1.46 us (2%)
    ppermute x6, waiting for transfers between devices, shift(): return lax.ppermute(value, axis, pairs)  34 us
    ppermute x6, starting transfers between devices, shift(): return lax.ppermute(value, axis, pairs)  33.4 us
    pallas_call x4, Pallas kernels, call(): pl.pallas_call(kernel, out_shape=results, in_specs=specs, out_specs=[pl.B...  13.5 us
    unnamed x16, local copies, waits for them, and re-layouts  4.77 us
    another operation x3, local copies, waits for them, and re-layouts, both(): return jnp.stack([a[at], b[at]])  1.88 us
  transfers between devices with their start and end apart: 6, of which 2 were waited for; matrix products, arithmetic and copies ran while one was open for 2% of the time, Pallas kernels for 12%

profile of v3, /device:TPU:1, one launch (start us, length us, event | category | flops | bytes accessed | tf_op | source)
XLA Modules:
  0.0 93.3 jit_solution(18127753436947951396)
XLA Ops:
  0.0 1.4 %fusion = (bf16[12,6,4,512]{3,2,1,0:T(4,128)(2,1)S(1)}, bf16[12,6,4,512]{3,2,1,0:T(4,128)(2,1)S(1)}) fusion(bf16[12,12,4,512]{3,2,1,0:T(4,128)(2,1)} %bitcast.29), kind=kLoop, calls=%fused_computation.13 | loop fusion | bytes 1179648 | tf_op jit(solution)/shard_map/slice | solution.py:228
  1.4 0.1 reshape.15.east_ref.own_e_ref
  1.5 16.3 %collective-permute-start = (bf16[288,512]{1,0:T(8,128)(2,1)S(1)}, bf16[288,512]{1,0:T(8,128)(2,1)}, u32[]{:S(2)}, u32[]{:S(2)}) collective-permute-start(bf16[288,512]{1,0:T(8,128)(2,1)S(1)} %reshape.15.east_ref.own_e_ref), channel_id=1, source_target_pairs={{0,16},{16,32},{32,48},{48,64},{64,80},{80,96},{96,112},{112,128},... | collective-permute-start | bytes 884744 | tf_op jit(solution)/shard_map/ppermute | solution.py:23
  17.7 0.1 reshape.16.west_ref.own_w_ref
  17.8 6.6 %collective-permute-start.1 = (bf16[288,512]{1,0:T(8,128)(2,1)S(1)}, bf16[288,512]{1,0:T(8,128)(2,1)}, u32[]{:S(2)}, u32[]{:S(2)}) collective-permute-start(bf16[288,512]{1,0:T(8,128)(2,1)S(1)} %reshape.16.west_ref.own_w_ref), channel_id=1, source_target_pairs={{0,496},{16,0},{32,16},{48,32},{64,48},{80,64},{96,80},{112,96},{1... | collective-permute-start | bytes 884744 | tf_op jit(solution)/shard_map/ppermute | solution.py:23
  24.4 0.0 copy-done
  24.4 3.4 %shard_map.46 = (f32[576,512]{1,0:T(8,128)S(1)}, f32[3,288,512]{2,1,0:T(8,128)S(1)}, f32[3,288,512]{2,1,0:T(8,128)S(1)}) custom-call(bf16[288,512]{1,0:T(8,128)(2,1)S(1)} %reshape.16.west_ref.own_w_ref, bf16[288,512]{1,0:T(8,128)(2,1)S(1)} %reshape.15.east_ref.own_e_ref, f32[1,512]{1,0:T(1,128)S(1)} %bitcast.24, bf16[512,1536]{1,0:T(8,128)(2,1)S(1)} %copy-done), custom_call_target="tpu_custom_call" | custom-call | flops 2000000000 | bytes 6883328 | tf_op jit(solution)/shard_map/pallas_call | solution.py:214
  27.8 1.2 %copy-done.3 = f32[3,288,512]{2,1,0:T(8,128)} copy-done((f32[3,288,512]{2,1,0:T(8,128)}, f32[3,288,512]{2,1,0:T(8,128)S(1)}, u32[]{:S(2)}) %copy-start.3) | copy-done | bytes 1769496
  29.1 1.2 %copy-done.5 = f32[3,288,512]{2,1,0:T(8,128)} copy-done((f32[3,288,512]{2,1,0:T(8,128)}, f32[3,288,512]{2,1,0:T(8,128)S(1)}, u32[]{:S(2)}) %copy-start.5) | copy-done | bytes 1769496
  30.3 0.7 pad_maximum_fusion
  31.0 3.5 %collective-permute-start.2 = (bf16[2,72,512]{2,1,0:T(8,128)(2,1)}, bf16[2,72,512]{2,1,0:T(8,128)(2,1)S(1)}, u32[]{:S(2)}, u32[]{:S(2)}) collective-permute-start(bf16[2,72,512]{2,1,0:T(8,128)(2,1)} %pad_maximum_fusion), channel_id=1, source_target_pairs={{0,1},{1,2},{2,3},{3,4},{4,5},{5,6},{6,7},{7,8},{8,9},{9,10},{10,1... | collective-permute-start | bytes 442376 | tf_op jit(solution)/shard_map/ppermute | solution.py:23
  34.5 0.7 pad_maximum_fusion.1
  35.1 2.5 %collective-permute-start.3 = (bf16[2,72,512]{2,1,0:T(8,128)(2,1)}, bf16[2,72,512]{2,1,0:T(8,128)(2,1)}, u32[]{:S(2)}, u32[]{:S(2)}) collective-permute-start(bf16[2,72,512]{2,1,0:T(8,128)(2,1)} %pad_maximum_fusion.1), channel_id=1, source_target_pairs={{1,0},{2,1},{3,2},{4,3},{5,4},{6,5},{7,6},{8,7},{9,8},{10,9},{11,1... | collective-permute-start | bytes 442376 | tf_op jit(solution)/shard_map/ppermute | solution.py:23
  37.7 0.1 add_select_fusion.closed_ref
  37.8 31.8 %collective-permute-done.2.north_ref = bf16[2,72,512]{2,1,0:T(8,128)(2,1)S(1)} collective-permute-done((bf16[2,72,512]{2,1,0:T(8,128)(2,1)}, bf16[2,72,512]{2,1,0:T(8,128)(2,1)S(1)}, u32[]{:S(2)}, u32[]{:S(2)}) %collective-permute-start.2) | collective-permute-done | bytes 147488 | tf_op jit(solution)/shard_map/ppermute | solution.py:23
  69.6 2.2 %collective-permute-done.3.south_ref = bf16[2,72,512]{2,1,0:T(8,128)(2,1)} collective-permute-done((bf16[2,72,512]{2,1,0:T(8,128)(2,1)}, bf16[2,72,512]{2,1,0:T(8,128)(2,1)}, u32[]{:S(2)}, u32[]{:S(2)}) %collective-permute-start.3) | collective-permute-done | bytes 147488 | tf_op jit(solution)/shard_map/ppermute | solution.py:23
  71.8 1.5 %copy-done.6 = f32[3,288,512]{2,1,0:T(8,128)S(1)} copy-done((f32[3,288,512]{2,1,0:T(8,128)S(1)}, f32[3,288,512]{2,1,0:T(8,128)}, u32[]{:S(2)}) %copy-start.6) | copy-done | bytes 1769496
  73.3 2.9 %shard_map.47.rim_ref = f32[3,288,512]{2,1,0:T(8,128)S(1)} custom-call(f32[2]{0:T(128)S(1)} %add_select_fusion.closed_ref, f32[576,512]{1,0:T(8,128)S(1)} %get-tuple-element.24.query_ref, f32[3,288,512]{2,1,0:T(8,128)S(1)} %copy-done.6, bf16[2,72,512]{2,1,0:T(8,128)(2,1)S(1)} %collective-permute-done.2.north_ref, ...), custom_call_target="tpu_custom_call" | custom-call | flops 800000000 | bytes 6588424 | tf_op jit(solution)/shard_map/pallas_call | solution.py:214
  76.1 0.0 collective-permute-done.west_ref
  76.1 0.0 collective-permute-done.1.east_ref
  76.1 0.9 slice_bitcast_fusion
  77.1 0.9 slice_bitcast_fusion.1
  78.0 2.1 %collective-permute-start.4 = (bf16[2,72,512]{2,1,0:T(8,128)(2,1)S(1)}, bf16[2,72,512]{2,1,0:T(8,128)(2,1)S(1)}, u32[]{:S(2)}, u32[]{:S(2)}) collective-permute-start(bf16[2,72,512]{2,1,0:T(8,128)(2,1)S(1)} %pad_maximum_fusion.2), channel_id=1, source_target_pairs={{0,1},{1,2},{2,3},{3,4},{4,5},{5,6},{6,7},{7,8},{8,9},{9,10},{10,1... | collective-permute-start | bytes 442376 | tf_op jit(solution)/shard_map/ppermute | solution.py:23
  80.2 2.4 %collective-permute-start.5 = (bf16[2,72,512]{2,1,0:T(8,128)(2,1)S(1)}, bf16[2,72,512]{2,1,0:T(8,128)(2,1)S(1)}, u32[]{:S(2)}, u32[]{:S(2)}) collective-permute-start(bf16[2,72,512]{2,1,0:T(8,128)(2,1)S(1)} %pad_maximum_fusion.3), channel_id=1, source_target_pairs={{1,0},{2,1},{3,2},{4,3},{5,4},{6,5},{7,6},{8,7},{9,8},{10,9},{11,1... | collective-permute-start | bytes 442376 | tf_op jit(solution)/shard_map/ppermute | solution.py:23
  82.6 4.7 %shard_map.48 = (bf16[288,512]{1,0:T(8,128)(2,1)S(1)}, f32[3,288,512]{2,1,0:T(8,128)S(1)}) custom-call(f32[576,512]{1,0:T(8,128)S(1)} %get-tuple-element.24.query_ref, f32[3,288,512]{2,1,0:T(8,128)S(1)} %copy-done.4, f32[3,288,512]{2,1,0:T(8,128)S(1)} %shard_map.47.rim_ref, bf16[288,512]{1,0:T(8,128)(2,1)S(1)} %reshape.16.west_ref.own_w_ref, ...), custom_call_target="tpu_custom_call" | custom-call | flops 1500000000 | bytes 10061824 | tf_op jit(solution)/shard_map/pallas_call | solution.py:214
  87.4 0.0 collective-permute-done.4.north_ref
  87.4 0.0 collective-permute-done.5.south_ref
  87.4 2.5 %shard_map.49 = bf16[2,288,512]{2,1,0:T(8,128)(2,1)S(1)} custom-call(f32[2]{0:T(128)S(1)} %add_select_fusion.closed_ref, f32[576,512]{1,0:T(8,128)S(1)} %get-tuple-element.24.query_ref, f32[3,288,512]{2,1,0:T(8,128)S(1)} %get-tuple-element.29.rim_ref, bf16[2,72,512]{2,1,0:T(8,128)(2,1)S(1)} %collective-permute-done.4.north_ref, ...), custom_call_target="tpu_custom_call" | custom-call | flops 1000000000 | bytes 6817800 | tf_op jit(solution)/shard_map/pallas_call | solution.py:214
  89.9 0.0 copy-start.1
  89.9 0.8 copy-done.1
  90.7 1.5 %reshape.18 = bf16[2,12,6,4,512]{4,3,2,1,0:T(4,128)(2,1)S(1)} reshape(bf16[2,288,512]{2,1,0:T(8,128)(2,1)} %copy-done.1) | data formatting | bytes 1179648 | tf_op jit(solution)/shard_map/reshape | solution.py:294
  92.2 1.1 %copy.5 = bf16[12,2,6,4,512]{4,3,2,1,0:T(4,128)(2,1)} copy(bf16[12,2,6,4,512]{4,3,2,0,1:T(4,128)(2,1)S(1)} %bitcast.28) | data formatting | bytes 1179648 | tf_op jit(solution)/shard_map/transpose | solution.py:294
  (13 shorter events, 0.1 us)
Async XLA Ops:
  0.0 24.4 %copy-start = (bf16[512,1536]{1,0:T(8,128)(2,1)S(1)}, bf16[512,1536]{1,0:T(8,128)(2,1)}, u32[]{:S(2)}) copy-start(bf16[512,1536]{1,0:T(8,128)(2,1)} %qkv_ref.7) | copy-start | bytes 4718596
  0.0 24.4 %copy-start.7 = (f32[512]{0:T(512)S(1)}, f32[512]{0:T(512)}, u32[]{:S(2)}) copy-start(f32[512]{0:T(512)} %param.5) | copy-start | bytes 6148
  1.5 74.7 %collective-permute-start = (bf16[288,512]{1,0:T(8,128)(2,1)S(1)}, bf16[288,512]{1,0:T(8,128)(2,1)}, u32[]{:S(2)}, u32[]{:S(2)}) collective-permute-start(bf16[288,512]{1,0:T(8,128)(2,1)S(1)} %reshape.15.east_ref.own_e_ref), channel_id=1, source_target_pairs={{0,16},{16,32},{32,48},{48,64},{64,80},{80,96},{96,112},{112,128},... | collective-permute-start | bytes 884744 | tf_op jit(solution)/shard_map/ppermute | solution.py:23
  17.8 58.3 %collective-permute-start.1 = (bf16[288,512]{1,0:T(8,128)(2,1)S(1)}, bf16[288,512]{1,0:T(8,128)(2,1)}, u32[]{:S(2)}, u32[]{:S(2)}) collective-permute-start(bf16[288,512]{1,0:T(8,128)(2,1)S(1)} %reshape.16.west_ref.own_w_ref), channel_id=1, source_target_pairs={{0,496},{16,0},{32,16},{48,32},{64,48},{80,64},{96,80},{112,96},{1... | collective-permute-start | bytes 884744 | tf_op jit(solution)/shard_map/ppermute | solution.py:23
  27.8 1.3 %copy-start.3 = (f32[3,288,512]{2,1,0:T(8,128)}, f32[3,288,512]{2,1,0:T(8,128)S(1)}, u32[]{:S(2)}) copy-start(f32[3,288,512]{2,1,0:T(8,128)S(1)} %get-tuple-element.25.inner_ref) | copy-start | bytes 5308420
  29.1 1.2 %copy-start.5 = (f32[3,288,512]{2,1,0:T(8,128)}, f32[3,288,512]{2,1,0:T(8,128)S(1)}, u32[]{:S(2)}) copy-start(f32[3,288,512]{2,1,0:T(8,128)S(1)} %get-tuple-element.21.rim_ref) | copy-start | bytes 5308420
  31.0 38.6 %collective-permute-start.2 = (bf16[2,72,512]{2,1,0:T(8,128)(2,1)}, bf16[2,72,512]{2,1,0:T(8,128)(2,1)S(1)}, u32[]{:S(2)}, u32[]{:S(2)}) collective-permute-start(bf16[2,72,512]{2,1,0:T(8,128)(2,1)} %pad_maximum_fusion), channel_id=1, source_target_pairs={{0,1},{1,2},{2,3},{3,4},{4,5},{5,6},{6,7},{7,8},{8,9},{9,10},{10,1... | collective-permute-start | bytes 442376 | tf_op jit(solution)/shard_map/ppermute | solution.py:23
  35.1 36.6 %collective-permute-start.3 = (bf16[2,72,512]{2,1,0:T(8,128)(2,1)}, bf16[2,72,512]{2,1,0:T(8,128)(2,1)}, u32[]{:S(2)}, u32[]{:S(2)}) collective-permute-start(bf16[2,72,512]{2,1,0:T(8,128)(2,1)} %pad_maximum_fusion.1), channel_id=1, source_target_pairs={{1,0},{2,1},{3,2},{4,3},{5,4},{6,5},{7,6},{8,7},{9,8},{10,9},{11,1... | collective-permute-start | bytes 442376 | tf_op jit(solution)/shard_map/ppermute | solution.py:23
  37.8 44.8 %copy-start.2 = (bf16[512,512]{1,0:T(8,128)(2,1)S(1)}, bf16[512,512]{1,0:T(8,128)(2,1)}, u32[]{:S(2)}) copy-start(bf16[512,512]{1,0:T(8,128)(2,1)} %out_w_ref.3) | copy-start | bytes 1572868
  71.8 1.5 %copy-start.6 = (f32[3,288,512]{2,1,0:T(8,128)S(1)}, f32[3,288,512]{2,1,0:T(8,128)}, u32[]{:S(2)}) copy-start(f32[3,288,512]{2,1,0:T(8,128)} %copy-done.5) | copy-start | bytes 5308420
  73.3 9.3 %copy-start.4 = (f32[3,288,512]{2,1,0:T(8,128)S(1)}, f32[3,288,512]{2,1,0:T(8,128)}, u32[]{:S(2)}) copy-start(f32[3,288,512]{2,1,0:T(8,128)} %copy-done.3) | copy-start | bytes 5308420
  78.0 9.3 %collective-permute-start.4 = (bf16[2,72,512]{2,1,0:T(8,128)(2,1)S(1)}, bf16[2,72,512]{2,1,0:T(8,128)(2,1)S(1)}, u32[]{:S(2)}, u32[]{:S(2)}) collective-permute-start(bf16[2,72,512]{2,1,0:T(8,128)(2,1)S(1)} %pad_maximum_fusion.2), channel_id=1, source_target_pairs={{0,1},{1,2},{2,3},{3,4},{4,5},{5,6},{6,7},{7,8},{8,9},{9,10},{10,1... | collective-permute-start | bytes 442376 | tf_op jit(solution)/shard_map/ppermute | solution.py:23
  80.2 7.2 %collective-permute-start.5 = (bf16[2,72,512]{2,1,0:T(8,128)(2,1)S(1)}, bf16[2,72,512]{2,1,0:T(8,128)(2,1)S(1)}, u32[]{:S(2)}, u32[]{:S(2)}) collective-permute-start(bf16[2,72,512]{2,1,0:T(8,128)(2,1)S(1)} %pad_maximum_fusion.3), channel_id=1, source_target_pairs={{1,0},{2,1},{3,2},{4,3},{5,4},{6,5},{7,6},{8,7},{9,8},{10,9},{11,1... | collective-permute-start | bytes 442376 | tf_op jit(solution)/shard_map/ppermute | solution.py:23
  89.9 0.8 copy-start.1

commit v4 on v3

--- a/solution.py
+++ b/solution.py
@@ -100,7 +100,8 @@
     return (tokens + rounded(branch)).astype(jnp.bfloat16)
 
 
-def own_kernel(west_ref, east_ref, gain_ref, qkv_ref, query_ref, inner_ref, rim_ref):
+def own_kernel(west_ref, east_ref, gain_ref, qkv_ref, query_ref, inner_ref, rim_ref, ready_ref):
+    ready_ref[...] = jnp.zeros_like(ready_ref)
     width = west_ref.shape[-1]
     rows = west_ref.shape[0]
     mine = jnp.concatenate([r[...].astype(jnp.float32) for r in (west_ref, east_ref)], axis=0)
@@ -138,6 +139,15 @@
     return done
 
 
+def pack_kernel(ready_ref, *refs):
+    *parts, south_ref, north_ref = refs
+    rows = parts[0].shape[0]
+    for i, part in enumerate(parts):
+        values = part[...].astype(jnp.float32)
+        south_ref[i] = values[:RIM].astype(jnp.bfloat16)
+        north_ref[i] = values[rows - RIM :].astype(jnp.bfloat16)
+
+
 def halo_kernel(
     query_ref, inner_ref, rim_ref, own_w_ref, own_e_ref, west_ref, east_ref, gain_ref, qkv_ref, out_w_ref, out_ref, rim_out_ref
 ):
@@ -154,25 +164,21 @@
 def add_rims(closed_ref, query_ref, rim_ref, north_ref, south_ref, gain_ref, qkv_ref):
     width = query_ref.shape[-1]
     rows = query_ref.shape[0] // 2
-    beyond = jnp.concatenate([r[s].astype(jnp.float32) for r in (north_ref, south_ref) for s in range(2)], axis=0)
+    beyond = jnp.concatenate([r[p].astype(jnp.float32) for r in (north_ref, south_ref) for p in range(4)], axis=0)
     beyond = matmul(layer_norm(beyond, gain_ref[...]), qkv_ref[:, width:])
-    rim = level_bias(RIM, RIM)
+    rim = level_bias(RIM, 2 * RIM)
     done = []
     for edge in range(2):
         for side in range(2):
             begin = side * rows + edge * (rows - RIM)
             place = slice((edge * 2 + side) * RIM, (edge * 2 + side + 1) * RIM)
-            kv = beyond[place].astype(jnp.bfloat16)
+            first, second = ((edge * 4 + part) * RIM for part in (side, side + 2))
+            kv = jnp.concatenate([beyond[first : first + RIM], beyond[second : second + RIM]], axis=0)
+            kv = kv.astype(jnp.bfloat16)
             query = query_ref[begin : begin + RIM]
             more = attend(query, kv[:, :width], kv[:, width:], rim + closed_ref[edge])
             done.append(add_keys(load(rim_ref, place), more))
     return done
-
-
-def latitude_kernel(closed_ref, query_ref, rim_ref, north_ref, south_ref, gain_ref, qkv_ref, rim_out_ref):
-    done = add_rims(closed_ref, query_ref, rim_ref, north_ref, south_ref, gain_ref, qkv_ref)
-    for place, state in enumerate(done):
-        store(rim_out_ref, slice(place * RIM, (place + 1) * RIM), state)
 
 
 def corner_kernel(
@@ -229,11 +235,6 @@
     own_e = by_place[:, HALF:].reshape(rows, width)
     east = shift(own_w, "lon", -1, True)
     west = shift(own_e, "lon", 1, True)
-
-    def both(a, b, at):
-        return jnp.stack([a[at], b[at]])
-
-    top, bottom = slice(0, RIM), slice(rows - RIM, rows)
     gain = gain_attn.reshape(1, width)
     place = lax.axis_index("lat")
     closed = jnp.stack([place == 0, place == lax.axis_size("lat") - 1])
@@ -244,22 +245,19 @@
 
     inner_shape = shape(3, 2 * (rows - 2 * RIM), width)
     rim_shape = shape(3, 4 * RIM, width)
-    query, inner, rim = call(
+    query, inner, rim, ready = call(
         own_kernel,
-        [shape(2 * rows, width), inner_shape, rim_shape],
+        [shape(2 * rows, width), inner_shape, rim_shape, shape(8, 128)],
         2_000_000_000,
         own_w,
         own_e,
         gain,
         weight_qkv,
     )
-    lat_w, lat_e, query, rim = lax.optimization_barrier((own_w, own_e, query, rim))
-    south = shift(both(lat_w, lat_e, top), "lat", -1, False)
-    north = shift(both(lat_w, lat_e, bottom), "lat", 1, False)
-    (rim,) = call(latitude_kernel, [rim_shape], 800_000_000, closed, query, rim, north, south, gain, weight_qkv)
-    west, east, query, rim = lax.optimization_barrier((west, east, query, rim))
-    far_south = shift(both(west, east, top), "lat", -1, False)
-    far_north = shift(both(west, east, bottom), "lat", 1, False)
+    packed = shape(4, RIM, width, dtype=jnp.bfloat16)
+    to_south, to_north = call(pack_kernel, [packed, packed], 1_000_000, ready, own_w, own_e, west, east)
+    far_south = shift(to_south, "lat", -1, False)
+    far_north = shift(to_north, "lat", 1, False)
     middle, rim = call(
         halo_kernel,
         [shape(2 * (rows - 2 * RIM), width, dtype=jnp.bfloat16), rim_shape],

time: 93.8 us -> 93.7 us (level)
  waiting for transfers between devices: 34 us -> 12.4 us
  starting transfers between devices: 33.4 us -> 54.1 us
  local copies, waits for them, and re-layouts: 10.8 us -> 13.1 us
  other arithmetic: 1.46 us -> 0.08 us
    ppermute x6 -> x4, waiting for transfers between devices: 34 us -> 12.4 us  [shift(): return lax.ppermute(value, axis, pairs)]
    ppermute x6 -> x4, starting transfers between devices: 33.4 us -> 54.1 us  [shift(): return lax.ppermute(value, axis, pairs)]
    unnamed x16 -> x20, local copies, waits for them, and re-layouts: 4.77 us -> 8.93 us
    another operation x3 -> x0, local copies, waits for them, and re-layouts: 1.88 us -> none  [both(): return jnp.stack([a[at], b[at]])]
    another operation x4 -> x0, other arithmetic: 1.39 us -> none  [both(): return jnp.stack([a[at], b[at]])]
  transfers between devices with their start and end apart: 6 -> 4, of which waited for: 2 -> 1; matrix products, arithmetic and copies ran while one was open for 2% -> 0% of each run, Pallas kernels for 12% -> 9%
where the time goes in v4:
time: 93.7 us; the launch traced here: 93.3 us
  starting transfers between devices  54.1 us (58%)
  Pallas kernels  13.4 us (14%)
  local copies, waits for them, and re-layouts  13.1 us (14%)
  waiting for transfers between devices  12.4 us (13%)
    ppermute x4, starting transfers between devices, shift(): return lax.ppermute(value, axis, pairs)  54.1 us
    pallas_call x4, Pallas kernels, call(): pl.pallas_call(kernel, out_shape=results, in_specs=specs, out_specs=[pl.B...  13.4 us
    ppermute x4, waiting for transfers between devices, shift(): return lax.ppermute(value, axis, pairs)  12.4 us
    unnamed x20, local copies, waits for them, and re-layouts  8.93 us
  transfers between devices with their start and end apart: 4, of which 1 were waited for; matrix products, arithmetic and copies ran while one was open for 0% of the time, Pallas kernels for 9%

profile of v4, /device:TPU:1, one launch (start us, length us, event | category | flops | bytes accessed | tf_op | source)
XLA Modules:
  0.0 93.3 jit_solution(8176819034598856485)
XLA Ops:
  0.0 0.0 copy-start.9
  0.0 0.0 copy-start
  0.0 1.4 %fusion = (bf16[12,6,4,512]{3,2,1,0:T(4,128)(2,1)S(1)}, bf16[12,6,4,512]{3,2,1,0:T(4,128)(2,1)S(1)}) fusion(bf16[12,12,4,512]{3,2,1,0:T(4,128)(2,1)} %bitcast.12), kind=kLoop, calls=%fused_computation.1 | loop fusion | bytes 1179648 | tf_op jit(solution)/shard_map/slice | solution.py:235
  1.4 0.1 reshape.16.east_ref.own_e_ref.refs_1_
  1.5 16.3 %collective-permute-start = (bf16[288,512]{1,0:T(8,128)(2,1)S(1)}, bf16[288,512]{1,0:T(8,128)(2,1)}, u32[]{:S(2)}, u32[]{:S(2)}) collective-permute-start(bf16[288,512]{1,0:T(8,128)(2,1)S(1)} %reshape.16.east_ref.own_e_ref.refs_1_), channel_id=1, source_target_pairs={{0,16},{16,32},{32,48},{48,64},{64,80},{80,96},{96,112},{112,128},... | collective-permute-start | bytes 884744 | tf_op jit(solution)/shard_map/ppermute | solution.py:23
  17.7 0.1 reshape.15.west_ref.own_w_ref.refs_0_
  17.8 6.6 %collective-permute-start.1 = (bf16[288,512]{1,0:T(8,128)(2,1)S(1)}, bf16[288,512]{1,0:T(8,128)(2,1)S(1)}, u32[]{:S(2)}, u32[]{:S(2)}) collective-permute-start(bf16[288,512]{1,0:T(8,128)(2,1)S(1)} %reshape.15.west_ref.own_w_ref.refs_0_), channel_id=1, source_target_pairs={{0,496},{16,0},{32,16},{48,32},{64,48},{80,64},{96,80},{112,96},{1... | collective-permute-start | bytes 884744 | tf_op jit(solution)/shard_map/ppermute | solution.py:23
  24.4 0.0 copy-done.9
  24.4 0.0 copy-done
  24.4 3.4 %shard_map.46 = (f32[576,512]{1,0:T(8,128)S(1)}, f32[3,288,512]{2,1,0:T(8,128)S(1)}, f32[3,288,512]{2,1,0:T(8,128)S(1)}, f32[8,128]{1,0:T(8,128)S(1)}) custom-call(bf16[288,512]{1,0:T(8,128)(2,1)S(1)} %reshape.15.west_ref.own_w_ref.refs_0_, bf16[288,512]{1,0:T(8,128)(2,1)S(1)} %reshape.16.east_ref.own_e_ref.refs_1_, f32[1,512]{1,0:T(1,128)S(1)} %bitcast.8, ...), custom_call_target="tpu_custom_call" | custom-call | flops 2000000000 | bytes 6887424 | tf_op jit(solution)/shard_map/pallas_call | solution.py:220
  27.8 0.0 copy-start.3
  27.8 1.2 %copy-done.3 = f32[3,288,512]{2,1,0:T(8,128)} copy-done((f32[3,288,512]{2,1,0:T(8,128)}, f32[3,288,512]{2,1,0:T(8,128)S(1)}, u32[]{:S(2)}) %copy-start.3) | copy-done | bytes 1769496
  29.1 1.2 %copy-done.5 = f32[3,288,512]{2,1,0:T(8,128)} copy-done((f32[3,288,512]{2,1,0:T(8,128)}, f32[3,288,512]{2,1,0:T(8,128)S(1)}, u32[]{:S(2)}) %copy-start.5) | copy-done | bytes 1769496
  30.3 0.0 collective-permute-done.west_ref.refs_2_
  30.3 12.4 %collective-permute-done.1.east_ref.refs_3_ = bf16[288,512]{1,0:T(8,128)(2,1)S(1)} collective-permute-done((bf16[288,512]{1,0:T(8,128)(2,1)S(1)}, bf16[288,512]{1,0:T(8,128)(2,1)S(1)}, u32[]{:S(2)}, u32[]{:S(2)}) %collective-permute-start.1) | collective-permute-done | bytes 294944 | tf_op jit(solution)/shard_map/ppermute | solution.py:23
  42.7 1.8 %shard_map.48 = (bf16[4,72,512]{2,1,0:T(8,128)(2,1)}, bf16[4,72,512]{2,1,0:T(8,128)(2,1)}) custom-call(f32[8,128]{1,0:T(8,128)S(1)} %get-tuple-element.17.ready_ref, bf16[288,512]{1,0:T(8,128)(2,1)S(1)} %reshape.15.west_ref.own_w_ref.refs_0_, bf16[288,512]{1,0:T(8,128)(2,1)S(1)} %reshape.16.east_ref.own_e_ref.refs_1_, ...), custom_call_target="tpu_custom_call" | custom-call | flops 1000000 | bytes 1773568 | tf_op jit(solution)/shard_map/pallas_call | solution.py:220
  44.5 0.7 copy-done.7
  45.2 29.3 %collective-permute-start.2 = (bf16[4,72,512]{2,1,0:T(8,128)(2,1)}, bf16[4,72,512]{2,1,0:T(8,128)(2,1)}, u32[]{:S(2)}, u32[]{:S(2)}) collective-permute-start(bf16[4,72,512]{2,1,0:T(8,128)(2,1)} %get-tuple-element.18), channel_id=1, source_target_pairs={{0,1},{1,2},{2,3},{3,4},{4,5},{5,6},{6,7},{7,8},{8,9},{9,10},{10,1... | collective-permute-start | bytes 884744 | tf_op jit(solution)/shard_map/ppermute | solution.py:23
  74.6 1.9 %collective-permute-start.3 = (bf16[4,72,512]{2,1,0:T(8,128)(2,1)}, bf16[4,72,512]{2,1,0:T(8,128)(2,1)}, u32[]{:S(2)}, u32[]{:S(2)}) collective-permute-start(bf16[4,72,512]{2,1,0:T(8,128)(2,1)} %get-tuple-element.19), channel_id=1, source_target_pairs={{1,0},{2,1},{3,2},{4,3},{5,4},{6,5},{7,6},{8,7},{9,8},{10,9},{11,1... | collective-permute-start | bytes 884744 | tf_op jit(solution)/shard_map/ppermute | solution.py:23
  76.5 0.1 add_select_fusion.closed_ref
  76.6 1.0 %copy-done.2 = bf16[512,512]{1,0:T(8,128)(2,1)S(1)} copy-done((bf16[512,512]{1,0:T(8,128)(2,1)S(1)}, bf16[512,512]{1,0:T(8,128)(2,1)}, u32[]{:S(2)}) %copy-start.2) | copy-done | bytes 524312
  77.6 1.5 %copy-done.4 = f32[3,288,512]{2,1,0:T(8,128)S(1)} copy-done((f32[3,288,512]{2,1,0:T(8,128)S(1)}, f32[3,288,512]{2,1,0:T(8,128)}, u32[]{:S(2)}) %copy-start.4) | copy-done | bytes 1769496
  79.1 1.5 %copy-done.6 = f32[3,288,512]{2,1,0:T(8,128)S(1)} copy-done((f32[3,288,512]{2,1,0:T(8,128)S(1)}, f32[3,288,512]{2,1,0:T(8,128)}, u32[]{:S(2)}) %copy-start.6) | copy-done | bytes 1769496
  80.6 1.0 %copy-done.8 = bf16[288,512]{1,0:T(8,128)(2,1)S(1)} copy-done((bf16[288,512]{1,0:T(8,128)(2,1)S(1)}, bf16[288,512]{1,0:T(8,128)(2,1)}, u32[]{:S(2)}) %copy-start.8) | copy-done | bytes 294936
  81.6 4.5 %shard_map.47 = (bf16[288,512]{1,0:T(8,128)(2,1)S(1)}, f32[3,288,512]{2,1,0:T(8,128)S(1)}) custom-call(f32[576,512]{1,0:T(8,128)S(1)} %get-tuple-element.13.query_ref, f32[3,288,512]{2,1,0:T(8,128)S(1)} %copy-done.4, f32[3,288,512]{2,1,0:T(8,128)S(1)} %copy-done.6, bf16[288,512]{1,0:T(8,128)(2,1)S(1)} %reshape.15.west_ref.own_w_ref.refs_0_, ...), custom_call_target="tpu_custom_call" | custom-call | flops 1500000000 | bytes 10061824 | tf_op jit(solution)/shard_map/pallas_call | solution.py:220
  86.1 0.0 collective-permute-done.2.north_ref
  86.1 0.0 collective-permute-done.3.south_ref
  86.1 3.7 %shard_map.49 = bf16[2,288,512]{2,1,0:T(8,128)(2,1)S(1)} custom-call(f32[2]{0:T(128)S(1)} %add_select_fusion.closed_ref, f32[576,512]{1,0:T(8,128)S(1)} %get-tuple-element.13.query_ref, f32[3,288,512]{2,1,0:T(8,128)S(1)} %get-tuple-element.16.rim_ref, bf16[4,72,512]{2,1,0:T(8,128)(2,1)} %collective-permute-done.2.north_ref, ...), custom_call_target="tpu_custom_call" | custom-call | flops 1000000000 | bytes 7112712 | tf_op jit(solution)/shard_map/pallas_call | solution.py:220
  89.8 0.0 copy-start.1
  89.8 0.8 copy-done.1
  90.6 1.5 %reshape.18 = bf16[2,12,6,4,512]{4,3,2,1,0:T(4,128)(2,1)S(1)} reshape(bf16[2,288,512]{2,1,0:T(8,128)(2,1)} %copy-done.1) | data formatting | bytes 1179648 | tf_op jit(solution)/shard_map/reshape | solution.py:292
  92.2 1.1 %copy.5 = bf16[12,2,6,4,512]{4,3,2,1,0:T(4,128)(2,1)} copy(bf16[12,2,6,4,512]{4,3,2,0,1:T(4,128)(2,1)S(1)} %bitcast.11) | data formatting | bytes 1179648 | tf_op jit(solution)/shard_map/transpose | solution.py:292
  (6 shorter events, 0.0 us)
Async XLA Ops:
  0.0 24.4 %copy-start.9 = (f32[512]{0:T(512)S(1)}, f32[512]{0:T(512)}, u32[]{:S(2)}) copy-start(f32[512]{0:T(512)} %param.5) | copy-start | bytes 6148
  0.0 24.4 %copy-start = (bf16[512,1536]{1,0:T(8,128)(2,1)S(1)}, bf16[512,1536]{1,0:T(8,128)(2,1)}, u32[]{:S(2)}) copy-start(bf16[512,1536]{1,0:T(8,128)(2,1)} %qkv_ref.5) | copy-start | bytes 4718596
  1.5 28.8 %collective-permute-start = (bf16[288,512]{1,0:T(8,128)(2,1)S(1)}, bf16[288,512]{1,0:T(8,128)(2,1)}, u32[]{:S(2)}, u32[]{:S(2)}) collective-permute-start(bf16[288,512]{1,0:T(8,128)(2,1)S(1)} %reshape.16.east_ref.own_e_ref.refs_1_), channel_id=1, source_target_pairs={{0,16},{16,32},{32,48},{48,64},{64,80},{80,96},{96,112},{112,128},... | collective-permute-start | bytes 884744 | tf_op jit(solution)/shard_map/ppermute | solution.py:23
  17.8 24.9 %collective-permute-start.1 = (bf16[288,512]{1,0:T(8,128)(2,1)S(1)}, bf16[288,512]{1,0:T(8,128)(2,1)S(1)}, u32[]{:S(2)}, u32[]{:S(2)}) collective-permute-start(bf16[288,512]{1,0:T(8,128)(2,1)S(1)} %reshape.15.west_ref.own_w_ref.refs_0_), channel_id=1, source_target_pairs={{0,496},{16,0},{32,16},{48,32},{64,48},{80,64},{96,80},{112,96},{1... | collective-permute-start | bytes 884744 | tf_op jit(solution)/shard_map/ppermute | solution.py:23
  27.8 1.2 %copy-start.3 = (f32[3,288,512]{2,1,0:T(8,128)}, f32[3,288,512]{2,1,0:T(8,128)S(1)}, u32[]{:S(2)}) copy-start(f32[3,288,512]{2,1,0:T(8,128)S(1)} %get-tuple-element.14.inner_ref) | copy-start | bytes 5308420
  29.1 1.2 %copy-start.5 = (f32[3,288,512]{2,1,0:T(8,128)}, f32[3,288,512]{2,1,0:T(8,128)S(1)}, u32[]{:S(2)}) copy-start(f32[3,288,512]{2,1,0:T(8,128)S(1)} %get-tuple-element.15.rim_ref) | copy-start | bytes 5308420
  44.5 0.7 copy-start.7
  45.2 40.9 %collective-permute-start.2 = (bf16[4,72,512]{2,1,0:T(8,128)(2,1)}, bf16[4,72,512]{2,1,0:T(8,128)(2,1)}, u32[]{:S(2)}, u32[]{:S(2)}) collective-permute-start(bf16[4,72,512]{2,1,0:T(8,128)(2,1)} %get-tuple-element.18), channel_id=1, source_target_pairs={{0,1},{1,2},{2,3},{3,4},{4,5},{5,6},{6,7},{7,8},{8,9},{9,10},{10,1... | collective-permute-start | bytes 884744 | tf_op jit(solution)/shard_map/ppermute | solution.py:23
  74.6 11.5 %collective-permute-start.3 = (bf16[4,72,512]{2,1,0:T(8,128)(2,1)}, bf16[4,72,512]{2,1,0:T(8,128)(2,1)}, u32[]{:S(2)}, u32[]{:S(2)}) collective-permute-start(bf16[4,72,512]{2,1,0:T(8,128)(2,1)} %get-tuple-element.19), channel_id=1, source_target_pairs={{1,0},{2,1},{3,2},{4,3},{5,4},{6,5},{7,6},{8,7},{9,8},{10,9},{11,1... | collective-permute-start | bytes 884744 | tf_op jit(solution)/shard_map/ppermute | solution.py:23
  76.6 1.0 %copy-start.2 = (bf16[512,512]{1,0:T(8,128)(2,1)S(1)}, bf16[512,512]{1,0:T(8,128)(2,1)}, u32[]{:S(2)}) copy-start(bf16[512,512]{1,0:T(8,128)(2,1)} %out_w_ref.3) | copy-start | bytes 1572868
  77.6 1.5 %copy-start.4 = (f32[3,288,512]{2,1,0:T(8,128)S(1)}, f32[3,288,512]{2,1,0:T(8,128)}, u32[]{:S(2)}) copy-start(f32[3,288,512]{2,1,0:T(8,128)} %copy-done.3) | copy-start | bytes 5308420
  79.1 1.5 %copy-start.6 = (f32[3,288,512]{2,1,0:T(8,128)S(1)}, f32[3,288,512]{2,1,0:T(8,128)}, u32[]{:S(2)}) copy-start(f32[3,288,512]{2,1,0:T(8,128)} %copy-done.5) | copy-start | bytes 5308420
  80.6 1.0 %copy-start.8 = (bf16[288,512]{1,0:T(8,128)(2,1)S(1)}, bf16[288,512]{1,0:T(8,128)(2,1)}, u32[]{:S(2)}) copy-start(bf16[288,512]{1,0:T(8,128)(2,1)} %copy-done.7) | copy-start | bytes 884740
  89.8 0.8 copy-start.1

commit v5 on v4

--- a/solution.py
+++ b/solution.py
@@ -222,7 +222,7 @@
         out_shape=results,
         in_specs=specs,
         out_specs=[pl.BlockSpec(memory_space=pltpu.VMEM)] * len(results),
-        compiler_params=pltpu.CompilerParams(vmem_limit_bytes=40 * 2**20),
+        compiler_params=pltpu.CompilerParams(vmem_limit_bytes=14 * 2**20),
         cost_estimate=pl.CostEstimate(flops=flops, bytes_accessed=moved, transcendentals=0),
     )(*operands)
 

time: 93.7 us -> 93.7 us (level)
  no operation moved by 1% of the time
where the time goes in v5:
time: 93.7 us; the launch traced here: 93.3 us
  starting transfers between devices  54.1 us (58%)
  Pallas kernels  13.4 us (14%)
  local copies, waits for them, and re-layouts  13.1 us (14%)
  waiting for transfers between devices  12.4 us (13%)
    ppermute x4, starting transfers between devices, shift(): return lax.ppermute(value, axis, pairs)  54.1 us
    pallas_call x4, Pallas kernels, call(): pl.pallas_call(kernel, out_shape=results, in_specs=specs, out_specs=[pl.B...  13.4 us
    ppermute x4, waiting for transfers between devices, shift(): return lax.ppermute(value, axis, pairs)  12.4 us
    unnamed x20, local copies, waits for them, and re-layouts  8.93 us
  transfers between devices with their start and end apart: 4, of which 1 were waited for; matrix products, arithmetic and copies ran while one was open for 0% of the time, Pallas kernels for 9%

profile of v5, /device:TPU:1, one launch (start us, length us, event | category | flops | bytes accessed | tf_op | source)
XLA Modules:
  0.0 93.3 jit_solution(14346094984220255127)
XLA Ops:
  0.0 0.0 copy-start.9
  0.0 0.0 copy-start
  0.0 1.4 %fusion = (bf16[12,6,4,512]{3,2,1,0:T(4,128)(2,1)S(1)}, bf16[12,6,4,512]{3,2,1,0:T(4,128)(2,1)S(1)}) fusion(bf16[12,12,4,512]{3,2,1,0:T(4,128)(2,1)} %bitcast.12), kind=kLoop, calls=%fused_computation.1 | loop fusion | bytes 1179648 | tf_op jit(solution)/shard_map/slice | solution.py:235
  1.4 0.1 reshape.16.east_ref.own_e_ref.refs_1_
  1.5 16.3 %collective-permute-start = (bf16[288,512]{1,0:T(8,128)(2,1)S(1)}, bf16[288,512]{1,0:T(8,128)(2,1)}, u32[]{:S(2)}, u32[]{:S(2)}) collective-permute-start(bf16[288,512]{1,0:T(8,128)(2,1)S(1)} %reshape.16.east_ref.own_e_ref.refs_1_), channel_id=1, source_target_pairs={{0,16},{16,32},{32,48},{48,64},{64,80},{80,96},{96,112},{112,128},... | collective-permute-start | bytes 884744 | tf_op jit(solution)/shard_map/ppermute | solution.py:23
  17.7 0.1 reshape.15.west_ref.own_w_ref.refs_0_
  17.8 6.6 %collective-permute-start.1 = (bf16[288,512]{1,0:T(8,128)(2,1)S(1)}, bf16[288,512]{1,0:T(8,128)(2,1)S(1)}, u32[]{:S(2)}, u32[]{:S(2)}) collective-permute-start(bf16[288,512]{1,0:T(8,128)(2,1)S(1)} %reshape.15.west_ref.own_w_ref.refs_0_), channel_id=1, source_target_pairs={{0,496},{16,0},{32,16},{48,32},{64,48},{80,64},{96,80},{112,96},{1... | collective-permute-start | bytes 884744 | tf_op jit(solution)/shard_map/ppermute | solution.py:23
  24.4 0.0 copy-done.9
  24.4 0.0 copy-done
  24.4 3.4 %shard_map.46 = (f32[576,512]{1,0:T(8,128)S(1)}, f32[3,288,512]{2,1,0:T(8,128)S(1)}, f32[3,288,512]{2,1,0:T(8,128)S(1)}, f32[8,128]{1,0:T(8,128)S(1)}) custom-call(bf16[288,512]{1,0:T(8,128)(2,1)S(1)} %reshape.15.west_ref.own_w_ref.refs_0_, bf16[288,512]{1,0:T(8,128)(2,1)S(1)} %reshape.16.east_ref.own_e_ref.refs_1_, f32[1,512]{1,0:T(1,128)S(1)} %bitcast.8, ...), custom_call_target="tpu_custom_call" | custom-call | flops 2000000000 | bytes 6887424 | tf_op jit(solution)/shard_map/pallas_call | solution.py:220
  27.8 0.0 copy-start.3
  27.8 1.2 %copy-done.3 = f32[3,288,512]{2,1,0:T(8,128)} copy-done((f32[3,288,512]{2,1,0:T(8,128)}, f32[3,288,512]{2,1,0:T(8,128)S(1)}, u32[]{:S(2)}) %copy-start.3) | copy-done | bytes 1769496
  29.1 1.2 %copy-done.5 = f32[3,288,512]{2,1,0:T(8,128)} copy-done((f32[3,288,512]{2,1,0:T(8,128)}, f32[3,288,512]{2,1,0:T(8,128)S(1)}, u32[]{:S(2)}) %copy-start.5) | copy-done | bytes 1769496
  30.3 0.0 collective-permute-done.west_ref.refs_2_
  30.3 12.4 %collective-permute-done.1.east_ref.refs_3_ = bf16[288,512]{1,0:T(8,128)(2,1)S(1)} collective-permute-done((bf16[288,512]{1,0:T(8,128)(2,1)S(1)}, bf16[288,512]{1,0:T(8,128)(2,1)S(1)}, u32[]{:S(2)}, u32[]{:S(2)}) %collective-permute-start.1) | collective-permute-done | bytes 294944 | tf_op jit(solution)/shard_map/ppermute | solution.py:23
  42.7 1.8 %shard_map.48 = (bf16[4,72,512]{2,1,0:T(8,128)(2,1)}, bf16[4,72,512]{2,1,0:T(8,128)(2,1)}) custom-call(f32[8,128]{1,0:T(8,128)S(1)} %get-tuple-element.17.ready_ref, bf16[288,512]{1,0:T(8,128)(2,1)S(1)} %reshape.15.west_ref.own_w_ref.refs_0_, bf16[288,512]{1,0:T(8,128)(2,1)S(1)} %reshape.16.east_ref.own_e_ref.refs_1_, ...), custom_call_target="tpu_custom_call" | custom-call | flops 1000000 | bytes 1773568 | tf_op jit(solution)/shard_map/pallas_call | solution.py:220
  44.5 0.7 copy-done.7
  45.2 29.3 %collective-permute-start.2 = (bf16[4,72,512]{2,1,0:T(8,128)(2,1)}, bf16[4,72,512]{2,1,0:T(8,128)(2,1)}, u32[]{:S(2)}, u32[]{:S(2)}) collective-permute-start(bf16[4,72,512]{2,1,0:T(8,128)(2,1)} %get-tuple-element.18), channel_id=1, source_target_pairs={{0,1},{1,2},{2,3},{3,4},{4,5},{5,6},{6,7},{7,8},{8,9},{9,10},{10,1... | collective-permute-start | bytes 884744 | tf_op jit(solution)/shard_map/ppermute | solution.py:23
  74.6 1.9 %collective-permute-start.3 = (bf16[4,72,512]{2,1,0:T(8,128)(2,1)}, bf16[4,72,512]{2,1,0:T(8,128)(2,1)}, u32[]{:S(2)}, u32[]{:S(2)}) collective-permute-start(bf16[4,72,512]{2,1,0:T(8,128)(2,1)} %get-tuple-element.19), channel_id=1, source_target_pairs={{1,0},{2,1},{3,2},{4,3},{5,4},{6,5},{7,6},{8,7},{9,8},{10,9},{11,1... | collective-permute-start | bytes 884744 | tf_op jit(solution)/shard_map/ppermute | solution.py:23
  76.5 0.1 add_select_fusion.closed_ref
  76.6 1.0 %copy-done.2 = bf16[512,512]{1,0:T(8,128)(2,1)S(1)} copy-done((bf16[512,512]{1,0:T(8,128)(2,1)S(1)}, bf16[512,512]{1,0:T(8,128)(2,1)}, u32[]{:S(2)}) %copy-start.2) | copy-done | bytes 524312
  77.6 1.5 %copy-done.4 = f32[3,288,512]{2,1,0:T(8,128)S(1)} copy-done((f32[3,288,512]{2,1,0:T(8,128)S(1)}, f32[3,288,512]{2,1,0:T(8,128)}, u32[]{:S(2)}) %copy-start.4) | copy-done | bytes 1769496
  79.1 1.5 %copy-done.6 = f32[3,288,512]{2,1,0:T(8,128)S(1)} copy-done((f32[3,288,512]{2,1,0:T(8,128)S(1)}, f32[3,288,512]{2,1,0:T(8,128)}, u32[]{:S(2)}) %copy-start.6) | copy-done | bytes 1769496
  80.6 1.0 %copy-done.8 = bf16[288,512]{1,0:T(8,128)(2,1)S(1)} copy-done((bf16[288,512]{1,0:T(8,128)(2,1)S(1)}, bf16[288,512]{1,0:T(8,128)(2,1)}, u32[]{:S(2)}) %copy-start.8) | copy-done | bytes 294936
  81.6 4.5 %shard_map.47 = (bf16[288,512]{1,0:T(8,128)(2,1)S(1)}, f32[3,288,512]{2,1,0:T(8,128)S(1)}) custom-call(f32[576,512]{1,0:T(8,128)S(1)} %get-tuple-element.13.query_ref, f32[3,288,512]{2,1,0:T(8,128)S(1)} %copy-done.4, f32[3,288,512]{2,1,0:T(8,128)S(1)} %copy-done.6, bf16[288,512]{1,0:T(8,128)(2,1)S(1)} %reshape.15.west_ref.own_w_ref.refs_0_, ...), custom_call_target="tpu_custom_call" | custom-call | flops 1500000000 | bytes 10061824 | tf_op jit(solution)/shard_map/pallas_call | solution.py:220
  86.1 0.0 collective-permute-done.2.north_ref
  86.1 0.0 collective-permute-done.3.south_ref
  86.1 3.7 %shard_map.49 = bf16[2,288,512]{2,1,0:T(8,128)(2,1)S(1)} custom-call(f32[2]{0:T(128)S(1)} %add_select_fusion.closed_ref, f32[576,512]{1,0:T(8,128)S(1)} %get-tuple-element.13.query_ref, f32[3,288,512]{2,1,0:T(8,128)S(1)} %get-tuple-element.16.rim_ref, bf16[4,72,512]{2,1,0:T(8,128)(2,1)} %collective-permute-done.2.north_ref, ...), custom_call_target="tpu_custom_call" | custom-call | flops 1000000000 | bytes 7112712 | tf_op jit(solution)/shard_map/pallas_call | solution.py:220
  89.8 0.0 copy-start.1
  89.8 0.8 copy-done.1
  90.6 1.5 %reshape.18 = bf16[2,12,6,4,512]{4,3,2,1,0:T(4,128)(2,1)S(1)} reshape(bf16[2,288,512]{2,1,0:T(8,128)(2,1)} %copy-done.1) | data formatting | bytes 1179648 | tf_op jit(solution)/shard_map/reshape | solution.py:292
  92.2 1.1 %copy.5 = bf16[12,2,6,4,512]{4,3,2,1,0:T(4,128)(2,1)} copy(bf16[12,2,6,4,512]{4,3,2,0,1:T(4,128)(2,1)S(1)} %bitcast.11) | data formatting | bytes 1179648 | tf_op jit(solution)/shard_map/transpose | solution.py:292
  (6 shorter events, 0.0 us)
Async XLA Ops:
  0.0 24.4 %copy-start.9 = (f32[512]{0:T(512)S(1)}, f32[512]{0:T(512)}, u32[]{:S(2)}) copy-start(f32[512]{0:T(512)} %param.5) | copy-start | bytes 6148
  0.0 24.4 %copy-start = (bf16[512,1536]{1,0:T(8,128)(2,1)S(1)}, bf16[512,1536]{1,0:T(8,128)(2,1)}, u32[]{:S(2)}) copy-start(bf16[512,1536]{1,0:T(8,128)(2,1)} %qkv_ref.5) | copy-start | bytes 4718596
  1.5 28.8 %collective-permute-start = (bf16[288,512]{1,0:T(8,128)(2,1)S(1)}, bf16[288,512]{1,0:T(8,128)(2,1)}, u32[]{:S(2)}, u32[]{:S(2)}) collective-permute-start(bf16[288,512]{1,0:T(8,128)(2,1)S(1)} %reshape.16.east_ref.own_e_ref.refs_1_), channel_id=1, source_target_pairs={{0,16},{16,32},{32,48},{48,64},{64,80},{80,96},{96,112},{112,128},... | collective-permute-start | bytes 884744 | tf_op jit(solution)/shard_map/ppermute | solution.py:23
  17.8 24.9 %collective-permute-start.1 = (bf16[288,512]{1,0:T(8,128)(2,1)S(1)}, bf16[288,512]{1,0:T(8,128)(2,1)S(1)}, u32[]{:S(2)}, u32[]{:S(2)}) collective-permute-start(bf16[288,512]{1,0:T(8,128)(2,1)S(1)} %reshape.15.west_ref.own_w_ref.refs_0_), channel_id=1, source_target_pairs={{0,496},{16,0},{32,16},{48,32},{64,48},{80,64},{96,80},{112,96},{1... | collective-permute-start | bytes 884744 | tf_op jit(solution)/shard_map/ppermute | solution.py:23
  27.8 1.2 %copy-start.3 = (f32[3,288,512]{2,1,0:T(8,128)}, f32[3,288,512]{2,1,0:T(8,128)S(1)}, u32[]{:S(2)}) copy-start(f32[3,288,512]{2,1,0:T(8,128)S(1)} %get-tuple-element.14.inner_ref) | copy-start | bytes 5308420
  29.1 1.2 %copy-start.5 = (f32[3,288,512]{2,1,0:T(8,128)}, f32[3,288,512]{2,1,0:T(8,128)S(1)}, u32[]{:S(2)}) copy-start(f32[3,288,512]{2,1,0:T(8,128)S(1)} %get-tuple-element.15.rim_ref) | copy-start | bytes 5308420
  44.5 0.7 copy-start.7
  45.2 40.9 %collective-permute-start.2 = (bf16[4,72,512]{2,1,0:T(8,128)(2,1)}, bf16[4,72,512]{2,1,0:T(8,128)(2,1)}, u32[]{:S(2)}, u32[]{:S(2)}) collective-permute-start(bf16[4,72,512]{2,1,0:T(8,128)(2,1)} %get-tuple-element.18), channel_id=1, source_target_pairs={{0,1},{1,2},{2,3},{3,4},{4,5},{5,6},{6,7},{7,8},{8,9},{9,10},{10,1... | collective-permute-start | bytes 884744 | tf_op jit(solution)/shard_map/ppermute | solution.py:23
  74.6 11.5 %collective-permute-start.3 = (bf16[4,72,512]{2,1,0:T(8,128)(2,1)}, bf16[4,72,512]{2,1,0:T(8,128)(2,1)}, u32[]{:S(2)}, u32[]{:S(2)}) collective-permute-start(bf16[4,72,512]{2,1,0:T(8,128)(2,1)} %get-tuple-element.19), channel_id=1, source_target_pairs={{1,0},{2,1},{3,2},{4,3},{5,4},{6,5},{7,6},{8,7},{9,8},{10,9},{11,1... | collective-permute-start | bytes 884744 | tf_op jit(solution)/shard_map/ppermute | solution.py:23
  76.6 1.0 %copy-start.2 = (bf16[512,512]{1,0:T(8,128)(2,1)S(1)}, bf16[512,512]{1,0:T(8,128)(2,1)}, u32[]{:S(2)}) copy-start(bf16[512,512]{1,0:T(8,128)(2,1)} %out_w_ref.3) | copy-start | bytes 1572868
  77.6 1.5 %copy-start.4 = (f32[3,288,512]{2,1,0:T(8,128)S(1)}, f32[3,288,512]{2,1,0:T(8,128)}, u32[]{:S(2)}) copy-start(f32[3,288,512]{2,1,0:T(8,128)} %copy-done.3) | copy-start | bytes 5308420
  79.1 1.5 %copy-start.6 = (f32[3,288,512]{2,1,0:T(8,128)S(1)}, f32[3,288,512]{2,1,0:T(8,128)}, u32[]{:S(2)}) copy-start(f32[3,288,512]{2,1,0:T(8,128)} %copy-done.5) | copy-start | bytes 5308420
  80.6 1.0 %copy-start.8 = (bf16[288,512]{1,0:T(8,128)(2,1)S(1)}, bf16[288,512]{1,0:T(8,128)(2,1)}, u32[]{:S(2)}) copy-start(bf16[288,512]{1,0:T(8,128)(2,1)} %copy-done.7) | copy-start | bytes 884740
  89.8 0.8 copy-start.1

commit v6 on v2

v6 whole, which is shorter than its diff:
```python
import jax
import jax.numpy as jnp
from jax import lax
from jax.experimental import pallas as pl
from jax.experimental.pallas import tpu as pltpu
from jax.sharding import PartitionSpec as P

HEADS = 8
HEAD_SIZE = 64
GROUP = 4
SPAN = GROUP * HEAD_SIZE
EPS = 1e-05
FAR = -1e30
HALF = 6
EDGE = 3
LEVELS = 4
RIM = EDGE * HALF * LEVELS


def shift(value, axis, by, wrap):
    count = lax.axis_size(axis)
    pairs = [(i, (i + by) % count) for i in range(count) if wrap or 0 <= i + by < count]
    return lax.ppermute(value, axis, pairs)


def layer_norm(values, gain):
    center = values - jnp.mean(values, axis=-1, keepdims=True)
    spread = jnp.mean(center * center, axis=-1, keepdims=True)
    return (center * lax.rsqrt(spread + EPS) * gain).astype(jnp.bfloat16)


def matmul(a, b):
    return jnp.dot(a, b, preferred_element_type=jnp.float32)


def rounded(values):
    return values.astype(jnp.bfloat16).astype(jnp.float32)


def level_bias(rows, keys):
    def part(axis):
        level = lax.broadcasted_iota(jnp.int32, (rows, keys), axis) % LEVELS
        return jnp.where(level == 0, 2, jnp.where(level == LEVELS - 1, 1, 0))

    return jnp.where(part(0) == part(1), 0.0, FAR).astype(jnp.float32)


def attend(query, keys, values, bias):
    rows = query.shape[0]
    owner = lax.broadcasted_iota(jnp.int32, (rows, SPAN), 1) // HEAD_SIZE
    tall = jnp.concatenate([bias] * GROUP, axis=0)
    parts = []
    for start in range(0, query.shape[1], SPAN):
        piece = query[:, start : start + SPAN]
        spread = jnp.concatenate(
            [jnp.where(owner == h, piece, 0.0) for h in range(GROUP)], axis=0
        ).astype(jnp.bfloat16)
        scores = lax.dot_general(
            spread,
            keys[:, start : start + SPAN],
            (((1,), (1,)), ((), ())),
            preferred_element_type=jnp.float32,
        )
        scores = scores + tall
        expo = jnp.exp(scores - jnp.max(scores, axis=-1, keepdims=True))
        scale = 1.0 / jnp.sum(expo, axis=-1, keepdims=True)
        out = matmul(expo.astype(jnp.bfloat16), values[:, start : start + SPAN]) * scale
        merged = out[:rows]
        for h in range(1, GROUP):
            merged = jnp.where(owner == h, out[h * rows : (h + 1) * rows], merged)
        parts.append(merged)
    return jnp.concatenate(parts, axis=1)


def project(tokens, heads, weight_ref):
    branch = matmul(heads.astype(jnp.bfloat16), weight_ref[...])
    return (tokens + rounded(branch)).astype(jnp.bfloat16)


def make_query(normed, qkv_ref):
    width = normed.shape[-1]
    return rounded(matmul(normed, qkv_ref[:, :width])) * HEAD_SIZE**-0.5


def make_keys(normed, qkv_ref):
    width = normed.shape[-1]
    return matmul(normed, qkv_ref[:, width:])


def inner_kernel(
    own_w_ref,
    own_e_ref,
    west_ref,
    east_ref,
    gain_ref,
    qkv_ref,
    out_w_ref,
    out_ref,
    query_ref,
    keys_ref,
):
    rows, width = own_w_ref.shape
    count = rows - 2 * RIM
    gain = gain_ref[...]
    own = jnp.concatenate([r[...].astype(jnp.float32) for r in (own_w_ref, own_e_ref)], axis=0)
    normed = layer_norm(own, gain)
    query = make_query(normed, qkv_ref)
    mine = make_keys(normed, qkv_ref)
    halos = jnp.concatenate([r[...].astype(jnp.float32) for r in (west_ref, east_ref)], axis=0)
    halos = make_keys(layer_norm(halos, gain), qkv_ref)
    for edge in range(2):
        for side in range(2):
            place = edge * 2 + side
            begin = side * rows + edge * (rows - RIM)
            at = slice(begin, begin + RIM)
            query_ref[place] = query[at]
            keys_ref[place] = jnp.concatenate([mine[at], halos[at]], axis=0).astype(jnp.bfloat16)
    bias = level_bias(count, 2 * count)
    heads, tokens = [], []
    for side in range(2):
        at = slice(side * rows + RIM, (side + 1) * rows - RIM)
        kv = jnp.concatenate([mine[at], halos[at]], axis=0).astype(jnp.bfloat16)
        heads.append(attend(query[at], kv[:, :width], kv[:, width:], bias))
        tokens.append(own[at])
    out_ref[...] = project(jnp.concatenate(tokens, axis=0), jnp.concatenate(heads, axis=0), out_w_ref)


def edge_kernel(
    closed_ref,
    query_ref,
    keys_ref,
    north_ref,
    south_ref,
    far_north_ref,
    far_south_ref,
    own_w_ref,
    own_e_ref,
    middle_ref,
    gain_ref,
    qkv_ref,
    out_w_ref,
    out_ref,
):
    rows, width = own_w_ref.shape
    count = rows - 2 * RIM
    refs = ((north_ref, far_north_ref), (south_ref, far_south_ref))
    beyond = [r[side].astype(jnp.float32) for pair in refs for side in range(2) for r in pair]
    beyond = make_keys(layer_norm(jnp.concatenate(beyond, axis=0), gain_ref[...]), qkv_ref).astype(jnp.bfloat16)
    levels = level_bias(RIM, 4 * RIM)
    distant = lax.broadcasted_iota(jnp.int32, (RIM, 4 * RIM), 1) >= 2 * RIM
    own = [r[...].astype(jnp.float32) for r in (own_w_ref, own_e_ref)]
    heads, tokens = [], []
    for edge in range(2):
        bias = levels + jnp.where(distant, closed_ref[edge], 0.0)
        for side in range(2):
            place = edge * 2 + side
            begin = edge * (rows - RIM)
            kv = jnp.concatenate([keys_ref[place], beyond[2 * place * RIM : 2 * (place + 1) * RIM]], axis=0)
            heads.append(attend(query_ref[place], kv[:, :width], kv[:, width:], bias))
            tokens.append(own[side][begin : begin + RIM])
    mixed = project(jnp.concatenate(tokens, axis=0), jnp.concatenate(heads, axis=0), out_w_ref).astype(jnp.float32)
    middle = middle_ref[...].astype(jnp.float32)
    for side in range(2):
        out_ref[side] = jnp.concatenate(
            [
                mixed[side * RIM : (side + 1) * RIM],
                middle[side * count : (side + 1) * count],
                mixed[(2 + side) * RIM : (3 + side) * RIM],
            ],
            axis=0,
        ).astype(jnp.bfloat16)


def call(kernel, results, flops, *operands):
    moved = sum(x.size * x.dtype.itemsize for x in (*operands, *results))
    specs = [pl.BlockSpec(memory_space=pltpu.SMEM if x.ndim == 1 else pltpu.VMEM) for x in operands]
    return pl.pallas_call(
        kernel,
        out_shape=results,
        in_specs=specs,
        out_specs=[pl.BlockSpec(memory_space=pltpu.VMEM)] * len(results),
        compiler_params=pltpu.CompilerParams(vmem_limit_bytes=14 * 2**20),
        cost_estimate=pl.CostEstimate(flops=flops, bytes_accessed=moved, transcendentals=0),
    )(*operands)


def shards(tokens, gain_attn, weight_qkv, weight_out):
    lev_count, row_count, col_count, width = tokens.shape
    rows = row_count * HALF * lev_count
    by_place = tokens.transpose(1, 2, 0, 3)
    own_w = by_place[:, :HALF].reshape(rows, width)
    own_e = by_place[:, HALF:].reshape(rows, width)
    east = shift(own_w, "lon", -1, True)
    west = shift(own_e, "lon", 1, True)

    def rim(*halves):
        return jnp.stack([h[:RIM] for h in halves]), jnp.stack([h[rows - RIM :] for h in halves])

    first, last = rim(own_w, own_e)
    south = shift(first, "lat", -1, False)
    north = shift(last, "lat", 1, False)
    first, last = rim(west, east)
    far_south = shift(first, "lat", -1, False)
    far_north = shift(last, "lat", 1, False)
    gain = gain_attn.reshape(1, width)
    place = lax.axis_index("lat")
    closed = jnp.stack([place == 0, place == lax.axis_size("lat") - 1])
    closed = jnp.where(closed, FAR, 0.0).astype(jnp.float32)

    def shape(*dims, dtype=jnp.float32):
        return jax.ShapeDtypeStruct(dims, dtype)

    middle, query, keys = call(
        inner_kernel,
        [
            shape(2 * (rows - 2 * RIM), width, dtype=jnp.bfloat16),
            shape(4, RIM, width),
            shape(4, 2 * RIM, 2 * width, dtype=jnp.bfloat16),
        ],
        2_500_000_000,
        own_w,
        own_e,
        west,
        east,
        gain,
        weight_qkv,
        weight_out,
    )
    (mixed,) = call(
        edge_kernel,
        [shape(2, rows, width, dtype=jnp.bfloat16)],
        1_000_000_000,
        closed,
        query,
        keys,
        north,
        south,
        far_north,
        far_south,
        own_w,
        own_e,
        middle,
        gain,
        weight_qkv,
        weight_out,
    )
    mixed = mixed.reshape(2, row_count, HALF, lev_count, width).transpose(1, 0, 2, 3, 4)
    return mixed.reshape(row_count, col_count, lev_count, width).transpose(2, 0, 1, 3)


def solution(mesh):
    placed = (P(None, "lat", "lon", None), P(), P(), P())
    return jax.shard_map(
        shards, mesh=mesh, in_specs=placed, out_specs=P(None, "lat", "lon", None), check_vma=False
    )
```

time: 91.2 us -> 86.8 us (0.952)
  waiting for transfers between devices: 44.1 us -> 10.9 us
  starting transfers between devices: 33 us -> 58.8 us
  local copies, waits for them, and re-layouts: 2.93 us -> 6.35 us
  Pallas kernels: 10.4 us -> 8.12 us
  other arithmetic: 0.15 us -> 1.46 us
    ppermute x6, waiting for transfers between devices: 44.1 us -> 10.9 us  [shift(): return lax.ppermute(value, axis, pairs)]
    ppermute x6, starting transfers between devices: 33 us -> 58.8 us  [shift(): return lax.ppermute(value, axis, pairs)]
    pallas_call x3 -> x2, Pallas kernels: 10.4 us -> 8.12 us  [call(): pl.pallas_call(kernel, out_shape=results, in_specs=specs, out_specs=[pl.B...]
    unnamed x8 -> x10, local copies, waits for them, and re-layouts: 0.02 us -> 1.58 us
    another operation x4, other arithmetic: 0.07 us -> 1.38 us  [the longest x2 0.69 us: rim(): jnp.stack([h[rows - RIM:] for h in halves])]
    slice x1, local copies, waits for them, and re-layouts: 0.1 us -> 1.11 us  [rim(): h[:RIM]]
    another operation x6, local copies, waits for them, and re-layouts: 0.11 us -> 1.03 us  [the longest x4 0.99 us: rim(): jnp.stack([h[:RIM] for h in halves])]
  transfers between devices with their start and end apart: 6 -> 6, of which waited for: 1 -> 1; matrix products, arithmetic and copies ran while one was open for 0% -> 4% of each run, Pallas kernels for 9% -> 6%
where the time goes in v6:
time: 86.8 us; the launch traced here: 85.8 us
  starting transfers between devices  58.8 us (68%)
  waiting for transfers between devices  10.9 us (13%)
  Pallas kernels  8.12 us (9%)
  local copies, waits for them, and re-layouts  6.35 us (7%)
  other arithmetic  1.46 us (2%)
    ppermute x6, starting transfers between devices, shift(): return lax.ppermute(value, axis, pairs)  58.8 us
    ppermute x6, waiting for transfers between devices, shift(): return lax.ppermute(value, axis, pairs)  10.9 us
    pallas_call x2, Pallas kernels, call(): pl.pallas_call(kernel, out_shape=results, in_specs=specs, out_specs=[pl.B...  8.12 us
  transfers between devices with their start and end apart: 6, of which 1 were waited for; matrix products, arithmetic and copies ran while one was open for 4% of the time, Pallas kernels for 6%

profile of v6, /device:TPU:1, one launch (start us, length us, event | category | flops | bytes accessed | tf_op | source)
XLA Modules:
  0.0 85.8 jit_solution(3091075135047174864)
XLA Ops:
  0.0 1.3 %fusion.1 = (bf16[12,6,4,512]{3,2,1,0:T(4,128)(2,1)S(1)}, bf16[12,6,4,512]{3,2,1,0:T(4,128)(2,1)S(1)}) fusion(bf16[12,12,4,512]{3,2,1,0:T(4,128)(2,1)} %bitcast.19), kind=kLoop, calls=%fused_computation.10 | loop fusion | bytes 1179648 | tf_op jit(solution)/shard_map/slice | solution.py:192
  1.3 0.1 reshape.24.own_e_ref
  1.3 16.3 %collective-permute-start = (bf16[288,512]{1,0:T(8,128)(2,1)S(1)}, bf16[288,512]{1,0:T(8,128)(2,1)S(1)}, u32[]{:S(2)}, u32[]{:S(2)}) collective-permute-start(bf16[288,512]{1,0:T(8,128)(2,1)S(1)} %reshape.24.own_e_ref), channel_id=1, source_target_pairs={{0,16},{16,32},{32,48},{48,64},{64,80},{80,96},{96,112},{112,128},... | collective-permute-start | bytes 884744 | tf_op jit(solution)/shard_map/ppermute | solution.py:23
  17.6 0.1 reshape.23.own_w_ref
  17.7 0.0 copy-start
  17.7 0.0 copy-start.1
  17.7 0.0 copy-start.4
  17.7 6.7 %collective-permute-start.1 = (bf16[288,512]{1,0:T(8,128)(2,1)S(1)}, bf16[288,512]{1,0:T(8,128)(2,1)}, u32[]{:S(2)}, u32[]{:S(2)}) collective-permute-start(bf16[288,512]{1,0:T(8,128)(2,1)S(1)} %reshape.23.own_w_ref), channel_id=1, source_target_pairs={{0,496},{16,0},{32,16},{48,32},{64,48},{80,64},{96,80},{112,96},{1... | collective-permute-start | bytes 884744 | tf_op jit(solution)/shard_map/ppermute | solution.py:23
  24.4 1.1 %fusion = (bf16[3,6,4,512]{3,2,1,0:T(4,128)(2,1)S(1)}, bf16[3,6,4,512]{3,2,1,0:T(4,128)(2,1)S(1)}, bf16[3,6,4,512]{3,2,1,0:T(4,128)(2,1)S(1)}, bf16[3,6,4,512]{3,2,1,0:T(4,128)(2,1)S(1)}) fusion(bf16[12,12,4,512]{3,2,1,0:T(4,128)(2,1)} %bitcast.20), kind=kLoop, calls=%fused_computation.9 | loop fusion | bytes 589824 | tf_op jit(solution)/shard_map/slice | solution.py:197
  25.6 0.7 pad_maximum_fusion
  26.3 3.5 %collective-permute-start.2 = (bf16[2,72,512]{2,1,0:T(8,128)(2,1)}, bf16[2,72,512]{2,1,0:T(8,128)(2,1)S(1)}, u32[]{:S(2)}, u32[]{:S(2)}) collective-permute-start(bf16[2,72,512]{2,1,0:T(8,128)(2,1)} %pad_maximum_fusion), channel_id=1, source_target_pairs={{0,1},{1,2},{2,3},{3,4},{4,5},{5,6},{6,7},{7,8},{8,9},{9,10},{10,1... | collective-permute-start | bytes 442376 | tf_op jit(solution)/shard_map/ppermute | solution.py:23
  29.8 0.7 pad_maximum_fusion.1
  30.5 2.5 %collective-permute-start.3 = (bf16[2,72,512]{2,1,0:T(8,128)(2,1)}, bf16[2,72,512]{2,1,0:T(8,128)(2,1)S(1)}, u32[]{:S(2)}, u32[]{:S(2)}) collective-permute-start(bf16[2,72,512]{2,1,0:T(8,128)(2,1)} %pad_maximum_fusion.1), channel_id=1, source_target_pairs={{1,0},{2,1},{3,2},{4,3},{5,4},{6,5},{7,6},{8,7},{9,8},{10,9},{11,1... | collective-permute-start | bytes 442376 | tf_op jit(solution)/shard_map/ppermute | solution.py:23
  33.0 0.1 add_select_fusion.closed_ref
  33.1 0.0 collective-permute-done.west_ref
  33.1 10.9 %collective-permute-done.1.east_ref = bf16[288,512]{1,0:T(8,128)(2,1)} collective-permute-done((bf16[288,512]{1,0:T(8,128)(2,1)S(1)}, bf16[288,512]{1,0:T(8,128)(2,1)}, u32[]{:S(2)}, u32[]{:S(2)}) %collective-permute-start.1) | collective-permute-done | bytes 294944 | tf_op jit(solution)/shard_map/ppermute | solution.py:23
  44.0 0.9 %slice_bitcast_fusion = (bf16[1,72,512]{2,1,0:T(8,128)(2,1)S(1)}, bf16[1,72,512]{2,1,0:T(8,128)(2,1)S(1)}) fusion(bf16[288,512]{1,0:T(8,128)(2,1)} %collective-permute-done.1.east_ref), kind=kLoop, calls=%fused_computation.4 | loop fusion | bytes 294912 | tf_op jit(solution)/shard_map/stack | solution.py:197
  45.0 27.9 %collective-permute-start.4 = (bf16[2,72,512]{2,1,0:T(8,128)(2,1)S(1)}, bf16[2,72,512]{2,1,0:T(8,128)(2,1)S(1)}, u32[]{:S(2)}, u32[]{:S(2)}) collective-permute-start(bf16[2,72,512]{2,1,0:T(8,128)(2,1)S(1)} %pad_maximum_fusion.2), channel_id=1, source_target_pairs={{0,1},{1,2},{2,3},{3,4},{4,5},{5,6},{6,7},{7,8},{8,9},{9,10},{10,1... | collective-permute-start | bytes 442376 | tf_op jit(solution)/shard_map/ppermute | solution.py:23
  72.9 1.9 %collective-permute-start.5 = (bf16[2,72,512]{2,1,0:T(8,128)(2,1)S(1)}, bf16[2,72,512]{2,1,0:T(8,128)(2,1)S(1)}, u32[]{:S(2)}, u32[]{:S(2)}) collective-permute-start(bf16[2,72,512]{2,1,0:T(8,128)(2,1)S(1)} %pad_maximum_fusion.3), channel_id=1, source_target_pairs={{1,0},{2,1},{3,2},{4,3},{5,4},{6,5},{7,6},{8,7},{9,8},{10,9},{11,1... | collective-permute-start | bytes 442376 | tf_op jit(solution)/shard_map/ppermute | solution.py:23
  74.8 0.0 copy-done
  74.9 0.0 copy-done.1
  74.9 4.8 %shard_map.46 = (bf16[288,512]{1,0:T(8,128)(2,1)S(1)}, f32[4,72,512]{2,1,0:T(8,128)S(1)}, bf16[4,144,1024]{2,1,0:T(8,128)(2,1)S(1)}) custom-call(bf16[288,512]{1,0:T(8,128)(2,1)S(1)} %reshape.23.own_w_ref, bf16[288,512]{1,0:T(8,128)(2,1)S(1)} %reshape.24.own_e_ref, bf16[288,512]{1,0:T(8,128)(2,1)S(1)} %collective-permute-done.west_ref, ...), custom_call_target="tpu_custom_call" | custom-call | flops 2500000000 | bytes 5343232 | tf_op jit(solution)/shard_map/pallas_call | solution.py:177
  79.7 0.0 collective-permute-done.2.north_ref
  79.7 0.0 collective-permute-done.3.south_ref
  79.7 0.0 copy-start.2
  79.7 0.7 copy-done.2
  80.3 0.0 collective-permute-done.4.far_north_ref
  80.3 0.0 collective-permute-done.5.far_south_ref
  80.3 0.9 %copy-done.3 = bf16[2,72,512]{2,1,0:T(8,128)(2,1)S(1)} copy-done((bf16[2,72,512]{2,1,0:T(8,128)(2,1)S(1)}, bf16[2,72,512]{2,1,0:T(8,128)(2,1)}, u32[]{:S(2)}) %copy-start.3) | copy-done | bytes 147480
  81.3 3.3 %shard_map.47 = bf16[2,288,512]{2,1,0:T(8,128)(2,1)S(1)} custom-call(f32[2]{0:T(128)S(1)} %add_select_fusion.closed_ref, f32[4,72,512]{2,1,0:T(8,128)S(1)} %get-tuple-element.8.query_ref, bf16[4,144,1024]{2,1,0:T(8,128)(2,1)S(1)} %get-tuple-element.9.keys_ref, bf16[2,72,512]{2,1,0:T(8,128)(2,1)S(1)} %collective-permute-done.2.north_ref, ...), custom_call_target="tpu_custom_call" | custom-call | flops 1000000000 | bytes 5933064 | tf_op jit(solution)/shard_map/pallas_call | solution.py:177
  84.6 0.1 reshape.26
  84.8 1.1 %copy.5 = bf16[12,2,6,4,512]{4,3,2,1,0:T(4,128)(2,1)} copy(bf16[12,2,6,4,512]{4,3,2,0,1:T(4,128)(2,1)S(1)} %bitcast.18) | data formatting | bytes 1179648 | tf_op jit(solution)/shard_map/transpose | solution.py:247
  (9 shorter events, 0.1 us)
Async XLA Ops:
  1.3 31.8 %collective-permute-start = (bf16[288,512]{1,0:T(8,128)(2,1)S(1)}, bf16[288,512]{1,0:T(8,128)(2,1)S(1)}, u32[]{:S(2)}, u32[]{:S(2)}) collective-permute-start(bf16[288,512]{1,0:T(8,128)(2,1)S(1)} %reshape.24.own_e_ref), channel_id=1, source_target_pairs={{0,16},{16,32},{32,48},{48,64},{64,80},{80,96},{96,112},{112,128},... | collective-permute-start | bytes 884744 | tf_op jit(solution)/shard_map/ppermute | solution.py:23
  17.7 57.2 %copy-start = (bf16[512,1536]{1,0:T(8,128)(2,1)S(1)}, bf16[512,1536]{1,0:T(8,128)(2,1)}, u32[]{:S(2)}) copy-start(bf16[512,1536]{1,0:T(8,128)(2,1)} %qkv_ref.3) | copy-start | bytes 4718596
  17.7 57.1 %copy-start.1 = (bf16[512,512]{1,0:T(8,128)(2,1)S(1)}, bf16[512,512]{1,0:T(8,128)(2,1)}, u32[]{:S(2)}) copy-start(bf16[512,512]{1,0:T(8,128)(2,1)} %out_w_ref.3) | copy-start | bytes 1572868
  17.7 57.1 %copy-start.4 = (f32[512]{0:T(512)S(1)}, f32[512]{0:T(512)}, u32[]{:S(2)}) copy-start(f32[512]{0:T(512)} %param.5) | copy-start | bytes 6148
  17.7 26.3 %collective-permute-start.1 = (bf16[288,512]{1,0:T(8,128)(2,1)S(1)}, bf16[288,512]{1,0:T(8,128)(2,1)}, u32[]{:S(2)}, u32[]{:S(2)}) collective-permute-start(bf16[288,512]{1,0:T(8,128)(2,1)S(1)} %reshape.23.own_w_ref), channel_id=1, source_target_pairs={{0,496},{16,0},{32,16},{48,32},{64,48},{80,64},{96,80},{112,96},{1... | collective-permute-start | bytes 884744 | tf_op jit(solution)/shard_map/ppermute | solution.py:23
  26.3 53.4 %collective-permute-start.2 = (bf16[2,72,512]{2,1,0:T(8,128)(2,1)}, bf16[2,72,512]{2,1,0:T(8,128)(2,1)S(1)}, u32[]{:S(2)}, u32[]{:S(2)}) collective-permute-start(bf16[2,72,512]{2,1,0:T(8,128)(2,1)} %pad_maximum_fusion), channel_id=1, source_target_pairs={{0,1},{1,2},{2,3},{3,4},{4,5},{5,6},{6,7},{7,8},{8,9},{9,10},{10,1... | collective-permute-start | bytes 442376 | tf_op jit(solution)/shard_map/ppermute | solution.py:23
  30.5 49.2 %collective-permute-start.3 = (bf16[2,72,512]{2,1,0:T(8,128)(2,1)}, bf16[2,72,512]{2,1,0:T(8,128)(2,1)S(1)}, u32[]{:S(2)}, u32[]{:S(2)}) collective-permute-start(bf16[2,72,512]{2,1,0:T(8,128)(2,1)} %pad_maximum_fusion.1), channel_id=1, source_target_pairs={{1,0},{2,1},{3,2},{4,3},{5,4},{6,5},{7,6},{8,7},{9,8},{10,9},{11,1... | collective-permute-start | bytes 442376 | tf_op jit(solution)/shard_map/ppermute | solution.py:23
  45.0 35.4 %collective-permute-start.4 = (bf16[2,72,512]{2,1,0:T(8,128)(2,1)S(1)}, bf16[2,72,512]{2,1,0:T(8,128)(2,1)S(1)}, u32[]{:S(2)}, u32[]{:S(2)}) collective-permute-start(bf16[2,72,512]{2,1,0:T(8,128)(2,1)S(1)} %pad_maximum_fusion.2), channel_id=1, source_target_pairs={{0,1},{1,2},{2,3},{3,4},{4,5},{5,6},{6,7},{7,8},{8,9},{9,10},{10,1... | collective-permute-start | bytes 442376 | tf_op jit(solution)/shard_map/ppermute | solution.py:23
  72.9 7.4 %collective-permute-start.5 = (bf16[2,72,512]{2,1,0:T(8,128)(2,1)S(1)}, bf16[2,72,512]{2,1,0:T(8,128)(2,1)S(1)}, u32[]{:S(2)}, u32[]{:S(2)}) collective-permute-start(bf16[2,72,512]{2,1,0:T(8,128)(2,1)S(1)} %pad_maximum_fusion.3), channel_id=1, source_target_pairs={{1,0},{2,1},{3,2},{4,3},{5,4},{6,5},{7,6},{8,7},{9,8},{10,9},{11,1... | collective-permute-start | bytes 442376 | tf_op jit(solution)/shard_map/ppermute | solution.py:23
  79.7 0.7 copy-start.2
  80.3 0.9 %copy-start.3 = (bf16[2,72,512]{2,1,0:T(8,128)(2,1)S(1)}, bf16[2,72,512]{2,1,0:T(8,128)(2,1)}, u32[]{:S(2)}) copy-start(bf16[2,72,512]{2,1,0:T(8,128)(2,1)} %copy-done.2) | copy-start | bytes 442372

commit v7 on v6

--- a/solution.py
+++ b/solution.py
@@ -39,7 +39,7 @@
 
 def level_bias(rows, keys):
     def part(axis):
-        level = lax.broadcasted_iota(jnp.int32, (rows, keys), axis) % LEVELS
+        level = lax.broadcasted_iota(jnp.int32, (rows, keys), axis) & (LEVELS - 1)
         return jnp.where(level == 0, 2, jnp.where(level == LEVELS - 1, 1, 0))
 
     return jnp.where(part(0) == part(1), 0.0, FAR).astype(jnp.float32)
@@ -47,7 +47,7 @@
 
 def attend(query, keys, values, bias):
     rows = query.shape[0]
-    owner = lax.broadcasted_iota(jnp.int32, (rows, SPAN), 1) // HEAD_SIZE
+    owner = lax.broadcasted_iota(jnp.int32, (rows, SPAN), 1) >> 6
     tall = jnp.concatenate([bias] * GROUP, axis=0)
     parts = []
     for start in range(0, query.shape[1], SPAN):
@@ -131,8 +131,6 @@
     keys_ref,
     north_ref,
     south_ref,
-    far_north_ref,
-    far_south_ref,
     own_w_ref,
     own_e_ref,
     middle_ref,
@@ -143,8 +141,7 @@
 ):
     rows, width = own_w_ref.shape
     count = rows - 2 * RIM
-    refs = ((north_ref, far_north_ref), (south_ref, far_south_ref))
-    beyond = [r[side].astype(jnp.float32) for pair in refs for side in range(2) for r in pair]
+    beyond = [r[part].astype(jnp.float32) for r in (north_ref, south_ref) for part in range(4)]
     beyond = make_keys(layer_norm(jnp.concatenate(beyond, axis=0), gain_ref[...]), qkv_ref).astype(jnp.bfloat16)
     levels = level_bias(RIM, 4 * RIM)
     distant = lax.broadcasted_iota(jnp.int32, (RIM, 4 * RIM), 1) >= 2 * RIM
@@ -161,14 +158,16 @@
     mixed = project(jnp.concatenate(tokens, axis=0), jnp.concatenate(heads, axis=0), out_w_ref).astype(jnp.float32)
     middle = middle_ref[...].astype(jnp.float32)
     for side in range(2):
-        out_ref[side] = jnp.concatenate(
+        half = jnp.concatenate(
             [
                 mixed[side * RIM : (side + 1) * RIM],
                 middle[side * count : (side + 1) * count],
                 mixed[(2 + side) * RIM : (3 + side) * RIM],
             ],
             axis=0,
-        ).astype(jnp.bfloat16)
+        )
+        half = half.reshape(rows // (HALF * LEVELS), HALF, LEVELS, width).astype(jnp.bfloat16)
+        out_ref[:, side * HALF : (side + 1) * HALF] = half
 
 
 def call(kernel, results, flops, *operands):
@@ -196,12 +195,9 @@
     def rim(*halves):
         return jnp.stack([h[:RIM] for h in halves]), jnp.stack([h[rows - RIM :] for h in halves])
 
-    first, last = rim(own_w, own_e)
+    first, last = rim(own_w, west, own_e, east)
     south = shift(first, "lat", -1, False)
     north = shift(last, "lat", 1, False)
-    first, last = rim(west, east)
-    far_south = shift(first, "lat", -1, False)
-    far_north = shift(last, "lat", 1, False)
     gain = gain_attn.reshape(1, width)
     place = lax.axis_index("lat")
     closed = jnp.stack([place == 0, place == lax.axis_size("lat") - 1])
@@ -228,15 +224,13 @@
     )
     (mixed,) = call(
         edge_kernel,
-        [shape(2, rows, width, dtype=jnp.bfloat16)],
+        [shape(row_count, col_count, lev_count, width, dtype=jnp.bfloat16)],
         1_000_000_000,
         closed,
         query,
         keys,
         north,
         south,
-        far_north,
-        far_south,
         own_w,
         own_e,
         middle,
@@ -244,8 +238,7 @@
         weight_qkv,
         weight_out,
     )
-    mixed = mixed.reshape(2, row_count, HALF, lev_count, width).transpose(1, 0, 2, 3, 4)
-    return mixed.reshape(row_count, col_count, lev_count, width).transpose(2, 0, 1, 3)
+    return mixed.transpose(2, 0, 1, 3)
 
 
 def solution(mesh):

time: 86.8 us -> 85.7 us (0.987)
  waiting for transfers between devices: 10.9 us -> 16.4 us
  starting transfers between devices: 58.8 us -> 53.8 us
    ppermute x6 -> x4, waiting for transfers between devices: 10.9 us -> 16.4 us  [shift(): return lax.ppermute(value, axis, pairs)]
    ppermute x6 -> x4, starting transfers between devices: 58.8 us -> 53.8 us  [shift(): return lax.ppermute(value, axis, pairs)]
    unnamed x10 -> x6, local copies, waits for them, and re-layouts: 1.58 us -> 0.02 us
    another operation x2, local copies, waits for them, and re-layouts: 0.05 us -> 1.56 us  [rim(): jnp.stack([h[rows - RIM:] for h in halves])]
    transpose x1 -> x0, local copies, waits for them, and re-layouts: 1.08 us -> none  [shards(): mixed.reshape(2, row_count, HALF, lev_count, width).transpose(1, 0, 2, 3, 4)]
  transfers between devices with their start and end apart: 6 -> 4, of which waited for: 1 -> 2; matrix products, arithmetic and copies ran while one was open for 4% -> 5% of each run, Pallas kernels for 6% -> 5%
where the time goes in v7:
time: 85.7 us; the launch traced here: 85.3 us
  starting transfers between devices  53.8 us (63%)
  waiting for transfers between devices  16.4 us (19%)
  Pallas kernels  8.23 us (10%)
  local copies, waits for them, and re-layouts  5.69 us (7%)
  other arithmetic  1.05 us (1%)
    ppermute x4, starting transfers between devices, shift(): return lax.ppermute(value, axis, pairs)  53.8 us
    ppermute x4, waiting for transfers between devices, shift(): return lax.ppermute(value, axis, pairs)  16.4 us
    pallas_call x2, Pallas kernels, call(): pl.pallas_call(kernel, out_shape=results, in_specs=specs, out_specs=[pl.B...  8.23 us
    slice x1, local copies, waits for them, and re-layouts, rim(): h[:RIM]  1.76 us
  transfers between devices with their start and end apart: 4, of which 2 were waited for; matrix products, arithmetic and copies ran while one was open for 5% of the time, Pallas kernels for 5%

profile of v7, /device:TPU:1, one launch (start us, length us, event | category | flops | bytes accessed | tf_op | source)
XLA Modules:
  0.0 85.3 jit_solution(451813722475778939)
XLA Ops:
  0.0 1.3 %fusion.1 = (bf16[12,6,4,512]{3,2,1,0:T(4,128)(2,1)S(1)}, bf16[12,6,4,512]{3,2,1,0:T(4,128)(2,1)S(1)}) fusion(bf16[12,12,4,512]{3,2,1,0:T(4,128)(2,1)} %bitcast.15), kind=kLoop, calls=%fused_computation.8 | loop fusion | bytes 1179648 | tf_op jit(solution)/shard_map/slice | solution.py:191
  1.3 0.1 reshape.18.own_e_ref
  1.3 16.3 %collective-permute-start = (bf16[288,512]{1,0:T(8,128)(2,1)S(1)}, bf16[288,512]{1,0:T(8,128)(2,1)S(1)}, u32[]{:S(2)}, u32[]{:S(2)}) collective-permute-start(bf16[288,512]{1,0:T(8,128)(2,1)S(1)} %reshape.18.own_e_ref), channel_id=1, source_target_pairs={{0,16},{16,32},{32,48},{48,64},{64,80},{80,96},{96,112},{112,128},... | collective-permute-start | bytes 884744 | tf_op jit(solution)/shard_map/ppermute | solution.py:23
  17.6 0.1 reshape.17.own_w_ref
  17.7 0.0 copy-start
  17.7 0.0 copy-start.1
  17.7 0.0 copy-start.2
  17.7 6.7 %collective-permute-start.1 = (bf16[288,512]{1,0:T(8,128)(2,1)S(1)}, bf16[288,512]{1,0:T(8,128)(2,1)S(1)}, u32[]{:S(2)}, u32[]{:S(2)}) collective-permute-start(bf16[288,512]{1,0:T(8,128)(2,1)S(1)} %reshape.17.own_w_ref), channel_id=1, source_target_pairs={{0,496},{16,0},{32,16},{48,32},{64,48},{80,64},{96,80},{112,96},{1... | collective-permute-start | bytes 884744 | tf_op jit(solution)/shard_map/ppermute | solution.py:23
  24.4 1.8 %fusion = (bf16[3,6,4,512]{3,2,1,0:T(4,128)(2,1)S(1)}, bf16[3,6,4,512]{3,2,1,0:T(4,128)(2,1)}, bf16[3,6,4,512]{3,2,1,0:T(4,128)(2,1)S(1)}, bf16[3,6,4,512]{3,2,1,0:T(4,128)(2,1)}) fusion(bf16[12,12,4,512]{3,2,1,0:T(4,128)(2,1)} %bitcast.16), kind=kLoop, calls=%fused_computation.7 | loop fusion | bytes 589824 | tf_op jit(solution)/shard_map/slice | solution.py:196
  26.2 0.9 %stack.42 = bf16[1,72,512]{2,1,0:T(8,128)(2,1)S(1)} reshape(bf16[3,6,4,512]{3,2,1,0:T(4,128)(2,1)} %get-tuple-element.14) | data formatting | bytes 147456 | tf_op jit(solution)/shard_map/stack | solution.py:196
  27.1 0.7 stack.44
  27.8 0.9 %stack.49 = bf16[1,72,512]{2,1,0:T(8,128)(2,1)S(1)} reshape(bf16[3,6,4,512]{3,2,1,0:T(4,128)(2,1)} %get-tuple-element.12) | data formatting | bytes 147456 | tf_op jit(solution)/shard_map/stack | solution.py:196
  28.7 0.0 collective-permute-done.west_ref
  28.7 14.2 %collective-permute-done.1.east_ref = bf16[288,512]{1,0:T(8,128)(2,1)S(1)} collective-permute-done((bf16[288,512]{1,0:T(8,128)(2,1)S(1)}, bf16[288,512]{1,0:T(8,128)(2,1)S(1)}, u32[]{:S(2)}, u32[]{:S(2)}) %collective-permute-start.1) | collective-permute-done | bytes 294944 | tf_op jit(solution)/shard_map/ppermute | solution.py:23
  42.9 0.9 %pad_maximum_fusion = bf16[4,72,512]{2,1,0:T(8,128)(2,1)S(1)} fusion(bf16[1,72,512]{2,1,0:T(8,128)(2,1)S(1)} %get-tuple-element.20, bf16[1,72,512]{2,1,0:T(8,128)(2,1)} %stack.44, bf16[1,72,512]{2,1,0:T(8,128)(2,1)S(1)} %get-tuple-element.18, bf16[1,72,512]{2,1,0:T(8,128)(2,1)S(1)} %stack.42), kind=kLoop, calls=%fused_computation | loop fusion | flops 442368 | bytes 589824 | tf_op jit(solution)/shard_map/stack | solution.py:196
  43.9 28.9 %collective-permute-start.2 = (bf16[4,72,512]{2,1,0:T(8,128)(2,1)S(1)}, bf16[4,72,512]{2,1,0:T(8,128)(2,1)S(1)}, u32[]{:S(2)}, u32[]{:S(2)}) collective-permute-start(bf16[4,72,512]{2,1,0:T(8,128)(2,1)S(1)} %pad_maximum_fusion), channel_id=1, source_target_pairs={{0,1},{1,2},{2,3},{3,4},{4,5},{5,6},{6,7},{7,8},{8,9},{9,10},{10,1... | collective-permute-start | bytes 884744 | tf_op jit(solution)/shard_map/ppermute | solution.py:23
  72.9 1.9 %collective-permute-start.3 = (bf16[4,72,512]{2,1,0:T(8,128)(2,1)S(1)}, bf16[4,72,512]{2,1,0:T(8,128)(2,1)S(1)}, u32[]{:S(2)}, u32[]{:S(2)}) collective-permute-start(bf16[4,72,512]{2,1,0:T(8,128)(2,1)S(1)} %pad_maximum_fusion.1), channel_id=1, source_target_pairs={{1,0},{2,1},{3,2},{4,3},{5,4},{6,5},{7,6},{8,7},{9,8},{10,9},{11,1... | collective-permute-start | bytes 884744 | tf_op jit(solution)/shard_map/ppermute | solution.py:23
  74.8 0.1 add_select_fusion.closed_ref
  74.9 0.0 copy-done
  74.9 0.0 copy-done.1
  74.9 0.0 copy-done.2
  74.9 3.8 %shard_map.46 = (bf16[288,512]{1,0:T(8,128)(2,1)S(1)}, f32[4,72,512]{2,1,0:T(8,128)S(1)}, bf16[4,144,1024]{2,1,0:T(8,128)(2,1)S(1)}) custom-call(bf16[288,512]{1,0:T(8,128)(2,1)S(1)} %reshape.17.own_w_ref, bf16[288,512]{1,0:T(8,128)(2,1)S(1)} %reshape.18.own_e_ref, bf16[288,512]{1,0:T(8,128)(2,1)S(1)} %collective-permute-done.west_ref, ...), custom_call_target="tpu_custom_call" | custom-call | flops 2500000000 | bytes 5343232 | tf_op jit(solution)/shard_map/pallas_call | solution.py:176
  78.7 0.0 collective-permute-done.2.north_ref
  78.7 2.2 %collective-permute-done.3.south_ref = bf16[4,72,512]{2,1,0:T(8,128)(2,1)S(1)} collective-permute-done((bf16[4,72,512]{2,1,0:T(8,128)(2,1)S(1)}, bf16[4,72,512]{2,1,0:T(8,128)(2,1)S(1)}, u32[]{:S(2)}, u32[]{:S(2)}) %collective-permute-start.3) | collective-permute-done | bytes 294944 | tf_op jit(solution)/shard_map/ppermute | solution.py:23
  80.9 4.4 %shard_map.47 = bf16[12,12,4,512]{3,2,1,0:T(4,128)(2,1)} custom-call(f32[2]{0:T(128)S(1)} %add_select_fusion.closed_ref, f32[4,72,512]{2,1,0:T(8,128)S(1)} %get-tuple-element.8.query_ref, bf16[4,144,1024]{2,1,0:T(8,128)(2,1)S(1)} %get-tuple-element.9.keys_ref, bf16[4,72,512]{2,1,0:T(8,128)(2,1)S(1)} %collective-permute-done.2.north_ref, ...), custom_call_target="tpu_custom_call" | custom-call | flops 1000000000 | bytes 5933064 | tf_op jit(solution)/shard_map/pallas_call | solution.py:176
  (4 shorter events, 0.1 us)
Async XLA Ops:
  1.3 27.4 %collective-permute-start = (bf16[288,512]{1,0:T(8,128)(2,1)S(1)}, bf16[288,512]{1,0:T(8,128)(2,1)S(1)}, u32[]{:S(2)}, u32[]{:S(2)}) collective-permute-start(bf16[288,512]{1,0:T(8,128)(2,1)S(1)} %reshape.18.own_e_ref), channel_id=1, source_target_pairs={{0,16},{16,32},{32,48},{48,64},{64,80},{80,96},{96,112},{112,128},... | collective-permute-start | bytes 884744 | tf_op jit(solution)/shard_map/ppermute | solution.py:23
  17.7 57.2 %copy-start = (bf16[512,1536]{1,0:T(8,128)(2,1)S(1)}, bf16[512,1536]{1,0:T(8,128)(2,1)}, u32[]{:S(2)}) copy-start(bf16[512,1536]{1,0:T(8,128)(2,1)} %qkv_ref.3) | copy-start | bytes 4718596
  17.7 57.2 %copy-start.1 = (bf16[512,512]{1,0:T(8,128)(2,1)S(1)}, bf16[512,512]{1,0:T(8,128)(2,1)}, u32[]{:S(2)}) copy-start(bf16[512,512]{1,0:T(8,128)(2,1)} %out_w_ref.3) | copy-start | bytes 1572868
  17.7 57.1 %copy-start.2 = (f32[512]{0:T(512)S(1)}, f32[512]{0:T(512)}, u32[]{:S(2)}) copy-start(f32[512]{0:T(512)} %param.5) | copy-start | bytes 6148
  17.7 25.2 %collective-permute-start.1 = (bf16[288,512]{1,0:T(8,128)(2,1)S(1)}, bf16[288,512]{1,0:T(8,128)(2,1)S(1)}, u32[]{:S(2)}, u32[]{:S(2)}) collective-permute-start(bf16[288,512]{1,0:T(8,128)(2,1)S(1)} %reshape.17.own_w_ref), channel_id=1, source_target_pairs={{0,496},{16,0},{32,16},{48,32},{64,48},{80,64},{96,80},{112,96},{1... | collective-permute-start | bytes 884744 | tf_op jit(solution)/shard_map/ppermute | solution.py:23
  43.9 34.9 %collective-permute-start.2 = (bf16[4,72,512]{2,1,0:T(8,128)(2,1)S(1)}, bf16[4,72,512]{2,1,0:T(8,128)(2,1)S(1)}, u32[]{:S(2)}, u32[]{:S(2)}) collective-permute-start(bf16[4,72,512]{2,1,0:T(8,128)(2,1)S(1)} %pad_maximum_fusion), channel_id=1, source_target_pairs={{0,1},{1,2},{2,3},{3,4},{4,5},{5,6},{6,7},{7,8},{8,9},{9,10},{10,1... | collective-permute-start | bytes 884744 | tf_op jit(solution)/shard_map/ppermute | solution.py:23
  72.9 8.0 %collective-permute-start.3 = (bf16[4,72,512]{2,1,0:T(8,128)(2,1)S(1)}, bf16[4,72,512]{2,1,0:T(8,128)(2,1)S(1)}, u32[]{:S(2)}, u32[]{:S(2)}) collective-permute-start(bf16[4,72,512]{2,1,0:T(8,128)(2,1)S(1)} %pad_maximum_fusion.1), channel_id=1, source_target_pairs={{1,0},{2,1},{3,2},{4,3},{5,4},{6,5},{7,6},{8,7},{9,8},{10,9},{11,1... | collective-permute-start | bytes 884744 | tf_op jit(solution)/shard_map/ppermute | solution.py:23

commit v8 on v7

--- a/solution.py
+++ b/solution.py
@@ -74,7 +74,7 @@
 
 def project(tokens, heads, weight_ref):
     branch = matmul(heads.astype(jnp.bfloat16), weight_ref[...])
-    return (tokens + rounded(branch)).astype(jnp.bfloat16)
+    return tokens + rounded(branch)
 
 
 def make_query(normed, qkv_ref):
@@ -122,13 +122,28 @@
         kv = jnp.concatenate([mine[at], halos[at]], axis=0).astype(jnp.bfloat16)
         heads.append(attend(query[at], kv[:, :width], kv[:, width:], bias))
         tokens.append(own[at])
-    out_ref[...] = project(jnp.concatenate(tokens, axis=0), jnp.concatenate(heads, axis=0), out_w_ref)
+    mixed = project(jnp.concatenate(tokens, axis=0), jnp.concatenate(heads, axis=0), out_w_ref)
+    for side in range(2):
+        place_half(out_ref, slice(None), side, mixed[side * count : (side + 1) * count])
+
+
+def place_half(out_ref, at, side, half):
+    half = half.reshape(-1, HALF, LEVELS, half.shape[-1]).astype(jnp.bfloat16)
+    out_ref[at, side * HALF : (side + 1) * HALF] = half
+
+
+def latitude_kernel(north_ref, south_ref, gain_ref, qkv_ref, keys_ref):
+    beyond = jnp.concatenate([r[s].astype(jnp.float32) for r in (north_ref, south_ref) for s in range(2)], axis=0)
+    beyond = make_keys(layer_norm(beyond, gain_ref[...]), qkv_ref)
+    for place in range(4):
+        keys_ref[place] = beyond[place * RIM : (place + 1) * RIM]
 
 
 def edge_kernel(
     closed_ref,
     query_ref,
     keys_ref,
+    beyond_ref,
     north_ref,
     south_ref,
     own_w_ref,
@@ -140,9 +155,8 @@
     out_ref,
 ):
     rows, width = own_w_ref.shape
-    count = rows - 2 * RIM
-    beyond = [r[part].astype(jnp.float32) for r in (north_ref, south_ref) for part in range(4)]
-    beyond = make_keys(layer_norm(jnp.concatenate(beyond, axis=0), gain_ref[...]), qkv_ref).astype(jnp.bfloat16)
+    corners = jnp.concatenate([r[s].astype(jnp.float32) for r in (north_ref, south_ref) for s in range(2)], axis=0)
+    corners = make_keys(layer_norm(corners, gain_ref[...]), qkv_ref)
     levels = level_bias(RIM, 4 * RIM)
     distant = lax.broadcasted_iota(jnp.int32, (RIM, 4 * RIM), 1) >= 2 * RIM
     own = [r[...].astype(jnp.float32) for r in (own_w_ref, own_e_ref)]
@@ -152,22 +166,17 @@
         for side in range(2):
             place = edge * 2 + side
             begin = edge * (rows - RIM)
-            kv = jnp.concatenate([keys_ref[place], beyond[2 * place * RIM : 2 * (place + 1) * RIM]], axis=0)
+            outer = jnp.concatenate([beyond_ref[place], corners[place * RIM : (place + 1) * RIM]], axis=0)
+            kv = jnp.concatenate([keys_ref[place], outer.astype(jnp.bfloat16)], axis=0)
             heads.append(attend(query_ref[place], kv[:, :width], kv[:, width:], bias))
             tokens.append(own[side][begin : begin + RIM])
-    mixed = project(jnp.concatenate(tokens, axis=0), jnp.concatenate(heads, axis=0), out_w_ref).astype(jnp.float32)
-    middle = middle_ref[...].astype(jnp.float32)
-    for side in range(2):
-        half = jnp.concatenate(
-            [
-                mixed[side * RIM : (side + 1) * RIM],
-                middle[side * count : (side + 1) * count],
-                mixed[(2 + side) * RIM : (3 + side) * RIM],
-            ],
-            axis=0,
-        )
-        half = half.reshape(rows // (HALF * LEVELS), HALF, LEVELS, width).astype(jnp.bfloat16)
-        out_ref[:, side * HALF : (side + 1) * HALF] = half
+    mixed = project(jnp.concatenate(tokens, axis=0), jnp.concatenate(heads, axis=0), out_w_ref)
+    out_ref[EDGE : out_ref.shape[0] - EDGE] = middle_ref[...]
+    for edge in range(2):
+        at = slice(0, EDGE) if edge == 0 else slice(out_ref.shape[0] - EDGE, out_ref.shape[0])
+        for side in range(2):
+            place = edge * 2 + side
+            place_half(out_ref, at, side, mixed[place * RIM : (place + 1) * RIM])
 
 
 def call(kernel, results, flops, *operands):
@@ -195,9 +204,12 @@
     def rim(*halves):
         return jnp.stack([h[:RIM] for h in halves]), jnp.stack([h[rows - RIM :] for h in halves])
 
-    first, last = rim(own_w, west, own_e, east)
+    first, last = rim(own_w, own_e)
     south = shift(first, "lat", -1, False)
     north = shift(last, "lat", 1, False)
+    first, last = rim(west, east)
+    far_south = shift(first, "lat", -1, False)
+    far_north = shift(last, "lat", 1, False)
     gain = gain_attn.reshape(1, width)
     place = lax.axis_index("lat")
     closed = jnp.stack([place == 0, place == lax.axis_size("lat") - 1])
@@ -209,7 +221,7 @@
     middle, query, keys = call(
         inner_kernel,
         [
-            shape(2 * (rows - 2 * RIM), width, dtype=jnp.bfloat16),
+            shape(row_count - 2 * EDGE, col_count, lev_count, width, dtype=jnp.bfloat16),
             shape(4, RIM, width),
             shape(4, 2 * RIM, 2 * width, dtype=jnp.bfloat16),
         ],
@@ -222,6 +234,7 @@
         weight_qkv,
         weight_out,
     )
+    (beyond,) = call(latitude_kernel, [shape(4, RIM, 2 * width)], 300_000_000, north, south, gain, weight_qkv)
     (mixed,) = call(
         edge_kernel,
         [shape(row_count, col_count, lev_count, width, dtype=jnp.bfloat16)],
@@ -229,8 +242,9 @@
         closed,
         query,
         keys,
-        north,
-        south,
+        beyond,
+        far_north,
+        far_south,
         own_w,
         own_e,
         middle,

time: 85.7 us -> 87.3 us (1.019)
  waiting for transfers between devices: 16.4 us -> 43.5 us
  starting transfers between devices: 53.8 us -> 33 us
  local copies, waits for them, and re-layouts: 5.69 us -> 1.71 us
  other arithmetic: 1.05 us -> 0.15 us
    ppermute x4 -> x6, waiting for transfers between devices: 16.4 us -> 43.5 us  [shift(): return lax.ppermute(value, axis, pairs)]
    ppermute x4 -> x6, starting transfers between devices: 53.8 us -> 33 us  [shift(): return lax.ppermute(value, axis, pairs)]
    slice x1, local copies, waits for them, and re-layouts: 1.76 us -> 0.1 us  [rim(): h[:RIM]]
    another operation x2, local copies, waits for them, and re-layouts: 1.56 us -> 0.05 us  [rim(): jnp.stack([h[rows - RIM:] for h in halves])]
    another operation x1 -> x2, other arithmetic: 0.93 us -> 0.04 us  [rim(): jnp.stack([h[rows - RIM:] for h in halves])]
    another operation x4, local copies, waits for them, and re-layouts: 0.95 us -> 0.07 us  [rim(): jnp.stack([h[:RIM] for h in halves])]
    pallas_call x2 -> x3, Pallas kernels: 8.23 us -> 8.45 us  [call(): pl.pallas_call(kernel, out_shape=results, in_specs=specs, out_specs=[pl.B...]
  transfers between devices with their start and end apart: 4 -> 6, of which waited for: 2 -> 3; matrix products, arithmetic and copies ran while one was open for 5% -> 0% of each run, Pallas kernels for 5% -> 5%
where the time goes in v8:
time: 87.3 us; the launch traced here: 87.1 us
  waiting for transfers between devices  43.5 us (50%)
  starting transfers between devices  33 us (38%)
  Pallas kernels  8.45 us (10%)
  local copies, waits for them, and re-layouts  1.71 us (2%)
    ppermute x6, waiting for transfers between devices, shift(): return lax.ppermute(value, axis, pairs)  43.5 us
    ppermute x6, starting transfers between devices, shift(): return lax.ppermute(value, axis, pairs)  33 us
    pallas_call x3, Pallas kernels, call(): pl.pallas_call(kernel, out_shape=results, in_specs=specs, out_specs=[pl.B...  8.45 us
  transfers between devices with their start and end apart: 6, of which 3 were waited for; matrix products, arithmetic and copies ran while one was open for 0% of the time, Pallas kernels for 5%

profile of v8, /device:TPU:1, one launch (start us, length us, event | category | flops | bytes accessed | tf_op | source)
XLA Modules:
  0.0 87.1 jit_solution(7360475128683873492)
XLA Ops:
  0.0 0.0 copy-start.3
  0.0 1.3 %fusion.1 = (bf16[12,6,4,512]{3,2,1,0:T(4,128)(2,1)S(1)}, bf16[12,6,4,512]{3,2,1,0:T(4,128)(2,1)S(1)}) fusion(bf16[12,12,4,512]{3,2,1,0:T(4,128)(2,1)} %bitcast.16), kind=kLoop, calls=%fused_computation.10 | loop fusion | bytes 1179648 | tf_op jit(solution)/shard_map/slice | solution.py:200
  1.3 0.1 reshape.18.own_e_ref
  1.4 0.0 copy-start
  1.4 0.0 copy-start.2
  1.4 16.4 %collective-permute-start = (bf16[288,512]{1,0:T(8,128)(2,1)S(1)}, bf16[288,512]{1,0:T(8,128)(2,1)S(1)}, u32[]{:S(2)}, u32[]{:S(2)}) collective-permute-start(bf16[288,512]{1,0:T(8,128)(2,1)S(1)} %reshape.18.own_e_ref), channel_id=1, source_target_pairs={{0,16},{16,32},{32,48},{48,64},{64,80},{80,96},{96,112},{112,128},... | collective-permute-start | bytes 884744 | tf_op jit(solution)/shard_map/ppermute | solution.py:23
  17.8 0.0 copy-done.3
  17.8 0.1 fusion
  18.0 3.5 %collective-permute-start.2 = (bf16[2,72,512]{2,1,0:T(8,128)(2,1)S(1)}, bf16[2,72,512]{2,1,0:T(8,128)(2,1)S(1)}, u32[]{:S(2)}, u32[]{:S(2)}) collective-permute-start(bf16[2,72,512]{2,1,0:T(8,128)(2,1)S(1)} %pad_maximum_fusion), channel_id=1, source_target_pairs={{0,1},{1,2},{2,3},{3,4},{4,5},{5,6},{6,7},{7,8},{8,9},{9,10},{10,1... | collective-permute-start | bytes 442376 | tf_op jit(solution)/shard_map/ppermute | solution.py:23
  21.6 1.9 %collective-permute-start.3 = (bf16[2,72,512]{2,1,0:T(8,128)(2,1)S(1)}, bf16[2,72,512]{2,1,0:T(8,128)(2,1)S(1)}, u32[]{:S(2)}, u32[]{:S(2)}) collective-permute-start(bf16[2,72,512]{2,1,0:T(8,128)(2,1)S(1)} %pad_maximum_fusion.1), channel_id=1, source_target_pairs={{1,0},{2,1},{3,2},{4,3},{5,4},{6,5},{7,6},{8,7},{9,8},{10,9},{11,1... | collective-permute-start | bytes 442376 | tf_op jit(solution)/shard_map/ppermute | solution.py:23
  23.5 0.1 reshape.17.own_w_ref
  23.6 6.9 %collective-permute-start.1 = (bf16[288,512]{1,0:T(8,128)(2,1)S(1)}, bf16[288,512]{1,0:T(8,128)(2,1)S(1)}, u32[]{:S(2)}, u32[]{:S(2)}) collective-permute-start(bf16[288,512]{1,0:T(8,128)(2,1)S(1)} %reshape.17.own_w_ref), channel_id=1, source_target_pairs={{0,496},{16,0},{32,16},{48,32},{64,48},{80,64},{96,80},{112,96},{1... | collective-permute-start | bytes 884744 | tf_op jit(solution)/shard_map/ppermute | solution.py:23
  30.5 0.1 add_select_fusion.closed_ref
  30.6 24.6 %collective-permute-done.2.north_ref = bf16[2,72,512]{2,1,0:T(8,128)(2,1)S(1)} collective-permute-done((bf16[2,72,512]{2,1,0:T(8,128)(2,1)S(1)}, bf16[2,72,512]{2,1,0:T(8,128)(2,1)S(1)}, u32[]{:S(2)}, u32[]{:S(2)}) %collective-permute-start.2) | collective-permute-done | bytes 147488 | tf_op jit(solution)/shard_map/ppermute | solution.py:23
  55.2 0.0 collective-permute-done.3.south_ref
  55.2 0.0 copy-done
  55.2 0.0 copy-done.2
  55.2 0.7 shard_map.47.beyond_ref
  55.9 0.0 copy-start.1
  55.9 0.0 collective-permute-done.west_ref
  55.9 18.8 %collective-permute-done.1.east_ref = bf16[288,512]{1,0:T(8,128)(2,1)S(1)} collective-permute-done((bf16[288,512]{1,0:T(8,128)(2,1)S(1)}, bf16[288,512]{1,0:T(8,128)(2,1)S(1)}, u32[]{:S(2)}, u32[]{:S(2)}) %collective-permute-start.1) | collective-permute-done | bytes 294944 | tf_op jit(solution)/shard_map/ppermute | solution.py:23
  74.7 1.9 %collective-permute-start.4 = (bf16[2,72,512]{2,1,0:T(8,128)(2,1)S(1)}, bf16[2,72,512]{2,1,0:T(8,128)(2,1)S(1)}, u32[]{:S(2)}, u32[]{:S(2)}) collective-permute-start(bf16[2,72,512]{2,1,0:T(8,128)(2,1)S(1)} %pad_maximum_fusion.2), channel_id=1, source_target_pairs={{0,1},{1,2},{2,3},{3,4},{4,5},{5,6},{6,7},{7,8},{8,9},{9,10},{10,1... | collective-permute-start | bytes 442376 | tf_op jit(solution)/shard_map/ppermute | solution.py:23
  76.7 2.4 %collective-permute-start.5 = (bf16[2,72,512]{2,1,0:T(8,128)(2,1)S(1)}, bf16[2,72,512]{2,1,0:T(8,128)(2,1)S(1)}, u32[]{:S(2)}, u32[]{:S(2)}) collective-permute-start(bf16[2,72,512]{2,1,0:T(8,128)(2,1)S(1)} %pad_maximum_fusion.3), channel_id=1, source_target_pairs={{1,0},{2,1},{3,2},{4,3},{5,4},{6,5},{7,6},{8,7},{9,8},{10,9},{11,1... | collective-permute-start | bytes 442376 | tf_op jit(solution)/shard_map/ppermute | solution.py:23
  79.1 0.0 copy-done.1
  79.1 3.9 %shard_map.46 = (bf16[6,12,4,512]{3,2,1,0:T(4,128)(2,1)S(1)}, f32[4,72,512]{2,1,0:T(8,128)S(1)}, bf16[4,144,1024]{2,1,0:T(8,128)(2,1)S(1)}) custom-call(bf16[288,512]{1,0:T(8,128)(2,1)S(1)} %reshape.17.own_w_ref, bf16[288,512]{1,0:T(8,128)(2,1)S(1)} %reshape.18.own_e_ref, bf16[288,512]{1,0:T(8,128)(2,1)S(1)} %collective-permute-done.west_ref, ...), custom_call_target="tpu_custom_call" | custom-call | flops 2500000000 | bytes 5343232 | tf_op jit(solution)/shard_map/pallas_call | solution.py:185
  83.0 0.0 collective-permute-done.4.north_ref
  83.0 0.1 collective-permute-done.5.south_ref
  83.1 3.9 %shard_map.48 = bf16[12,12,4,512]{3,2,1,0:T(4,128)(2,1)} custom-call(f32[2]{0:T(128)S(1)} %add_select_fusion.closed_ref, f32[4,72,512]{2,1,0:T(8,128)S(1)} %get-tuple-element.8.query_ref, bf16[4,144,1024]{2,1,0:T(8,128)(2,1)S(1)} %get-tuple-element.9.keys_ref, f32[4,72,1024]{2,1,0:T(8,128)S(1)} %shard_map.47.beyond_ref, ...), custom_call_target="tpu_custom_call" | custom-call | flops 1000000000 | bytes 6817800 | tf_op jit(solution)/shard_map/pallas_call | solution.py:185
  (10 shorter events, 0.2 us)
Async XLA Ops:
  0.0 17.8 %copy-start.3 = (bf16[4,12,12,512]{3,0,2,1:T(4,128)(2,1)S(1)}, bf16[4,12,12,512]{3,0,2,1:T(4,128)(2,1)}, u32[]{:S(2)}) copy-start(bf16[4,12,12,512]{3,0,2,1:T(4,128)(2,1)} %param.4) | copy-start | bytes 1769476
  1.4 53.8 %copy-start = (bf16[512,1536]{1,0:T(8,128)(2,1)S(1)}, bf16[512,1536]{1,0:T(8,128)(2,1)}, u32[]{:S(2)}) copy-start(bf16[512,1536]{1,0:T(8,128)(2,1)} %qkv_ref.5) | copy-start | bytes 4718596
  1.4 53.8 %copy-start.2 = (f32[512]{0:T(512)S(1)}, f32[512]{0:T(512)}, u32[]{:S(2)}) copy-start(f32[512]{0:T(512)} %param.5) | copy-start | bytes 6148
  1.4 54.5 %collective-permute-start = (bf16[288,512]{1,0:T(8,128)(2,1)S(1)}, bf16[288,512]{1,0:T(8,128)(2,1)S(1)}, u32[]{:S(2)}, u32[]{:S(2)}) collective-permute-start(bf16[288,512]{1,0:T(8,128)(2,1)S(1)} %reshape.18.own_e_ref), channel_id=1, source_target_pairs={{0,16},{16,32},{32,48},{48,64},{64,80},{80,96},{96,112},{112,128},... | collective-permute-start | bytes 884744 | tf_op jit(solution)/shard_map/ppermute | solution.py:23
  18.0 37.2 %collective-permute-start.2 = (bf16[2,72,512]{2,1,0:T(8,128)(2,1)S(1)}, bf16[2,72,512]{2,1,0:T(8,128)(2,1)S(1)}, u32[]{:S(2)}, u32[]{:S(2)}) collective-permute-start(bf16[2,72,512]{2,1,0:T(8,128)(2,1)S(1)} %pad_maximum_fusion), channel_id=1, source_target_pairs={{0,1},{1,2},{2,3},{3,4},{4,5},{5,6},{6,7},{7,8},{8,9},{9,10},{10,1... | collective-permute-start | bytes 442376 | tf_op jit(solution)/shard_map/ppermute | solution.py:23
  21.6 33.6 %collective-permute-start.3 = (bf16[2,72,512]{2,1,0:T(8,128)(2,1)S(1)}, bf16[2,72,512]{2,1,0:T(8,128)(2,1)S(1)}, u32[]{:S(2)}, u32[]{:S(2)}) collective-permute-start(bf16[2,72,512]{2,1,0:T(8,128)(2,1)S(1)} %pad_maximum_fusion.1), channel_id=1, source_target_pairs={{1,0},{2,1},{3,2},{4,3},{5,4},{6,5},{7,6},{8,7},{9,8},{10,9},{11,1... | collective-permute-start | bytes 442376 | tf_op jit(solution)/shard_map/ppermute | solution.py:23
  23.6 51.1 %collective-permute-start.1 = (bf16[288,512]{1,0:T(8,128)(2,1)S(1)}, bf16[288,512]{1,0:T(8,128)(2,1)S(1)}, u32[]{:S(2)}, u32[]{:S(2)}) collective-permute-start(bf16[288,512]{1,0:T(8,128)(2,1)S(1)} %reshape.17.own_w_ref), channel_id=1, source_target_pairs={{0,496},{16,0},{32,16},{48,32},{64,48},{80,64},{96,80},{112,96},{1... | collective-permute-start | bytes 884744 | tf_op jit(solution)/shard_map/ppermute | solution.py:23
  55.9 23.2 %copy-start.1 = (bf16[512,512]{1,0:T(8,128)(2,1)S(1)}, bf16[512,512]{1,0:T(8,128)(2,1)}, u32[]{:S(2)}) copy-start(bf16[512,512]{1,0:T(8,128)(2,1)} %out_w_ref.3) | copy-start | bytes 1572868
  74.7 8.3 %collective-permute-start.4 = (bf16[2,72,512]{2,1,0:T(8,128)(2,1)S(1)}, bf16[2,72,512]{2,1,0:T(8,128)(2,1)S(1)}, u32[]{:S(2)}, u32[]{:S(2)}) collective-permute-start(bf16[2,72,512]{2,1,0:T(8,128)(2,1)S(1)} %pad_maximum_fusion.2), channel_id=1, source_target_pairs={{0,1},{1,2},{2,3},{3,4},{4,5},{5,6},{6,7},{7,8},{8,9},{9,10},{10,1... | collective-permute-start | bytes 442376 | tf_op jit(solution)/shard_map/ppermute | solution.py:23
  76.7 6.5 %collective-permute-start.5 = (bf16[2,72,512]{2,1,0:T(8,128)(2,1)S(1)}, bf16[2,72,512]{2,1,0:T(8,128)(2,1)S(1)}, u32[]{:S(2)}, u32[]{:S(2)}) collective-permute-start(bf16[2,72,512]{2,1,0:T(8,128)(2,1)S(1)} %pad_maximum_fusion.3), channel_id=1, source_target_pairs={{1,0},{2,1},{3,2},{4,3},{5,4},{6,5},{7,6},{8,7},{9,8},{10,9},{11,1... | collective-permute-start | bytes 442376 | tf_op jit(solution)/shard_map/ppermute | solution.py:23

commit v9 on v8

--- a/solution.py
+++ b/solution.py
@@ -45,35 +45,49 @@
     return jnp.where(part(0) == part(1), 0.0, FAR).astype(jnp.float32)
 
 
-def attend(query, keys, values, bias):
-    rows = query.shape[0]
+def attend(query, kv, bias):
+    rows, width = query.shape
     owner = lax.broadcasted_iota(jnp.int32, (rows, SPAN), 1) >> 6
     tall = jnp.concatenate([bias] * GROUP, axis=0)
+
+    def merge(values):
+        merged = jnp.broadcast_to(values[:rows], (rows, SPAN))
+        for h in range(1, GROUP):
+            merged = jnp.where(owner == h, values[h * rows : (h + 1) * rows], merged)
+        return merged
+
     parts = []
-    for start in range(0, query.shape[1], SPAN):
+    for start in range(0, width, SPAN):
         piece = query[:, start : start + SPAN]
         spread = jnp.concatenate(
             [jnp.where(owner == h, piece, 0.0) for h in range(GROUP)], axis=0
         ).astype(jnp.bfloat16)
         scores = lax.dot_general(
             spread,
-            keys[:, start : start + SPAN],
+            kv[:, start : start + SPAN],
             (((1,), (1,)), ((), ())),
             preferred_element_type=jnp.float32,
         )
         scores = scores + tall
-        expo = jnp.exp(scores - jnp.max(scores, axis=-1, keepdims=True))
-        scale = 1.0 / jnp.sum(expo, axis=-1, keepdims=True)
-        out = matmul(expo.astype(jnp.bfloat16), values[:, start : start + SPAN]) * scale
-        merged = out[:rows]
-        for h in range(1, GROUP):
-            merged = jnp.where(owner == h, out[h * rows : (h + 1) * rows], merged)
-        parts.append(merged)
-    return jnp.concatenate(parts, axis=1)
-
-
-def project(tokens, heads, weight_ref):
-    branch = matmul(heads.astype(jnp.bfloat16), weight_ref[...])
+        top = jnp.max(scores, axis=-1, keepdims=True)
+        expo = jnp.exp(scores - top)
+        total = jnp.sum(expo, axis=-1, keepdims=True)
+        out = matmul(expo.astype(jnp.bfloat16), kv[:, width + start : width + start + SPAN])
+        parts.append((merge(out), merge(top), merge(total)))
+    return tuple(jnp.concatenate(p, axis=1) for p in zip(*parts))
+
+
+def add_keys(state, more):
+    out, top, total = state
+    out_2, top_2, total_2 = more
+    peak = jnp.maximum(top, top_2)
+    old, new = jnp.exp(top - peak), jnp.exp(top_2 - peak)
+    return out * old + out_2 * new, peak, total * old + total_2 * new
+
+
+def project(tokens, states, weight_ref):
+    heads = [out * (1.0 / total) for out, _, total in states]
+    branch = matmul(jnp.concatenate(heads, axis=0).astype(jnp.bfloat16), weight_ref[...])
     return tokens + rounded(branch)
 
 
@@ -97,7 +111,7 @@
     out_w_ref,
     out_ref,
     query_ref,
-    keys_ref,
+    state_ref,
 ):
     rows, width = own_w_ref.shape
     count = rows - 2 * RIM
@@ -105,24 +119,27 @@
     own = jnp.concatenate([r[...].astype(jnp.float32) for r in (own_w_ref, own_e_ref)], axis=0)
     normed = layer_norm(own, gain)
     query = make_query(normed, qkv_ref)
-    mine = make_keys(normed, qkv_ref)
     halos = jnp.concatenate([r[...].astype(jnp.float32) for r in (west_ref, east_ref)], axis=0)
-    halos = make_keys(layer_norm(halos, gain), qkv_ref)
+    kv = make_keys(jnp.concatenate([normed, layer_norm(halos, gain)], axis=0), qkv_ref)
+    mine, halos = kv[: 2 * rows], kv[2 * rows :]
+    rim = level_bias(RIM, 2 * RIM)
     for edge in range(2):
         for side in range(2):
             place = edge * 2 + side
             begin = side * rows + edge * (rows - RIM)
             at = slice(begin, begin + RIM)
             query_ref[place] = query[at]
-            keys_ref[place] = jnp.concatenate([mine[at], halos[at]], axis=0).astype(jnp.bfloat16)
+            both = jnp.concatenate([mine[at], halos[at]], axis=0).astype(jnp.bfloat16)
+            for i, value in enumerate(attend(query[at], both, rim)):
+                state_ref[i, place] = value
     bias = level_bias(count, 2 * count)
-    heads, tokens = [], []
+    states, tokens = [], []
     for side in range(2):
         at = slice(side * rows + RIM, (side + 1) * rows - RIM)
-        kv = jnp.concatenate([mine[at], halos[at]], axis=0).astype(jnp.bfloat16)
-        heads.append(attend(query[at], kv[:, :width], kv[:, width:], bias))
+        both = jnp.concatenate([mine[at], halos[at]], axis=0).astype(jnp.bfloat16)
+        states.append(attend(query[at], both, bias))
         tokens.append(own[at])
-    mixed = project(jnp.concatenate(tokens, axis=0), jnp.concatenate(heads, axis=0), out_w_ref)
+    mixed = project(jnp.concatenate(tokens, axis=0), states, out_w_ref)
     for side in range(2):
         place_half(out_ref, slice(None), side, mixed[side * count : (side + 1) * count])
 
@@ -132,18 +149,10 @@
     out_ref[at, side * HALF : (side + 1) * HALF] = half
 
 
-def latitude_kernel(north_ref, south_ref, gain_ref, qkv_ref, keys_ref):
-    beyond = jnp.concatenate([r[s].astype(jnp.float32) for r in (north_ref, south_ref) for s in range(2)], axis=0)
-    beyond = make_keys(layer_norm(beyond, gain_ref[...]), qkv_ref)
-    for place in range(4):
-        keys_ref[place] = beyond[place * RIM : (place + 1) * RIM]
-
-
 def edge_kernel(
     closed_ref,
     query_ref,
-    keys_ref,
-    beyond_ref,
+    state_ref,
     north_ref,
     south_ref,
     own_w_ref,
@@ -155,22 +164,20 @@
     out_ref,
 ):
     rows, width = own_w_ref.shape
-    corners = jnp.concatenate([r[s].astype(jnp.float32) for r in (north_ref, south_ref) for s in range(2)], axis=0)
-    corners = make_keys(layer_norm(corners, gain_ref[...]), qkv_ref)
-    levels = level_bias(RIM, 4 * RIM)
-    distant = lax.broadcasted_iota(jnp.int32, (RIM, 4 * RIM), 1) >= 2 * RIM
+    beyond = [r[part].astype(jnp.float32) for r in (north_ref, south_ref) for part in range(4)]
+    beyond = make_keys(layer_norm(jnp.concatenate(beyond, axis=0), gain_ref[...]), qkv_ref).astype(jnp.bfloat16)
+    levels = level_bias(RIM, 2 * RIM)
     own = [r[...].astype(jnp.float32) for r in (own_w_ref, own_e_ref)]
-    heads, tokens = [], []
+    states, tokens = [], []
     for edge in range(2):
-        bias = levels + jnp.where(distant, closed_ref[edge], 0.0)
+        bias = levels + closed_ref[edge]
         for side in range(2):
             place = edge * 2 + side
             begin = edge * (rows - RIM)
-            outer = jnp.concatenate([beyond_ref[place], corners[place * RIM : (place + 1) * RIM]], axis=0)
-            kv = jnp.concatenate([keys_ref[place], outer.astype(jnp.bfloat16)], axis=0)
-            heads.append(attend(query_ref[place], kv[:, :width], kv[:, width:], bias))
+            more = attend(query_ref[place], beyond[2 * place * RIM : 2 * (place + 1) * RIM], bias)
+            states.append(add_keys(tuple(state_ref[i, place] for i in range(3)), more))
             tokens.append(own[side][begin : begin + RIM])
-    mixed = project(jnp.concatenate(tokens, axis=0), jnp.concatenate(heads, axis=0), out_w_ref)
+    mixed = project(jnp.concatenate(tokens, axis=0), states, out_w_ref)
     out_ref[EDGE : out_ref.shape[0] - EDGE] = middle_ref[...]
     for edge in range(2):
         at = slice(0, EDGE) if edge == 0 else slice(out_ref.shape[0] - EDGE, out_ref.shape[0])
@@ -204,12 +211,9 @@
     def rim(*halves):
         return jnp.stack([h[:RIM] for h in halves]), jnp.stack([h[rows - RIM :] for h in halves])
 
-    first, last = rim(own_w, own_e)
+    first, last = rim(own_w, west, own_e, east)
     south = shift(first, "lat", -1, False)
     north = shift(last, "lat", 1, False)
-    first, last = rim(west, east)
-    far_south = shift(first, "lat", -1, False)
-    far_north = shift(last, "lat", 1, False)
     gain = gain_attn.reshape(1, width)
     place = lax.axis_index("lat")
     closed = jnp.stack([place == 0, place == lax.axis_size("lat") - 1])
@@ -218,12 +222,12 @@
     def shape(*dims, dtype=jnp.float32):
         return jax.ShapeDtypeStruct(dims, dtype)
 
-    middle, query, keys = call(
+    middle, query, state = call(
         inner_kernel,
         [
             shape(row_count - 2 * EDGE, col_count, lev_count, width, dtype=jnp.bfloat16),
             shape(4, RIM, width),
-            shape(4, 2 * RIM, 2 * width, dtype=jnp.bfloat16),
+            shape(3, 4, RIM, width),
         ],
         2_500_000_000,
         own_w,
@@ -234,17 +238,15 @@
         weight_qkv,
         weight_out,
     )
-    (beyond,) = call(latitude_kernel, [shape(4, RIM, 2 * width)], 300_000_000, north, south, gain, weight_qkv)
     (mixed,) = call(
         edge_kernel,
         [shape(row_count, col_count, lev_count, width, dtype=jnp.bfloat16)],
         1_000_000_000,
         closed,
         query,
-        keys,
-        beyond,
-        far_north,
-        far_south,
+        state,
+        north,
+        south,
         own_w,
         own_e,
         middle,

time: 87.3 us -> 85.5 us (0.979)
  waiting for transfers between devices: 43.5 us -> 15.2 us
  starting transfers between devices: 33 us -> 53.8 us
  local copies, waits for them, and re-layouts: 1.71 us -> 5.69 us
  other arithmetic: 0.15 us -> 1.05 us
    ppermute x6 -> x4, waiting for transfers between devices: 43.5 us -> 15.2 us  [shift(): return lax.ppermute(value, axis, pairs)]
    ppermute x6 -> x4, starting transfers between devices: 33 us -> 53.8 us  [shift(): return lax.ppermute(value, axis, pairs)]
    slice x1, local copies, waits for them, and re-layouts: 0.1 us -> 1.76 us  [rim(): h[:RIM]]
    another operation x2, local copies, waits for them, and re-layouts: 0.05 us -> 1.56 us  [rim(): jnp.stack([h[rows - RIM:] for h in halves])]
    another operation x2 -> x1, other arithmetic: 0.04 us -> 0.93 us  [rim(): jnp.stack([h[rows - RIM:] for h in halves])]
    another operation x4, local copies, waits for them, and re-layouts: 0.07 us -> 0.95 us  [rim(): jnp.stack([h[:RIM] for h in halves])]
    pallas_call x3 -> x2, Pallas kernels: 8.45 us -> 9.22 us  [call(): pl.pallas_call(kernel, out_shape=results, in_specs=specs, out_specs=[pl.B...]
  transfers between devices with their start and end apart: 6 -> 4, of which waited for: 3 -> 2; matrix products, arithmetic and copies ran while one was open for 0% -> 5% of each run, Pallas kernels for 5% -> 6%
where the time goes in v9:
time: 85.5 us; the launch traced here: 85.1 us
  starting transfers between devices  53.8 us (63%)
  waiting for transfers between devices  15.2 us (18%)
  Pallas kernels  9.22 us (11%)
  local copies, waits for them, and re-layouts  5.69 us (7%)
  other arithmetic  1.05 us (1%)
    ppermute x4, starting transfers between devices, shift(): return lax.ppermute(value, axis, pairs)  53.8 us
    ppermute x4, waiting for transfers between devices, shift(): return lax.ppermute(value, axis, pairs)  15.2 us
    pallas_call x2, Pallas kernels, call(): pl.pallas_call(kernel, out_shape=results, in_specs=specs, out_specs=[pl.B...  9.22 us
    slice x1, local copies, waits for them, and re-layouts, rim(): h[:RIM]  1.76 us
  transfers between devices with their start and end apart: 4, of which 2 were waited for; matrix products, arithmetic and copies ran while one was open for 5% of the time, Pallas kernels for 6%

profile of v9, /device:TPU:1, one launch (start us, length us, event | category | flops | bytes accessed | tf_op | source)
XLA Modules:
  0.0 85.1 jit_solution(2122945670414399704)
XLA Ops:
  0.0 1.3 %fusion.1 = (bf16[12,6,4,512]{3,2,1,0:T(4,128)(2,1)S(1)}, bf16[12,6,4,512]{3,2,1,0:T(4,128)(2,1)S(1)}) fusion(bf16[12,12,4,512]{3,2,1,0:T(4,128)(2,1)} %bitcast.15), kind=kLoop, calls=%fused_computation.8 | loop fusion | bytes 1179648 | tf_op jit(solution)/shard_map/slice | solution.py:207
  1.3 0.1 reshape.18.own_e_ref
  1.3 16.3 %collective-permute-start = (bf16[288,512]{1,0:T(8,128)(2,1)S(1)}, bf16[288,512]{1,0:T(8,128)(2,1)S(1)}, u32[]{:S(2)}, u32[]{:S(2)}) collective-permute-start(bf16[288,512]{1,0:T(8,128)(2,1)S(1)} %reshape.18.own_e_ref), channel_id=1, source_target_pairs={{0,16},{16,32},{32,48},{48,64},{64,80},{80,96},{96,112},{112,128},... | collective-permute-start | bytes 884744 | tf_op jit(solution)/shard_map/ppermute | solution.py:23
  17.6 0.0 copy-start
  17.6 0.0 copy-start.1
  17.6 0.0 copy-start.2
  17.7 0.1 reshape.17.own_w_ref
  17.7 6.7 %collective-permute-start.1 = (bf16[288,512]{1,0:T(8,128)(2,1)S(1)}, bf16[288,512]{1,0:T(8,128)(2,1)S(1)}, u32[]{:S(2)}, u32[]{:S(2)}) collective-permute-start(bf16[288,512]{1,0:T(8,128)(2,1)S(1)} %reshape.17.own_w_ref), channel_id=1, source_target_pairs={{0,496},{16,0},{32,16},{48,32},{64,48},{80,64},{96,80},{112,96},{1... | collective-permute-start | bytes 884744 | tf_op jit(solution)/shard_map/ppermute | solution.py:23
  24.4 1.8 %fusion = (bf16[3,6,4,512]{3,2,1,0:T(4,128)(2,1)S(1)}, bf16[3,6,4,512]{3,2,1,0:T(4,128)(2,1)}, bf16[3,6,4,512]{3,2,1,0:T(4,128)(2,1)S(1)}, bf16[3,6,4,512]{3,2,1,0:T(4,128)(2,1)}) fusion(bf16[12,12,4,512]{3,2,1,0:T(4,128)(2,1)} %bitcast.16), kind=kLoop, calls=%fused_computation.7 | loop fusion | bytes 589824 | tf_op jit(solution)/shard_map/slice | solution.py:212
  26.2 0.9 %stack.42 = bf16[1,72,512]{2,1,0:T(8,128)(2,1)S(1)} reshape(bf16[3,6,4,512]{3,2,1,0:T(4,128)(2,1)} %get-tuple-element.14) | data formatting | bytes 147456 | tf_op jit(solution)/shard_map/stack | solution.py:212
  27.1 0.7 stack.44
  27.8 0.9 %stack.49 = bf16[1,72,512]{2,1,0:T(8,128)(2,1)S(1)} reshape(bf16[3,6,4,512]{3,2,1,0:T(4,128)(2,1)} %get-tuple-element.12) | data formatting | bytes 147456 | tf_op jit(solution)/shard_map/stack | solution.py:212
  28.7 0.0 collective-permute-done.west_ref
  28.7 14.2 %collective-permute-done.1.east_ref = bf16[288,512]{1,0:T(8,128)(2,1)S(1)} collective-permute-done((bf16[288,512]{1,0:T(8,128)(2,1)S(1)}, bf16[288,512]{1,0:T(8,128)(2,1)S(1)}, u32[]{:S(2)}, u32[]{:S(2)}) %collective-permute-start.1) | collective-permute-done | bytes 294944 | tf_op jit(solution)/shard_map/ppermute | solution.py:23
  42.9 0.9 %pad_maximum_fusion = bf16[4,72,512]{2,1,0:T(8,128)(2,1)S(1)} fusion(bf16[1,72,512]{2,1,0:T(8,128)(2,1)S(1)} %get-tuple-element.20, bf16[1,72,512]{2,1,0:T(8,128)(2,1)} %stack.44, bf16[1,72,512]{2,1,0:T(8,128)(2,1)S(1)} %get-tuple-element.18, bf16[1,72,512]{2,1,0:T(8,128)(2,1)S(1)} %stack.42), kind=kLoop, calls=%fused_computation | loop fusion | flops 442368 | bytes 589824 | tf_op jit(solution)/shard_map/stack | solution.py:212
  43.9 28.9 %collective-permute-start.2 = (bf16[4,72,512]{2,1,0:T(8,128)(2,1)S(1)}, bf16[4,72,512]{2,1,0:T(8,128)(2,1)S(1)}, u32[]{:S(2)}, u32[]{:S(2)}) collective-permute-start(bf16[4,72,512]{2,1,0:T(8,128)(2,1)S(1)} %pad_maximum_fusion), channel_id=1, source_target_pairs={{0,1},{1,2},{2,3},{3,4},{4,5},{5,6},{6,7},{7,8},{8,9},{9,10},{10,1... | collective-permute-start | bytes 884744 | tf_op jit(solution)/shard_map/ppermute | solution.py:23
  72.9 1.9 %collective-permute-start.3 = (bf16[4,72,512]{2,1,0:T(8,128)(2,1)S(1)}, bf16[4,72,512]{2,1,0:T(8,128)(2,1)S(1)}, u32[]{:S(2)}, u32[]{:S(2)}) collective-permute-start(bf16[4,72,512]{2,1,0:T(8,128)(2,1)S(1)} %pad_maximum_fusion.1), channel_id=1, source_target_pairs={{1,0},{2,1},{3,2},{4,3},{5,4},{6,5},{7,6},{8,7},{9,8},{10,9},{11,1... | collective-permute-start | bytes 884744 | tf_op jit(solution)/shard_map/ppermute | solution.py:23
  74.8 0.1 add_select_fusion.closed_ref
  74.9 0.0 copy-done
  74.9 0.0 copy-done.1
  74.9 0.0 copy-done.2
  74.9 5.0 %shard_map.46 = (bf16[6,12,4,512]{3,2,1,0:T(4,128)(2,1)S(1)}, f32[4,72,512]{2,1,0:T(8,128)S(1)}, f32[3,4,72,512]{3,2,1,0:T(8,128)S(1)}) custom-call(bf16[288,512]{1,0:T(8,128)(2,1)S(1)} %reshape.17.own_w_ref, bf16[288,512]{1,0:T(8,128)(2,1)S(1)} %reshape.18.own_e_ref, bf16[288,512]{1,0:T(8,128)(2,1)S(1)} %collective-permute-done.west_ref, ...), custom_call_target="tpu_custom_call" | custom-call | flops 2500000000 | bytes 5933056 | tf_op jit(solution)/shard_map/pallas_call | solution.py:192
  79.9 0.0 collective-permute-done.2.north_ref
  79.9 1.0 %collective-permute-done.3.south_ref = bf16[4,72,512]{2,1,0:T(8,128)(2,1)S(1)} collective-permute-done((bf16[4,72,512]{2,1,0:T(8,128)(2,1)S(1)}, bf16[4,72,512]{2,1,0:T(8,128)(2,1)S(1)}, u32[]{:S(2)}, u32[]{:S(2)}) %collective-permute-start.3) | collective-permute-done | bytes 294944 | tf_op jit(solution)/shard_map/ppermute | solution.py:23
  80.9 4.2 %shard_map.47 = bf16[12,12,4,512]{3,2,1,0:T(4,128)(2,1)} custom-call(f32[2]{0:T(128)S(1)} %add_select_fusion.closed_ref, f32[4,72,512]{2,1,0:T(8,128)S(1)} %get-tuple-element.8.query_ref, f32[3,4,72,512]{3,2,1,0:T(8,128)S(1)} %get-tuple-element.9.state_ref, bf16[4,72,512]{2,1,0:T(8,128)(2,1)S(1)} %collective-permute-done.2.north_ref, ...), custom_call_target="tpu_custom_call" | custom-call | flops 1000000000 | bytes 6522888 | tf_op jit(solution)/shard_map/pallas_call | solution.py:192
  (4 shorter events, 0.1 us)
Async XLA Ops:
  1.3 27.4 %collective-permute-start = (bf16[288,512]{1,0:T(8,128)(2,1)S(1)}, bf16[288,512]{1,0:T(8,128)(2,1)S(1)}, u32[]{:S(2)}, u32[]{:S(2)}) collective-permute-start(bf16[288,512]{1,0:T(8,128)(2,1)S(1)} %reshape.18.own_e_ref), channel_id=1, source_target_pairs={{0,16},{16,32},{32,48},{48,64},{64,80},{80,96},{96,112},{112,128},... | collective-permute-start | bytes 884744 | tf_op jit(solution)/shard_map/ppermute | solution.py:23
  17.6 57.2 %copy-start = (bf16[512,1536]{1,0:T(8,128)(2,1)S(1)}, bf16[512,1536]{1,0:T(8,128)(2,1)}, u32[]{:S(2)}) copy-start(bf16[512,1536]{1,0:T(8,128)(2,1)} %qkv_ref.3) | copy-start | bytes 4718596
  17.6 57.2 %copy-start.1 = (bf16[512,512]{1,0:T(8,128)(2,1)S(1)}, bf16[512,512]{1,0:T(8,128)(2,1)}, u32[]{:S(2)}) copy-start(bf16[512,512]{1,0:T(8,128)(2,1)} %out_w_ref.3) | copy-start | bytes 1572868
  17.6 57.2 %copy-start.2 = (f32[512]{0:T(512)S(1)}, f32[512]{0:T(512)}, u32[]{:S(2)}) copy-start(f32[512]{0:T(512)} %param.5) | copy-start | bytes 6148
  17.7 25.2 %collective-permute-start.1 = (bf16[288,512]{1,0:T(8,128)(2,1)S(1)}, bf16[288,512]{1,0:T(8,128)(2,1)S(1)}, u32[]{:S(2)}, u32[]{:S(2)}) collective-permute-start(bf16[288,512]{1,0:T(8,128)(2,1)S(1)} %reshape.17.own_w_ref), channel_id=1, source_target_pairs={{0,496},{16,0},{32,16},{48,32},{64,48},{80,64},{96,80},{112,96},{1... | collective-permute-start | bytes 884744 | tf_op jit(solution)/shard_map/ppermute | solution.py:23
  43.9 36.0 %collective-permute-start.2 = (bf16[4,72,512]{2,1,0:T(8,128)(2,1)S(1)}, bf16[4,72,512]{2,1,0:T(8,128)(2,1)S(1)}, u32[]{:S(2)}, u32[]{:S(2)}) collective-permute-start(bf16[4,72,512]{2,1,0:T(8,128)(2,1)S(1)} %pad_maximum_fusion), channel_id=1, source_target_pairs={{0,1},{1,2},{2,3},{3,4},{4,5},{5,6},{6,7},{7,8},{8,9},{9,10},{10,1... | collective-permute-start | bytes 884744 | tf_op jit(solution)/shard_map/ppermute | solution.py:23
  72.9 8.0 %collective-permute-start.3 = (bf16[4,72,512]{2,1,0:T(8,128)(2,1)S(1)}, bf16[4,72,512]{2,1,0:T(8,128)(2,1)S(1)}, u32[]{:S(2)}, u32[]{:S(2)}) collective-permute-start(bf16[4,72,512]{2,1,0:T(8,128)(2,1)S(1)} %pad_maximum_fusion.1), channel_id=1, source_target_pairs={{1,0},{2,1},{3,2},{4,3},{5,4},{6,5},{7,6},{8,7},{9,8},{10,9},{11,1... | collective-permute-start | bytes 884744 | tf_op jit(solution)/shard_map/ppermute | solution.py:23

commit v10 on v9

--- a/solution.py
+++ b/solution.py
@@ -208,10 +208,11 @@
     east = shift(own_w, "lon", -1, True)
     west = shift(own_e, "lon", 1, True)
 
-    def rim(*halves):
-        return jnp.stack([h[:RIM] for h in halves]), jnp.stack([h[rows - RIM :] for h in halves])
-
-    first, last = rim(own_w, west, own_e, east)
+    first = jnp.zeros((4, RIM, width), tokens.dtype)
+    last = first
+    for part, half in ((0, own_w), (2, own_e), (1, west), (3, east)):
+        first = lax.dynamic_update_slice(first, half[None, :RIM], (part, 0, 0))
+        last = lax.dynamic_update_slice(last, half[None, rows - RIM :], (part, 0, 0))
     south = shift(first, "lat", -1, False)
     north = shift(last, "lat", 1, False)
     gain = gain_attn.reshape(1, width)

time: 85.5 us -> 86.2 us (level)
  local copies, waits for them, and re-layouts: 5.69 us -> 10.6 us
  waiting for transfers between devices: 15.2 us -> 11 us
  starting transfers between devices: 53.8 us -> 54.8 us
  other arithmetic: 1.05 us -> 0.08 us
    dynamic_update_slice x0 -> x5, local copies, waits for them, and re-layouts: none -> 5.26 us  [the longest x4 3.63 us: shards(): first = lax.dynamic_update_slice(first, half[None, :RIM], (part, 0, 0))]
    ppermute x4, waiting for transfers between devices: 15.2 us -> 11 us  [shift(): return lax.ppermute(value, axis, pairs)]
    another operation x6 -> x0, local copies, waits for them, and re-layouts: 2.51 us -> none  [the longest x2 1.56 us: rim(): jnp.stack([h[rows - RIM:] for h in halves])]
    broadcast_in_dim x0 -> x4, local copies, waits for them, and re-layouts: none -> 2.21 us  [the longest x2 1.54 us: shards(): last = lax.dynamic_update_slice(last, half[None, rows - RIM:], (part, 0, 0))]
    ppermute x4, starting transfers between devices: 53.8 us -> 54.8 us  [shift(): return lax.ppermute(value, axis, pairs)]
    another operation x2 -> x0, other arithmetic: 0.97 us -> none  [the longest x1 0.93 us: rim(): jnp.stack([h[rows - RIM:] for h in halves])]
  transfers between devices with their start and end apart: 4 -> 4, of which waited for: 2 -> 2; matrix products, arithmetic and copies ran while one was open for 5% -> 10% of each run, Pallas kernels for 6% -> 6%
where the time goes in v10:
time: 86.2 us; the launch traced here: 85.8 us
  starting transfers between devices  54.8 us (64%)
  waiting for transfers between devices  11 us (13%)
  local copies, waits for them, and re-layouts  10.6 us (12%)
  Pallas kernels  9.22 us (11%)
    ppermute x4, starting transfers between devices, shift(): return lax.ppermute(value, axis, pairs)  54.8 us
    ppermute x4, waiting for transfers between devices, shift(): return lax.ppermute(value, axis, pairs)  11 us
    pallas_call x2, Pallas kernels, call(): pl.pallas_call(kernel, out_shape=results, in_specs=specs, out_specs=[pl.B...  9.22 us
    dynamic_update_slice x4, local copies, waits for them, and re-layouts, shards(): first = lax.dynamic_update_slice(first, half[None, :RIM], (part, 0, 0))  3.63 us
    slice x1, local copies, waits for them, and re-layouts, shards(): first = lax.dynamic_update_slice(first, half[None, :RIM], (part, 0, 0))  1.74 us
  transfers between devices with their start and end apart: 4, of which 2 were waited for; matrix products, arithmetic and copies ran while one was open for 10% of the time, Pallas kernels for 6%

profile of v10, /device:TPU:1, one launch (start us, length us, event | category | flops | bytes accessed | tf_op | source)
XLA Modules:
  0.0 85.8 jit_solution(6949804486441259651)
XLA Ops:
  0.0 1.3 %fusion.5 = (bf16[12,6,4,512]{3,2,1,0:T(4,128)(2,1)S(1)}, bf16[12,6,4,512]{3,2,1,0:T(4,128)(2,1)S(1)}) fusion(bf16[12,12,4,512]{3,2,1,0:T(4,128)(2,1)} %bitcast.23), kind=kLoop, calls=%fused_computation.12 | loop fusion | bytes 1179648 | tf_op jit(solution)/shard_map/slice | solution.py:207
  1.3 0.1 reshape.18.own_e_ref
  1.3 0.0 copy-start
  1.4 0.0 copy-start.1
  1.4 0.0 copy-start.2
  1.4 16.4 %collective-permute-start = (bf16[288,512]{1,0:T(8,128)(2,1)S(1)}, bf16[288,512]{1,0:T(8,128)(2,1)S(1)}, u32[]{:S(2)}, u32[]{:S(2)}) collective-permute-start(bf16[288,512]{1,0:T(8,128)(2,1)S(1)} %reshape.18.own_e_ref), channel_id=1, source_target_pairs={{0,16},{16,32},{32,48},{48,64},{64,80},{80,96},{96,112},{112,128},... | collective-permute-start | bytes 884744 | tf_op jit(solution)/shard_map/ppermute | solution.py:23
  17.8 0.1 reshape.17.own_w_ref
  17.9 6.6 %collective-permute-start.1 = (bf16[288,512]{1,0:T(8,128)(2,1)S(1)}, bf16[288,512]{1,0:T(8,128)(2,1)S(1)}, u32[]{:S(2)}, u32[]{:S(2)}) collective-permute-start(bf16[288,512]{1,0:T(8,128)(2,1)S(1)} %reshape.17.own_w_ref), channel_id=1, source_target_pairs={{0,496},{16,0},{32,16},{48,32},{64,48},{80,64},{96,80},{112,96},{1... | collective-permute-start | bytes 884744 | tf_op jit(solution)/shard_map/ppermute | solution.py:23
  24.4 1.7 %fusion.4 = (bf16[3,6,4,512]{3,2,1,0:T(4,128)(2,1)S(1)}, bf16[3,6,4,512]{3,2,1,0:T(4,128)(2,1)S(1)}, bf16[3,6,4,512]{3,2,1,0:T(4,128)(2,1)S(1)}, bf16[3,6,4,512]{3,2,1,0:T(4,128)(2,1)}) fusion(bf16[12,12,4,512]{3,2,1,0:T(4,128)(2,1)} %bitcast.24), kind=kLoop, calls=%fused_computation.11 | loop fusion | bytes 589824 | tf_op jit(solution)/shard_map/slice | solution.py:214
  26.2 1.5 %broadcast_in_dim.35 = bf16[1,72,512]{2,1,0:T(8,128)(2,1)} reshape(bf16[3,6,4,512]{3,2,1,0:T(4,128)(2,1)} %get-tuple-element.14) | data formatting | bytes 147456 | tf_op jit(solution)/shard_map/broadcast_in_dim | solution.py:215
  27.7 0.6 broadcast_in_dim.39
  28.4 1.6 %dynamic_update_slice.24 = bf16[4,72,512]{2,1,0:T(8,128)(2,1)} pad(bf16[1,72,512]{2,1,0:T(8,128)(2,1)} %broadcast_in_dim.35, bf16[]{:T(256)} %constant.5.clone.1), padding=0_3x0_0x0_0 | pad | bytes 368642 | tf_op jit(solution)/shard_map/dynamic_update_slice | solution.py:215
  30.0 1.6 %dynamic_update_slice.28 = bf16[4,72,512]{2,1,0:T(8,128)(2,1)} pad(bf16[1,72,512]{2,1,0:T(8,128)(2,1)} %broadcast_in_dim.39, bf16[]{:T(256)} %constant.5.clone.1), padding=0_3x0_0x0_0 | pad | bytes 368642 | tf_op jit(solution)/shard_map/dynamic_update_slice | solution.py:214
  31.7 0.7 constant_dynamic-update-slice_fusion
  32.3 0.0 collective-permute-done.west_ref
  32.3 0.7 fusion.1
  33.0 9.8 %collective-permute-done.1.east_ref = bf16[288,512]{1,0:T(8,128)(2,1)S(1)} collective-permute-done((bf16[288,512]{1,0:T(8,128)(2,1)S(1)}, bf16[288,512]{1,0:T(8,128)(2,1)S(1)}, u32[]{:S(2)}, u32[]{:S(2)}) %collective-permute-start.1) | collective-permute-done | bytes 294944 | tf_op jit(solution)/shard_map/ppermute | solution.py:23
  42.8 0.7 fusion
  43.4 29.9 %collective-permute-start.2 = (bf16[4,72,512]{2,1,0:T(8,128)(2,1)}, bf16[4,72,512]{2,1,0:T(8,128)(2,1)S(1)}, u32[]{:S(2)}, u32[]{:S(2)}) collective-permute-start(bf16[4,72,512]{2,1,0:T(8,128)(2,1)} %get-tuple-element.18), channel_id=1, source_target_pairs={{0,1},{1,2},{2,3},{3,4},{4,5},{5,6},{6,7},{7,8},{8,9},{9,10},{10,1... | collective-permute-start | bytes 884744 | tf_op jit(solution)/shard_map/ppermute | solution.py:23
  73.3 1.9 %collective-permute-start.3 = (bf16[4,72,512]{2,1,0:T(8,128)(2,1)}, bf16[4,72,512]{2,1,0:T(8,128)(2,1)S(1)}, u32[]{:S(2)}, u32[]{:S(2)}) collective-permute-start(bf16[4,72,512]{2,1,0:T(8,128)(2,1)} %get-tuple-element.17), channel_id=1, source_target_pairs={{1,0},{2,1},{3,2},{4,3},{5,4},{6,5},{7,6},{8,7},{9,8},{10,9},{11,1... | collective-permute-start | bytes 884744 | tf_op jit(solution)/shard_map/ppermute | solution.py:23
  75.3 0.1 add_select_fusion.closed_ref
  75.3 0.0 copy-done
  75.3 0.0 copy-done.1
  75.3 0.0 copy-done.2
  75.3 5.0 %shard_map.46 = (bf16[6,12,4,512]{3,2,1,0:T(4,128)(2,1)S(1)}, f32[4,72,512]{2,1,0:T(8,128)S(1)}, f32[3,4,72,512]{3,2,1,0:T(8,128)S(1)}) custom-call(bf16[288,512]{1,0:T(8,128)(2,1)S(1)} %reshape.17.own_w_ref, bf16[288,512]{1,0:T(8,128)(2,1)S(1)} %reshape.18.own_e_ref, bf16[288,512]{1,0:T(8,128)(2,1)S(1)} %collective-permute-done.west_ref, ...), custom_call_target="tpu_custom_call" | custom-call | flops 2500000000 | bytes 5933056 | tf_op jit(solution)/shard_map/pallas_call | solution.py:192
  80.4 0.0 collective-permute-done.2.north_ref
  80.4 1.2 %collective-permute-done.3.south_ref = bf16[4,72,512]{2,1,0:T(8,128)(2,1)S(1)} collective-permute-done((bf16[4,72,512]{2,1,0:T(8,128)(2,1)}, bf16[4,72,512]{2,1,0:T(8,128)(2,1)S(1)}, u32[]{:S(2)}, u32[]{:S(2)}) %collective-permute-start.3) | collective-permute-done | bytes 294944 | tf_op jit(solution)/shard_map/ppermute | solution.py:23
  81.6 4.2 %shard_map.47 = bf16[12,12,4,512]{3,2,1,0:T(4,128)(2,1)} custom-call(f32[2]{0:T(128)S(1)} %add_select_fusion.closed_ref, f32[4,72,512]{2,1,0:T(8,128)S(1)} %get-tuple-element.8.query_ref, f32[3,4,72,512]{3,2,1,0:T(8,128)S(1)} %get-tuple-element.9.state_ref, bf16[4,72,512]{2,1,0:T(8,128)(2,1)S(1)} %collective-permute-done.2.north_ref, ...), custom_call_target="tpu_custom_call" | custom-call | flops 1000000000 | bytes 6522888 | tf_op jit(solution)/shard_map/pallas_call | solution.py:192
  (2 shorter events, 0.0 us)
Async XLA Ops:
  1.3 74.0 %copy-start = (bf16[512,1536]{1,0:T(8,128)(2,1)S(1)}, bf16[512,1536]{1,0:T(8,128)(2,1)}, u32[]{:S(2)}) copy-start(bf16[512,1536]{1,0:T(8,128)(2,1)} %qkv_ref.3) | copy-start | bytes 4718596
  1.4 74.0 %copy-start.1 = (bf16[512,512]{1,0:T(8,128)(2,1)S(1)}, bf16[512,512]{1,0:T(8,128)(2,1)}, u32[]{:S(2)}) copy-start(bf16[512,512]{1,0:T(8,128)(2,1)} %out_w_ref.3) | copy-start | bytes 1572868
  1.4 74.0 %copy-start.2 = (f32[512]{0:T(512)S(1)}, f32[512]{0:T(512)}, u32[]{:S(2)}) copy-start(f32[512]{0:T(512)} %param.5) | copy-start | bytes 6148
  1.4 31.0 %collective-permute-start = (bf16[288,512]{1,0:T(8,128)(2,1)S(1)}, bf16[288,512]{1,0:T(8,128)(2,1)S(1)}, u32[]{:S(2)}, u32[]{:S(2)}) collective-permute-start(bf16[288,512]{1,0:T(8,128)(2,1)S(1)} %reshape.18.own_e_ref), channel_id=1, source_target_pairs={{0,16},{16,32},{32,48},{48,64},{64,80},{80,96},{96,112},{112,128},... | collective-permute-start | bytes 884744 | tf_op jit(solution)/shard_map/ppermute | solution.py:23
  17.9 24.9 %collective-permute-start.1 = (bf16[288,512]{1,0:T(8,128)(2,1)S(1)}, bf16[288,512]{1,0:T(8,128)(2,1)S(1)}, u32[]{:S(2)}, u32[]{:S(2)}) collective-permute-start(bf16[288,512]{1,0:T(8,128)(2,1)S(1)} %reshape.17.own_w_ref), channel_id=1, source_target_pairs={{0,496},{16,0},{32,16},{48,32},{64,48},{80,64},{96,80},{112,96},{1... | collective-permute-start | bytes 884744 | tf_op jit(solution)/shard_map/ppermute | solution.py:23
  43.4 36.9 %collective-permute-start.2 = (bf16[4,72,512]{2,1,0:T(8,128)(2,1)}, bf16[4,72,512]{2,1,0:T(8,128)(2,1)S(1)}, u32[]{:S(2)}, u32[]{:S(2)}) collective-permute-start(bf16[4,72,512]{2,1,0:T(8,128)(2,1)} %get-tuple-element.18), channel_id=1, source_target_pairs={{0,1},{1,2},{2,3},{3,4},{4,5},{5,6},{6,7},{7,8},{8,9},{9,10},{10,1... | collective-permute-start | bytes 884744 | tf_op jit(solution)/shard_map/ppermute | solution.py:23
  73.3 8.3 %collective-permute-start.3 = (bf16[4,72,512]{2,1,0:T(8,128)(2,1)}, bf16[4,72,512]{2,1,0:T(8,128)(2,1)S(1)}, u32[]{:S(2)}, u32[]{:S(2)}) collective-permute-start(bf16[4,72,512]{2,1,0:T(8,128)(2,1)} %get-tuple-element.17), channel_id=1, source_target_pairs={{1,0},{2,1},{3,2},{4,3},{5,4},{6,5},{7,6},{8,7},{9,8},{10,9},{11,1... | collective-permute-start | bytes 884744 | tf_op jit(solution)/shard_map/ppermute | solution.py:23

commit v11 on v9

--- a/solution.py
+++ b/solution.py
@@ -155,6 +155,8 @@
     state_ref,
     north_ref,
     south_ref,
+    far_north_ref,
+    far_south_ref,
     own_w_ref,
     own_e_ref,
     middle_ref,
@@ -164,7 +166,8 @@
     out_ref,
 ):
     rows, width = own_w_ref.shape
-    beyond = [r[part].astype(jnp.float32) for r in (north_ref, south_ref) for part in range(4)]
+    refs = ((north_ref, far_north_ref), (south_ref, far_south_ref))
+    beyond = [r[side].astype(jnp.float32) for pair in refs for side in range(2) for r in pair]
     beyond = make_keys(layer_norm(jnp.concatenate(beyond, axis=0), gain_ref[...]), qkv_ref).astype(jnp.bfloat16)
     levels = level_bias(RIM, 2 * RIM)
     own = [r[...].astype(jnp.float32) for r in (own_w_ref, own_e_ref)]
@@ -211,9 +214,12 @@
     def rim(*halves):
         return jnp.stack([h[:RIM] for h in halves]), jnp.stack([h[rows - RIM :] for h in halves])
 
-    first, last = rim(own_w, west, own_e, east)
+    first, last = rim(own_w, own_e)
     south = shift(first, "lat", -1, False)
     north = shift(last, "lat", 1, False)
+    first, last = rim(west, east)
+    far_south = shift(first, "lat", -1, False)
+    far_north = shift(last, "lat", 1, False)
     gain = gain_attn.reshape(1, width)
     place = lax.axis_index("lat")
     closed = jnp.stack([place == 0, place == lax.axis_size("lat") - 1])
@@ -247,6 +253,8 @@
         state,
         north,
         south,
+        far_north,
+        far_south,
         own_w,
         own_e,
         middle,

time: 85.5 us -> 85.9 us (level)
  starting transfers between devices: 53.8 us -> 58.7 us
  waiting for transfers between devices: 15.2 us -> 11.8 us
  local copies, waits for them, and re-layouts: 5.69 us -> 3.56 us
    ppermute x4 -> x6, starting transfers between devices: 53.8 us -> 58.7 us  [shift(): return lax.ppermute(value, axis, pairs)]
    ppermute x4 -> x6, waiting for transfers between devices: 15.2 us -> 11.8 us  [shift(): return lax.ppermute(value, axis, pairs)]
    another operation x2, local copies, waits for them, and re-layouts: 1.56 us -> 0.05 us  [rim(): jnp.stack([h[rows - RIM:] for h in halves])]
    another operation x1 -> x2, other arithmetic: 0.93 us -> 0.04 us  [rim(): jnp.stack([h[rows - RIM:] for h in halves])]
  transfers between devices with their start and end apart: 4 -> 6, of which waited for: 2 -> 1; matrix products, arithmetic and copies ran while one was open for 5% -> 4% of each run, Pallas kernels for 6% -> 7%
where the time goes in v11:
time: 85.9 us; the launch traced here: 85.1 us
  starting transfers between devices  58.7 us (68%)
  waiting for transfers between devices  11.8 us (14%)
  Pallas kernels  10 us (12%)
  local copies, waits for them, and re-layouts  3.56 us (4%)
    ppermute x6, starting transfers between devices, shift(): return lax.ppermute(value, axis, pairs)  58.7 us
    ppermute x6, waiting for transfers between devices, shift(): return lax.ppermute(value, axis, pairs)  11.8 us
    pallas_call x2, Pallas kernels, call(): pl.pallas_call(kernel, out_shape=results, in_specs=specs, out_specs=[pl.B...  10 us
  transfers between devices with their start and end apart: 6, of which 1 were waited for; matrix products, arithmetic and copies ran while one was open for 4% of the time, Pallas kernels for 7%

profile of v11, /device:TPU:1, one launch (start us, length us, event | category | flops | bytes accessed | tf_op | source)
XLA Modules:
  0.0 85.1 jit_solution(7902710040480989801)
XLA Ops:
  0.0 1.3 %fusion.1 = (bf16[12,6,4,512]{3,2,1,0:T(4,128)(2,1)S(1)}, bf16[12,6,4,512]{3,2,1,0:T(4,128)(2,1)S(1)}) fusion(bf16[12,12,4,512]{3,2,1,0:T(4,128)(2,1)} %bitcast.15), kind=kLoop, calls=%fused_computation.10 | loop fusion | bytes 1179648 | tf_op jit(solution)/shard_map/slice | solution.py:210
  1.3 0.1 reshape.18.own_e_ref
  1.3 16.3 %collective-permute-start = (bf16[288,512]{1,0:T(8,128)(2,1)S(1)}, bf16[288,512]{1,0:T(8,128)(2,1)S(1)}, u32[]{:S(2)}, u32[]{:S(2)}) collective-permute-start(bf16[288,512]{1,0:T(8,128)(2,1)S(1)} %reshape.18.own_e_ref), channel_id=1, source_target_pairs={{0,16},{16,32},{32,48},{48,64},{64,80},{80,96},{96,112},{112,128},... | collective-permute-start | bytes 884744 | tf_op jit(solution)/shard_map/ppermute | solution.py:23
  17.6 0.0 copy-start
  17.6 0.0 copy-start.1
  17.6 0.0 copy-start.2
  17.7 0.1 reshape.17.own_w_ref
  17.7 6.7 %collective-permute-start.1 = (bf16[288,512]{1,0:T(8,128)(2,1)S(1)}, bf16[288,512]{1,0:T(8,128)(2,1)}, u32[]{:S(2)}, u32[]{:S(2)}) collective-permute-start(bf16[288,512]{1,0:T(8,128)(2,1)S(1)} %reshape.17.own_w_ref), channel_id=1, source_target_pairs={{0,496},{16,0},{32,16},{48,32},{64,48},{80,64},{96,80},{112,96},{1... | collective-permute-start | bytes 884744 | tf_op jit(solution)/shard_map/ppermute | solution.py:23
  24.4 1.1 %fusion = (bf16[3,6,4,512]{3,2,1,0:T(4,128)(2,1)S(1)}, bf16[3,6,4,512]{3,2,1,0:T(4,128)(2,1)S(1)}, bf16[3,6,4,512]{3,2,1,0:T(4,128)(2,1)S(1)}, bf16[3,6,4,512]{3,2,1,0:T(4,128)(2,1)S(1)}) fusion(bf16[12,12,4,512]{3,2,1,0:T(4,128)(2,1)} %bitcast.16), kind=kLoop, calls=%fused_computation.9 | loop fusion | bytes 589824 | tf_op jit(solution)/shard_map/slice | solution.py:215
  25.6 3.5 %collective-permute-start.2 = (bf16[2,72,512]{2,1,0:T(8,128)(2,1)S(1)}, bf16[2,72,512]{2,1,0:T(8,128)(2,1)S(1)}, u32[]{:S(2)}, u32[]{:S(2)}) collective-permute-start(bf16[2,72,512]{2,1,0:T(8,128)(2,1)S(1)} %pad_maximum_fusion), channel_id=1, source_target_pairs={{0,1},{1,2},{2,3},{3,4},{4,5},{5,6},{6,7},{7,8},{8,9},{9,10},{10,1... | collective-permute-start | bytes 442376 | tf_op jit(solution)/shard_map/ppermute | solution.py:23
  29.2 0.7 pad_maximum_fusion.1
  29.9 2.5 %collective-permute-start.3 = (bf16[2,72,512]{2,1,0:T(8,128)(2,1)}, bf16[2,72,512]{2,1,0:T(8,128)(2,1)S(1)}, u32[]{:S(2)}, u32[]{:S(2)}) collective-permute-start(bf16[2,72,512]{2,1,0:T(8,128)(2,1)} %pad_maximum_fusion.1), channel_id=1, source_target_pairs={{1,0},{2,1},{3,2},{4,3},{5,4},{6,5},{7,6},{8,7},{9,8},{10,9},{11,1... | collective-permute-start | bytes 442376 | tf_op jit(solution)/shard_map/ppermute | solution.py:23
  32.4 0.1 add_select_fusion.closed_ref
  32.5 0.0 collective-permute-done.west_ref
  32.5 11.8 %collective-permute-done.1.east_ref = bf16[288,512]{1,0:T(8,128)(2,1)} collective-permute-done((bf16[288,512]{1,0:T(8,128)(2,1)S(1)}, bf16[288,512]{1,0:T(8,128)(2,1)}, u32[]{:S(2)}, u32[]{:S(2)}) %collective-permute-start.1) | collective-permute-done | bytes 294944 | tf_op jit(solution)/shard_map/ppermute | solution.py:23
  44.3 0.9 %slice_bitcast_fusion = (bf16[1,72,512]{2,1,0:T(8,128)(2,1)S(1)}, bf16[1,72,512]{2,1,0:T(8,128)(2,1)S(1)}) fusion(bf16[288,512]{1,0:T(8,128)(2,1)} %collective-permute-done.1.east_ref), kind=kLoop, calls=%fused_computation.4 | loop fusion | bytes 294912 | tf_op jit(solution)/shard_map/stack | solution.py:215
  45.2 27.8 %collective-permute-start.4 = (bf16[2,72,512]{2,1,0:T(8,128)(2,1)S(1)}, bf16[2,72,512]{2,1,0:T(8,128)(2,1)S(1)}, u32[]{:S(2)}, u32[]{:S(2)}) collective-permute-start(bf16[2,72,512]{2,1,0:T(8,128)(2,1)S(1)} %pad_maximum_fusion.2), channel_id=1, source_target_pairs={{0,1},{1,2},{2,3},{3,4},{4,5},{5,6},{6,7},{7,8},{8,9},{9,10},{10,1... | collective-permute-start | bytes 442376 | tf_op jit(solution)/shard_map/ppermute | solution.py:23
  73.1 1.9 %collective-permute-start.5 = (bf16[2,72,512]{2,1,0:T(8,128)(2,1)S(1)}, bf16[2,72,512]{2,1,0:T(8,128)(2,1)S(1)}, u32[]{:S(2)}, u32[]{:S(2)}) collective-permute-start(bf16[2,72,512]{2,1,0:T(8,128)(2,1)S(1)} %pad_maximum_fusion.3), channel_id=1, source_target_pairs={{1,0},{2,1},{3,2},{4,3},{5,4},{6,5},{7,6},{8,7},{9,8},{10,9},{11,1... | collective-permute-start | bytes 442376 | tf_op jit(solution)/shard_map/ppermute | solution.py:23
  75.0 0.0 copy-done
  75.0 0.0 copy-done.1
  75.0 0.0 copy-done.2
  75.0 5.9 %shard_map.46 = (bf16[6,12,4,512]{3,2,1,0:T(4,128)(2,1)S(1)}, f32[4,72,512]{2,1,0:T(8,128)S(1)}, f32[3,4,72,512]{3,2,1,0:T(8,128)S(1)}) custom-call(bf16[288,512]{1,0:T(8,128)(2,1)S(1)} %reshape.17.own_w_ref, bf16[288,512]{1,0:T(8,128)(2,1)S(1)} %reshape.18.own_e_ref, bf16[288,512]{1,0:T(8,128)(2,1)S(1)} %collective-permute-done.west_ref, ...), custom_call_target="tpu_custom_call" | custom-call | flops 2500000000 | bytes 5933056 | tf_op jit(solution)/shard_map/pallas_call | solution.py:195
  80.9 0.0 collective-permute-done.2.north_ref
  80.9 0.0 collective-permute-done.3.south_ref
  80.9 0.0 collective-permute-done.4.far_north_ref
  80.9 0.0 collective-permute-done.5.far_south_ref
  80.9 4.2 %shard_map.47 = bf16[12,12,4,512]{3,2,1,0:T(4,128)(2,1)} custom-call(f32[2]{0:T(128)S(1)} %add_select_fusion.closed_ref, f32[4,72,512]{2,1,0:T(8,128)S(1)} %get-tuple-element.8.query_ref, f32[3,4,72,512]{3,2,1,0:T(8,128)S(1)} %get-tuple-element.9.state_ref, bf16[2,72,512]{2,1,0:T(8,128)(2,1)S(1)} %collective-permute-done.2.north_ref, ...), custom_call_target="tpu_custom_call" | custom-call | flops 1000000000 | bytes 6522888 | tf_op jit(solution)/shard_map/pallas_call | solution.py:195
  (8 shorter events, 0.2 us)
Async XLA Ops:
  1.3 31.1 %collective-permute-start = (bf16[288,512]{1,0:T(8,128)(2,1)S(1)}, bf16[288,512]{1,0:T(8,128)(2,1)S(1)}, u32[]{:S(2)}, u32[]{:S(2)}) collective-permute-start(bf16[288,512]{1,0:T(8,128)(2,1)S(1)} %reshape.18.own_e_ref), channel_id=1, source_target_pairs={{0,16},{16,32},{32,48},{48,64},{64,80},{80,96},{96,112},{112,128},... | collective-permute-start | bytes 884744 | tf_op jit(solution)/shard_map/ppermute | solution.py:23
  17.6 57.4 %copy-start = (bf16[512,1536]{1,0:T(8,128)(2,1)S(1)}, bf16[512,1536]{1,0:T(8,128)(2,1)}, u32[]{:S(2)}) copy-start(bf16[512,1536]{1,0:T(8,128)(2,1)} %qkv_ref.3) | copy-start | bytes 4718596
  17.6 57.4 %copy-start.1 = (bf16[512,512]{1,0:T(8,128)(2,1)S(1)}, bf16[512,512]{1,0:T(8,128)(2,1)}, u32[]{:S(2)}) copy-start(bf16[512,512]{1,0:T(8,128)(2,1)} %out_w_ref.3) | copy-start | bytes 1572868
  17.6 57.4 %copy-start.2 = (f32[512]{0:T(512)S(1)}, f32[512]{0:T(512)}, u32[]{:S(2)}) copy-start(f32[512]{0:T(512)} %param.5) | copy-start | bytes 6148
  17.7 26.5 %collective-permute-start.1 = (bf16[288,512]{1,0:T(8,128)(2,1)S(1)}, bf16[288,512]{1,0:T(8,128)(2,1)}, u32[]{:S(2)}, u32[]{:S(2)}) collective-permute-start(bf16[288,512]{1,0:T(8,128)(2,1)S(1)} %reshape.17.own_w_ref), channel_id=1, source_target_pairs={{0,496},{16,0},{32,16},{48,32},{64,48},{80,64},{96,80},{112,96},{1... | collective-permute-start | bytes 884744 | tf_op jit(solution)/shard_map/ppermute | solution.py:23
  25.6 55.3 %collective-permute-start.2 = (bf16[2,72,512]{2,1,0:T(8,128)(2,1)S(1)}, bf16[2,72,512]{2,1,0:T(8,128)(2,1)S(1)}, u32[]{:S(2)}, u32[]{:S(2)}) collective-permute-start(bf16[2,72,512]{2,1,0:T(8,128)(2,1)S(1)} %pad_maximum_fusion), channel_id=1, source_target_pairs={{0,1},{1,2},{2,3},{3,4},{4,5},{5,6},{6,7},{7,8},{8,9},{9,10},{10,1... | collective-permute-start | bytes 442376 | tf_op jit(solution)/shard_map/ppermute | solution.py:23
  29.9 51.1 %collective-permute-start.3 = (bf16[2,72,512]{2,1,0:T(8,128)(2,1)}, bf16[2,72,512]{2,1,0:T(8,128)(2,1)S(1)}, u32[]{:S(2)}, u32[]{:S(2)}) collective-permute-start(bf16[2,72,512]{2,1,0:T(8,128)(2,1)} %pad_maximum_fusion.1), channel_id=1, source_target_pairs={{1,0},{2,1},{3,2},{4,3},{5,4},{6,5},{7,6},{8,7},{9,8},{10,9},{11,1... | collective-permute-start | bytes 442376 | tf_op jit(solution)/shard_map/ppermute | solution.py:23
  45.2 35.7 %collective-permute-start.4 = (bf16[2,72,512]{2,1,0:T(8,128)(2,1)S(1)}, bf16[2,72,512]{2,1,0:T(8,128)(2,1)S(1)}, u32[]{:S(2)}, u32[]{:S(2)}) collective-permute-start(bf16[2,72,512]{2,1,0:T(8,128)(2,1)S(1)} %pad_maximum_fusion.2), channel_id=1, source_target_pairs={{0,1},{1,2},{2,3},{3,4},{4,5},{5,6},{6,7},{7,8},{8,9},{9,10},{10,1... | collective-permute-start | bytes 442376 | tf_op jit(solution)/shard_map/ppermute | solution.py:23
  73.1 7.9 %collective-permute-start.5 = (bf16[2,72,512]{2,1,0:T(8,128)(2,1)S(1)}, bf16[2,72,512]{2,1,0:T(8,128)(2,1)S(1)}, u32[]{:S(2)}, u32[]{:S(2)}) collective-permute-start(bf16[2,72,512]{2,1,0:T(8,128)(2,1)S(1)} %pad_maximum_fusion.3), channel_id=1, source_target_pairs={{1,0},{2,1},{3,2},{4,3},{5,4},{6,5},{7,6},{8,7},{9,8},{10,9},{11,1... | collective-permute-start | bytes 442376 | tf_op jit(solution)/shard_map/ppermute | solution.py:23
